TPU v7x, 32 devices: a whole 2x2x4 slice. The times are simulated.
32 devices in a mesh: groups: 2 (over y), ctx: 16 (over z, x, core).
Axes of the slice: x: 2, y: 2, z: 4, core: 2. Of those that a mesh axis runs over, the one named last changes fastest.
Arguments:
- query_feat: bfloat16 [4096, 4096], P(('groups', 'ctx')), parts along dimension 0, may hold values from -6 to 6
- key_feat: bfloat16 [4096, 4096], P(('groups', 'ctx')), parts along dimension 0, may hold values from -6 to 6
- value_raw: bfloat16 [4096, 4096], P(('groups', 'ctx')), parts along dimension 0, may hold values from -6 to 6
- conv_out: bfloat16 [4096, 4096], P(('groups', 'ctx')), parts along dimension 0, may hold values from -6 to 6
- out_grad: bfloat16 [4096, 4096], P(('groups', 'ctx')), parts along dimension 0, may hold values from -11 to 15
- filter_taps: bfloat16 [4096, 2048], P('ctx'), may hold values from -0.75 to 0.75
- short_filter: float32 [3, 4096], replicated, may hold values from -3.5 to 3.5
- skip_gain: float32 [4096], replicated, may hold values from 0.25 to 1.75
Outputs:
- query_grad: bfloat16 [4096, 4096], P(('groups', 'ctx')), parts along dimension 0
- key_grad: bfloat16 [4096, 4096], P(('groups', 'ctx')), parts along dimension 0
- value_grad: bfloat16 [4096, 4096], P(('groups', 'ctx')), parts along dimension 0
- filter_grad: bfloat16 [8192, 2048], P(('groups', 'ctx')), parts along dimension 0
- skip_grad: float32 [8192], P(('groups', 'ctx')), parts along dimension 0
- short_grad: float32 [3, 8192], P(None, ('groups', 'ctx')), parts along dimension 1
There are 2 independent parts, one for each index of `groups`. A program takes and returns all parts, laid end to end along the dimension named above; an argument that names none is the same for every part. Nothing has to cross between parts.
All inputs are finite; a program needn't handle non-finite values.
Results may differ from a plain program's by a relative error of at most 0.0075.
Values may be sent and summed in bfloat16 or wider, within the bound.
No kernel may reach another device: no remote copies, remote signals or barrier semaphores. Data moves between devices by JAX's collectives and lax.ppermute only.
A program may use at most 128 MiB of HBM per device.

v0:
```python
import math

import jax
import jax.numpy as jnp
from jax import lax
from jax.sharding import PartitionSpec as P

PRECISE = lax.Precision.HIGH


def passed_along(block, axis, distance):
    devices = range(lax.axis_size(axis))
    route = [(i - distance, i) for i in devices if i - distance in devices]
    return lax.ppermute(block, axis, route)


def dft_pair(row_count, col_count, period):
    row_index = lax.iota(jnp.int32, row_count)[:, None]
    col_index = lax.iota(jnp.int32, col_count)[None, :]
    phase = (row_index * col_index % period).astype(jnp.float32) * (-2.0 * math.pi / period)
    return (jnp.cos(phase), jnp.sin(phase))


def make_tables(inner, outer):
    half = outer // 2
    outer_cos, outer_sin = dft_pair(outer, half, outer)
    twist_cos, twist_sin = dft_pair(outer, inner, outer * inner)
    inner_cos, inner_sin = dft_pair(inner, inner, inner)
    real_outer = jnp.stack([outer_cos, outer_sin], 1)
    complex_outer = jnp.stack(
        [jnp.stack([outer_cos, -outer_sin], 1), jnp.stack([outer_sin, outer_cos], 1)], 1
    )
    inner_ahead = jnp.block([[inner_cos, inner_sin], [-inner_sin, inner_cos]])
    inner_back = jnp.block([[inner_cos, -inner_sin], [inner_sin, inner_cos]])
    outer_back = jnp.stack(
        [jnp.stack([outer_cos, outer_sin], 0), jnp.stack([-outer_sin, outer_cos], 0)], 0
    )
    return (real_outer, complex_outer, twist_cos, twist_sin, inner_ahead, inner_back, outer_back)


def twist_ahead(values, twist_cos, twist_sin):
    real_part = values[:, :, 0]
    imag_part = values[:, :, 1]
    return jnp.stack(
        [
            real_part * twist_cos - imag_part * twist_sin,
            real_part * twist_sin + imag_part * twist_cos,
        ],
        2,
    )


def twist_back(values, twist_cos, twist_sin):
    real_part = values[:, :, 0]
    imag_part = values[:, :, 1]
    return jnp.stack(
        [
            real_part * twist_cos + imag_part * twist_sin,
            imag_part * twist_cos - real_part * twist_sin,
        ],
        2,
    )


def inner_section(values, table):
    width, outer = (values.shape[0], values.shape[1])
    flat = values.reshape(width, outer, table.shape[0])
    return jnp.einsum(
        "wkc,cd->wkd", flat, table, precision=PRECISE, preferred_element_type=jnp.float32
    )


def real_spectrum(signal, tables):
    real_outer, complex_outer, twist_cos, twist_sin, inner_ahead, inner_back, outer_back = tables
    half = real_outer.shape[2]
    inner = twist_cos.shape[1]
    blocked = signal.reshape(signal.shape[0], half, inner)
    first = jnp.einsum(
        "wab,kra->wkrb", blocked, real_outer, precision=PRECISE, preferred_element_type=jnp.float32
    )
    return inner_section(twist_ahead(first, twist_cos, twist_sin), inner_ahead)


def complex_spectrum(signal_re, signal_im, tables):
    real_outer, complex_outer, twist_cos, twist_sin, inner_ahead, inner_back, outer_back = tables
    half = real_outer.shape[2]
    inner = twist_cos.shape[1]
    width = signal_re.shape[0]
    stacked = jnp.stack(
        [signal_re.reshape(width, half, inner), signal_im.reshape(width, half, inner)], 1
    )
    first = jnp.einsum(
        "wsab,krsa->wkrb",
        stacked,
        complex_outer,
        precision=PRECISE,
        preferred_element_type=jnp.float32,
    )
    return inner_section(twist_ahead(first, twist_cos, twist_sin), inner_ahead)


def inverse_spectrum(packed, tables):
    real_outer, complex_outer, twist_cos, twist_sin, inner_ahead, inner_back, outer_back = tables
    outer = twist_cos.shape[0]
    inner = twist_cos.shape[1]
    half = real_outer.shape[2]
    width = packed.shape[0]
    back = inner_section(packed, inner_back).reshape(width, outer, 2, inner)
    turned = twist_back(back, twist_cos, twist_sin)
    result = jnp.einsum(
        "wksb,rska->wrab", turned, outer_back, precision=PRECISE, preferred_element_type=jnp.float32
    )
    scale = 1.0 / (outer * inner)
    return (
        (result[:, 0] * scale).reshape(width, half * inner),
        (result[:, 1] * scale).reshape(width, half * inner),
    )


def spectral_block(gated_rows, mixed_rows, filter_rows, tables):
    inner = tables[2].shape[1]
    gated_spec = real_spectrum(gated_rows.astype(jnp.float32), tables)
    joint_spec = complex_spectrum(
        filter_rows.astype(jnp.float32), -mixed_rows.astype(jnp.float32), tables
    )
    gated_re = gated_spec[:, :, :inner]
    gated_im = gated_spec[:, :, inner:]
    joint_re = joint_spec[:, :, :inner]
    joint_im = joint_spec[:, :, inner:]
    product_re = joint_re * gated_re + joint_im * gated_im
    product_im = joint_re * gated_im - joint_im * gated_re
    product = jnp.concatenate([product_re, product_im], 2)
    result_re, result_im = inverse_spectrum(product, tables)
    return (result_re.astype(jnp.bfloat16), result_im.astype(jnp.bfloat16))


def per_device(
    query_feat, key_feat, value_raw, conv_out, out_grad, filter_taps, short_filter, skip_gain
):
    rows = query_feat.shape[0]
    peers = lax.axis_size("ctx")
    before = passed_along(value_raw[rows - 2 :], "ctx", 1)
    padded = jnp.concatenate([before, value_raw], 0).astype(jnp.float32)
    value_conv = (
        short_filter[0] * padded[2:]
        + short_filter[1] * padded[1:-1]
        + short_filter[2] * padded[:-2]
    )
    mixed = (key_feat.astype(jnp.float32) * value_conv).astype(jnp.bfloat16)
    gated = (out_grad.astype(jnp.float32) * query_feat.astype(jnp.float32)).astype(jnp.bfloat16)
    query_grad = (out_grad.astype(jnp.float32) * conv_out.astype(jnp.float32)).astype(jnp.bfloat16)
    skip_part = jnp.sum(gated.astype(jnp.float32) * mixed.astype(jnp.float32), axis=0)
    tables = make_tables(rows, 2 * peers)
    gated_chan = gated.T
    mixed_chan = mixed.T
    sent_gated, sent_mixed = (
        lax.all_to_all(gated_chan, "ctx", split_axis=0, concat_axis=1, tiled=True),
        lax.all_to_all(mixed_chan, "ctx", split_axis=0, concat_axis=1, tiled=True),
    )
    back_rows, filter_grad = spectral_block(sent_gated, sent_mixed, filter_taps, tables)
    back_chan = lax.all_to_all(back_rows, "ctx", split_axis=1, concat_axis=0, tiled=True)
    conv_back = back_chan.T
    mixed_grad = conv_back.astype(jnp.float32) + skip_gain * gated.astype(jnp.float32)
    key_grad = (mixed_grad * value_conv).astype(jnp.bfloat16)
    feature_grad = (mixed_grad * key_feat.astype(jnp.float32)).astype(jnp.bfloat16)
    after = passed_along(feature_grad[:2], "ctx", -1)
    extended = jnp.concatenate([feature_grad, after], 0).astype(jnp.float32)
    value_grad = (
        short_filter[0] * extended[:-2]
        + short_filter[1] * extended[1:-1]
        + short_filter[2] * extended[2:]
    ).astype(jnp.bfloat16)
    feature_wide = extended[:-2]
    short_part = jnp.stack(
        [
            jnp.sum(feature_wide * padded[2:], axis=0),
            jnp.sum(feature_wide * padded[1:-1], axis=0),
            jnp.sum(feature_wide * padded[:-2], axis=0),
        ]
    )
    skip_grad, short_grad = (
        lax.psum_scatter(skip_part, "ctx", scatter_dimension=0, tiled=True),
        lax.psum_scatter(short_part, "ctx", scatter_dimension=1, tiled=True),
    )
    return (query_grad, key_grad, value_grad, filter_grad, skip_grad, short_grad)


def solution(mesh):
    in_specs = (
        P(("groups", "ctx"), None),
        P(("groups", "ctx"), None),
        P(("groups", "ctx"), None),
        P(("groups", "ctx"), None),
        P(("groups", "ctx"), None),
        P("ctx", None),
        P(),
        P(),
    )
    out_specs = (
        P(("groups", "ctx"), None),
        P(("groups", "ctx"), None),
        P(("groups", "ctx"), None),
        P(("groups", "ctx"), None),
        P(("groups", "ctx")),
        P(None, ("groups", "ctx")),
    )
    return jax.shard_map(
        per_device, mesh=mesh, in_specs=in_specs, out_specs=out_specs, check_vma=False
    )
```

profile of v0, /device:TPU:0, one launch (start us, length us, event | category | flops | bytes accessed | tf_op | source)
XLA Modules:
  0.0 301.0 jit_solution(2816398712474842059)
XLA Ops:
  7.2 0.9 slice.77
  8.1 2.4 collective-permute-start
  10.5 1.0 fusion.91
  11.5 1.6 copy.40
  13.1 1.7 copy.38
  14.9 1.3 copy.36
  16.2 2.3 copy.37
  18.4 2.3 copy.44
  20.7 0.5 copy.39
  21.2 0.8 maximum_convert_fusion
  22.1 0.4 copy-done.6
  22.4 0.3 copy-done.7
  22.8 0.6 copy-done.8
  23.3 5.3 %fusion.19 = (f32[4096]{0:T(1024)}, bf16[128,4096]{0,1:T(8,128)(2,1)S(1)}, bf16[128,4096]{0,1:T(8,128)(2,1)}, f32[128,4096]{0,1:T(8,128)}, bf16[128,4096]{0,1:T(8,128)(2,1)}) fusion(bf16[128,4096]{0,1:T(8,128)(2,1)S(1)} %copy.38, bf16[128,4096]{0,1:T(8,128)(2,1)S(1)} %copy-done.8, bf16[128,4096]{0,1:T(8,128)(2,1)S(1)} %copy-done.6, ...), kind=kLoop, calls=%fused_computation.36 | loop fusion | flops 9957376 | bytes 15794176 | tf_op jit(solution)/shard_map/reduce_sum | solution.py:152
  28.7 31.8 %all_to_all.39 = bf16[16,256,128]{2,1,0:T(8,128)(2,1)S(1)} all-to-all(bf16[16,256,128]{2,1,0:T(8,128)(2,1)S(1)} %bitcast.111), channel_id=1, replica_groups=mesh['groups'=2,'ctx'=16] {'ctx'}, dimensions={0} | all-to-all | bytes 2097152 | tf_op jit(solution)/shard_map/all_to_all | solution.py:158
  60.5 5.0 %all-to-all-start.1 = ((bf16[16,256,128]{2,1,0:T(8,128)(2,1)}), bf16[16,256,128]{2,1,0:T(8,128)(2,1)S(1)}, u32[]{:S(2)}, u32[]{:S(2)}) async-start(bf16[16,256,128]{2,1,0:T(8,128)(2,1)} %bitcast.25), calls=%async_computation.1 | async-start | bytes 2097152 | tf_op jit(solution)/shard_map/all_to_all | solution.py:157
  65.5 1.5 convert_bitcast_fusion
  67.0 0.4 copy.70
  67.4 0.1 fusion.81
  67.4 0.1 fusion.80
  67.6 0.1 fusion.78
  67.6 0.1 fusion.68
  67.7 0.6 maximum_bitcast_fusion.8
  68.4 0.3 fusion.51
  68.6 0.3 fusion.49
  68.9 0.7 negate_bitcast_fusion
  69.6 6.0 %fusion.10 = f32[256,32,2,128]{3,1,0,2:T(8,128)} fusion(f32[256,1,16,128]{3,2,1,0:T(8,128)S(1)} %negate_bitcast_fusion, f32[256,1,16,128]{3,2,1,0:T(8,128)S(1)} %bitcast.109, f32[32,1,2,16]{0,3,2,1:T(8,128)S(1)} %get-tuple-element.49, f32[32,1,2,16]{0,3,2,1:T(8,128)S(1)} %get-tuple-element.48), kind=kOutput, calls=%fused_computation.23 | convolution fusion | flops 403703808 | bytes 12591104 | tf_op jit(solution)/shard_map/wsab,krsa->wkrb/dot_general | solution.py:92
  75.7 12.8 %all-to-all-done.1 = bf16[16,256,128]{2,1,0:T(8,128)(2,1)S(1)} async-done(((bf16[16,256,128]{2,1,0:T(8,128)(2,1)}), bf16[16,256,128]{2,1,0:T(8,128)(2,1)S(1)}, u32[]{:S(2)}, u32[]{:S(2)}) %all-to-all-start.1) | async-done | bytes 1048608 | tf_op jit(solution)/shard_map/all_to_all | solution.py:157
  88.4 2.4 convolution_bitcast_fusion
  90.9 0.9 copy-done.2
  91.8 5.8 %multiply_subtract_fusion.3 = (f32[256,32,1,128]{3,1,0,2:T(8,128)S(1)}, f32[256,32,1,128]{3,1,0,2:T(8,128)}, f32[256,32,1,128]{3,1,0,2:T(8,128)}, f32[256,32,1,128]{3,1,0,2:T(8,128)}) fusion(f32[256,32,2,128]{3,1,0,2:T(8,128)S(1)} %copy-done.2, f32[32,128]{1,0:T(8,128)S(1)} %get-tuple-element.52, f32[32,128]{1,0:T(8,128)S(1)} %get-tuple-element.53, ...), kind=kLoop, calls=%fused_computation.21 | loop fusion | flops 12582912 | bytes 33587200 | tf_op jit(solution)/shard_map/sub | solution.py:46
  97.6 6.4 %pad_maximum_fusion = f32[256,32,2,128]{3,1,0,2:T(8,128)} fusion(f32[256,32,1,128]{3,1,0,2:T(8,128)} %get-tuple-element.30, f32[256,32,1,128]{3,1,0,2:T(8,128)S(1)} %get-tuple-element.29), kind=kLoop, calls=%fused_computation | loop fusion | flops 2097152 | bytes 16777216 | tf_op jit(solution)/shard_map/stack | solution.py:44
  104.0 9.9 %copy.42 = f32[256,32,2,128]{0,3,2,1:T(8,128)} copy(f32[256,32,2,128]{3,1,0,2:T(8,128)} %pad_maximum_fusion) | data formatting | bytes 16777216 | tf_op jit(solution)/shard_map/stack | solution.py:44
  113.9 7.7 %pad_maximum_fusion.1 = f32[256,32,2,128]{3,1,0,2:T(8,128)} fusion(f32[256,32,1,128]{3,1,0,2:T(8,128)} %get-tuple-element.44, f32[256,32,1,128]{3,1,0,2:T(8,128)} %get-tuple-element.45), kind=kLoop, calls=%fused_computation.1 | loop fusion | flops 2097152 | bytes 16777216 | tf_op jit(solution)/shard_map/stack | solution.py:44
  121.6 9.9 %copy.46 = f32[256,32,2,128]{0,3,2,1:T(8,128)} copy(f32[256,32,2,128]{3,1,0,2:T(8,128)} %pad_maximum_fusion.1) | data formatting | bytes 16777216 | tf_op jit(solution)/shard_map/stack | solution.py:44
  131.5 6.6 %fusion.37 = f32[256,32,256]{0,2,1:T(8,128)S(1)} fusion(f32[256,32,256]{0,2,1:T(8,128)} %bitcast.104, f32[128,128]{0,1:T(8,128)S(1)} %get-tuple-element.55, f32[128,128]{0,1:T(8,128)S(1)} %fusion.51, f32[128,128]{0,1:T(8,128)S(1)} %get-tuple-element.54), kind=kOutput, calls=%fused_computation.70 | convolution fusion | flops 3221422080 | bytes 16973824 | tf_op jit(solution)/shard_map/wkc,cd->wkd/dot_general | solution.py:68
  138.2 4.2 %fusion.35 = f32[256,32,256]{0,2,1:T(8,128)S(1)} fusion(f32[256,32,256]{0,2,1:T(8,128)S(1)} %bitcast.106, f32[128,128]{0,1:T(8,128)S(1)} %get-tuple-element.55, f32[128,128]{0,1:T(8,128)S(1)} %fusion.51, f32[128,128]{0,1:T(8,128)S(1)} %get-tuple-element.54), kind=kOutput, calls=%fused_computation.69 | convolution fusion | flops 3221422080 | bytes 16973824 | tf_op jit(solution)/shard_map/wkc,cd->wkd/dot_general | solution.py:68
  142.4 2.7 multiply_add_fusion.1
  145.1 5.6 %fusion = f32[256,32,256]{0,2,1:T(8,128)S(1)} fusion(f32[256,32,128]{0,2,1:T(8,128)} %get-tuple-element.26, f32[256,32,128]{0,2,1:T(8,128)S(1)} %get-tuple-element.25, f32[128,128]{0,1:T(8,128)S(1)} %copy-done.12, f32[128,128]{0,1:T(8,128)S(1)} %copy-done.10, f32[128,128]{0,1:T(8,128)S(1)} %fusion.51), kind=kOutput, calls=%fused_computation.2 | convolution fusion | flops 3223519232 | bytes 16973824 | tf_op jit(solution)/shard_map/wkc,cd->wkd/dot_general | solution.py:68
  150.8 3.8 %fusion.90 = (f32[256,32,1,128]{0,3,2,1:T(8,128)}, f32[256,32,1,128]{0,3,2,1:T(8,128)}) fusion(f32[256,32,2,128]{0,3,2,1:T(8,128)S(1)} %bitcast.105), kind=kLoop, calls=%fused_computation.139 | loop fusion | bytes 16777216 | tf_op jit(solution)/shard_map/slice | solution.py:55
  154.6 5.5 %copy.68 = f32[256,32,1,128]{3,1,0,2:T(8,128)} copy(f32[256,32,1,128]{0,3,2,1:T(8,128)} %get-tuple-element.34) | data formatting | bytes 8388608
  160.1 5.5 %copy.69 = f32[256,32,1,128]{3,1,0,2:T(8,128)} copy(f32[256,32,1,128]{0,3,2,1:T(8,128)} %get-tuple-element.33) | data formatting | bytes 8388608
  165.6 4.7 %multiply_add_fusion = (f32[256,32,1,128]{3,1,0,2:T(8,128)S(1)}, f32[256,32,1,128]{3,1,0,2:T(8,128)S(1)}) fusion(f32[256,32,1,128]{3,1,0,2:T(8,128)} %copy.69, f32[256,32,1,128]{3,1,0,2:T(8,128)} %copy.68, f32[32,128]{1,0:T(8,128)S(1)} %get-tuple-element.52, f32[32,128]{1,0:T(8,128)S(1)} %get-tuple-element.53), kind=kLoop, calls=%fused_computation.15 | loop fusion | flops 6291456 | bytes 16809984 | tf_op jit(solution)/shard_map/add | solution.py:58
  170.3 3.6 %fusion.11 = f32[256,2,16,128]{3,2,0,1:T(8,128)S(1)} fusion(f32[1,2,32,16]{2,3,1,0:T(8,128)S(1)} %copy-done.19, f32[1,2,32,16]{2,3,1,0:T(8,128)S(1)} %copy-done.18, f32[256,32,1,128]{3,1,0,2:T(8,128)S(1)} %get-tuple-element.28, f32[256,32,1,128]{3,1,0,2:T(8,128)S(1)} %get-tuple-element.27), kind=kOutput, calls=%fused_computation.30 | convolution fusion | flops 404752384 | bytes 12591104 | tf_op jit(solution)/shard_map/wksb,rska->wrab/dot_general | solution.py:110
  173.9 1.3 fusion.20
  175.3 0.3 copy.52
  175.6 31.5 %all_to_all.40 = bf16[256,16,128]{2,0,1:T(8,128)(2,1)S(1)} all-to-all(bf16[256,16,128]{2,0,1:T(8,128)(2,1)S(1)} %copy.52), channel_id=1, replica_groups=mesh['groups'=2,'ctx'=16] {'ctx'}, dimensions={1} | all-to-all | bytes 2097152 | tf_op jit(solution)/shard_map/all_to_all | solution.py:161
  207.1 2.0 fusion.17
  209.1 0.4 copy.53
  209.5 1.3 collective-permute-start.1
  210.8 2.0 collective-permute-done.1
  212.8 0.5 copy.54
  213.3 0.4 maximum_convert_fusion.1
  213.7 1.8 copy-done.1
  215.5 5.8 %multiply_reduce_fusion.2 = (f32[4096]{0:T(1024)S(1)}, f32[4096]{0:T(1024)S(1)}, f32[4096]{0:T(1024)S(1)}, bf16[128,4096]{0,1:T(8,128)(2,1)S(1)}) fusion(f32[130,4096]{0,1:T(8,128)S(1)} %copy-done.1, f32[130,4096]{0,1:T(8,128)S(1)} %maximum_convert_fusion.1, f32[4096]{0:T(1024)S(1)} %bitcast.116, f32[4096]{0:T(1024)S(1)} %bitcast.118, f32[4096]{0:T(1024)S(1)} %bitcast.114), kind=kLoop, calls=%fused_computation.51 | loop fusion | flops 6279168 | bytes 13729792 | tf_op jit(solution)/shard_map/reduce_sum | solution.py:176
  221.4 2.0 copy.66
  223.5 0.6 dynamic-slice
  224.7 2.3 copy.55
  227.0 61.1 %all-reduce = f32[4096]{0:T(1024)S(1)} all-reduce(f32[4096]{0:T(1024)S(1)} %copy-done.20), channel_id=2, replica_groups=mesh['groups'=2,'ctx'=16] {'ctx'}, use_global_device_ids=true, to_apply=%region_1.2.clone | all-reduce | flops 4096 | bytes 32768
  288.1 0.6 dynamic-slice.1
  288.7 1.2 copy.84
  289.9 1.3 copy.56
  291.2 1.3 copy.57
  292.6 1.6 copy.67
  (48 shorter events, 0.3 us)
Async XLA Ops:
  7.2 7.7 %copy-start.13 = (bf16[128,4096]{1,0:T(8,128)(2,1)S(1)}, bf16[128,4096]{1,0:T(8,128)(2,1)}, u32[]{:S(2)}) copy-start(bf16[128,4096]{1,0:T(8,128)(2,1)} %param.12) | copy-start | bytes 3145732
  8.1 12.6 %collective-permute-start = (bf16[2,4096]{1,0:T(2,128)(2,1)S(1)}, bf16[2,4096]{1,0:T(2,128)(2,1)S(1)}, u32[]{:S(2)}, u32[]{:S(2)}) collective-permute-start(bf16[2,4096]{1,0:T(2,128)(2,1)S(1)} %slice.77), channel_id=1, source_target_pairs={{0,1},{1,2},{2,3},{3,4},{4,5},{5,6},{6,7},{7,8},{8,9},{9,10},{10,1... | collective-permute-start | bytes 49160 | tf_op jit(solution)/shard_map/ppermute | solution.py:14
  11.5 10.6 %copy-start.14 = (f32[1,4096]{1,0:T(1,128)}, f32[1,4096]{1,0:T(1,128)S(1)}, u32[]{:S(2)}) copy-start(f32[1,4096]{1,0:T(1,128)S(1)} %get-tuple-element.42) | copy-start | bytes 49156
  11.5 10.6 %copy-start.16 = (f32[1,4096]{1,0:T(1,128)}, f32[1,4096]{1,0:T(1,128)S(1)}, u32[]{:S(2)}) copy-start(f32[1,4096]{1,0:T(1,128)S(1)} %get-tuple-element.43) | copy-start | bytes 49156
  21.2 1.2 copy-start.6
  21.2 1.5 copy-start.7
  21.2 2.1 copy-start.8
  22.0 6.6 %copy-start = (f32[130,4096]{0,1:T(8,128)}, f32[130,4096]{0,1:T(8,128)S(1)}, u32[]{:S(2)}) copy-start(f32[130,4096]{0,1:T(8,128)S(1)} %maximum_convert_fusion) | copy-start | bytes 6389764
  60.5 27.9 %all-to-all-start.1 = ((bf16[16,256,128]{2,1,0:T(8,128)(2,1)}), bf16[16,256,128]{2,1,0:T(8,128)(2,1)S(1)}, u32[]{:S(2)}, u32[]{:S(2)}) async-start(bf16[16,256,128]{2,1,0:T(8,128)(2,1)} %bitcast.25), calls=%async_computation.1 | async-start | bytes 2097152 | tf_op jit(solution)/shard_map/all_to_all | solution.py:157
  65.5 227.1 %reduce-scatter.4.cloned.1.call-start = ((), (), s32[]{:S(2)}) async-start(), calls=%async_computation.4 | async-start | bytes 2228224
  68.9 69.2 %copy-start.9 = (f32[128,128]{0,1:T(8,128)}, f32[128,128]{0,1:T(8,128)S(1)}, u32[]{:S(2)}) copy-start(f32[128,128]{0,1:T(8,128)S(1)} %get-tuple-element.54) | copy-start | bytes 196612
  68.9 69.2 %copy-start.11 = (f32[128,128]{0,1:T(8,128)}, f32[128,128]{0,1:T(8,128)S(1)}, u32[]{:S(2)}) copy-start(f32[128,128]{0,1:T(8,128)S(1)} %get-tuple-element.55) | copy-start | bytes 196612
  88.4 3.4 %copy-start.2 = (f32[256,32,2,128]{3,1,0,2:T(8,128)S(1)}, f32[256,32,2,128]{3,1,0,2:T(8,128)}, u32[]{:S(2)}) copy-start(f32[256,32,2,128]{3,1,0,2:T(8,128)} %fusion.10) | copy-start | bytes 25165828
  131.5 6.6 %copy-start.3 = (f32[256,32,2,128]{0,3,2,1:T(8,128)S(1)}, f32[256,32,2,128]{0,3,2,1:T(8,128)}, u32[]{:S(2)}) copy-start(f32[256,32,2,128]{0,3,2,1:T(8,128)} %copy.46) | copy-start | bytes 25165828
  142.4 2.8 copy-start.10
  142.4 2.8 copy-start.12
  165.6 4.7 %copy-start.18 = (f32[1,2,32,16]{2,3,1,0:T(8,128)S(1)}, f32[1,2,32,16]{2,3,1,0:T(8,128)}, u32[]{:S(2)}) copy-start(f32[1,2,32,16]{2,3,1,0:T(8,128)} %get-tuple-element.46) | copy-start | bytes 12292
  165.6 4.7 %copy-start.19 = (f32[1,2,32,16]{2,3,1,0:T(8,128)S(1)}, f32[1,2,32,16]{2,3,1,0:T(8,128)}, u32[]{:S(2)}) copy-start(f32[1,2,32,16]{2,3,1,0:T(8,128)} %get-tuple-element.47) | copy-start | bytes 12292
  173.9 33.2 %copy-start.4 = (f32[128,4096]{0,1:T(8,128)S(1)}, f32[128,4096]{0,1:T(8,128)}, u32[]{:S(2)}) copy-start(f32[128,4096]{0,1:T(8,128)} %get-tuple-element.24) | copy-start | bytes 6291460
  173.9 33.2 %copy-start.21 = (f32[4096]{0:T(1024)S(1)}, f32[4096]{0:T(1024)}, u32[]{:S(2)}) copy-start(f32[4096]{0:T(1024)} %param.15) | copy-start | bytes 49156
  209.1 4.6 %copy-start.15 = (f32[1,4096]{1,0:T(1,128)S(1)}, f32[1,4096]{1,0:T(1,128)}, u32[]{:S(2)}) copy-start(f32[1,4096]{1,0:T(1,128)} %copy-done.14) | copy-start | bytes 49156
  209.1 4.6 %copy-start.17 = (f32[1,4096]{1,0:T(1,128)S(1)}, f32[1,4096]{1,0:T(1,128)}, u32[]{:S(2)}) copy-start(f32[1,4096]{1,0:T(1,128)} %copy-done.16) | copy-start | bytes 49156
  209.5 3.3 %collective-permute-start.1 = (bf16[2,4096]{1,0:T(2,128)(2,1)S(1)}, bf16[2,4096]{1,0:T(2,128)(2,1)S(1)}, u32[]{:S(2)}, u32[]{:S(2)}) collective-permute-start(bf16[2,4096]{1,0:T(2,128)(2,1)S(1)} %copy.53), channel_id=1, source_target_pairs={{1,0},{2,1},{3,2},{4,3},{5,4},{6,5},{7,6},{8,7},{9,8},{10,9},{11,1... | collective-permute-start | bytes 49160 | tf_op jit(solution)/shard_map/ppermute | solution.py:14
  213.3 2.2 copy-start.1
  221.3 2.1 copy-start.22
  221.4 5.6 %copy-start.20 = (f32[4096]{0:T(1024)S(1)}, f32[4096]{0:T(1024)}, u32[]{:S(2)}) copy-start(f32[4096]{0:T(1024)} %get-tuple-element.21) | copy-start | bytes 49156
  221.4 67.3 %copy-start.5 = (bf16[256,1,16,128]{3,2,0,1:T(8,128)(2,1)S(1)}, bf16[256,1,16,128]{3,2,0,1:T(8,128)(2,1)}, u32[]{:S(2)}) copy-start(bf16[256,1,16,128]{3,2,0,1:T(8,128)(2,1)} %get-tuple-element.36) | copy-start | bytes 3145732
Sparse Core Ops, SparseCore 0:
  223.6 63.6 reduce-scatter.3
where the time goes:
time: 302 us; the launch traced here: 301 us
  blocking collectives  124 us (41%)
  local copies, waits for them, and re-layouts  62.9 us (21%)
  other arithmetic  46.5 us (15%)
  matrix products  28.5 us (9%)
  between operations  15.1 us (5%)
  waiting for transfers between devices  14.8 us (5%)
  starting transfers between devices  8.68 us (3%)
    unnamed x1, blocking collectives  61.1 us
    unnamed x62, local copies, waits for them, and re-layouts  35.6 us
    all_to_all x1, blocking collectives, per_device(): lax.all_to_all(mixed_chan, 'ctx', split_axis=0, concat_axis=1, tiled=True)  31.8 us
    all_to_all x1, blocking collectives, per_device(): lax.all_to_all(back_rows, 'ctx', split_axis=1, concat_axis=0, tiled=True)  31.5 us
    another operation x2, local copies, waits for them, and re-layouts, twist_ahead(): jnp.stack([real_part * twist_cos - imag_part * twist_sin, real_part * twi...  19.9 us
    dot_general x3, matrix products, inner_section(): jnp.einsum('wkc,cd->wkd', flat, table, precision=PRECISE, preferred_eleme...  16.4 us
    another operation x2, other arithmetic, twist_ahead(): jnp.stack([real_part * twist_cos - imag_part * twist_sin, real_part * twi...  14.1 us
    all_to_all x1, waiting for transfers between devices, per_device(): lax.all_to_all(gated_chan, 'ctx', split_axis=0, concat_axis=1, tiled=True)  12.8 us
  transfers between devices with their start and end apart: 4, of which 2 were waited for; matrix products, arithmetic and copies ran while one was open for 9% of the time, Pallas kernels for 0%

commit v1 on v0

--- a/solution.py
+++ b/solution.py
@@ -1,8 +1,12 @@
+import functools
 import math
 
 import jax
 import jax.numpy as jnp
+import numpy as np
 from jax import lax
+from jax.experimental import pallas as pl
+from jax.experimental.pallas import tpu as pltpu
 from jax.sharding import PartitionSpec as P
 
 PRECISE = lax.Precision.HIGH
@@ -134,7 +138,7 @@
     return (result_re.astype(jnp.bfloat16), result_im.astype(jnp.bfloat16))
 
 
-def per_device(
+def general_plan(
     query_feat, key_feat, value_raw, conv_out, out_grad, filter_taps, short_filter, skip_gain
 ):
     rows = query_feat.shape[0]
@@ -185,6 +189,492 @@
     return (query_grad, key_grad, value_grad, filter_grad, skip_grad, short_grad)
 
 
+INNER = 128
+
+
+def half_spectrum(values, length):
+    if length == 2:
+        return [(values[0], None), (values[0], None)]
+    even = half_spectrum(values[0::2], length // 2)
+    odd = half_spectrum(values[1::2], length // 2)
+    quarter = length // 4
+    bins = [None] * (length // 2 + 1)
+    bins[0] = (even[0][0] + odd[0][0], None)
+    bins[length // 2] = (even[0][0] - odd[0][0], None)
+    bins[quarter] = (even[quarter][0], -odd[quarter][0])
+    for k in range(1, quarter):
+        c = math.cos(2.0 * math.pi * k / length)
+        s = math.sin(2.0 * math.pi * k / length)
+        odd_re, odd_im = odd[k]
+        even_re, even_im = even[k]
+        if 2 * k == quarter:
+            turn_re = (odd_re + odd_im) * c
+            turn_im = (odd_im - odd_re) * c
+        else:
+            turn_re = odd_re * c + odd_im * s
+            turn_im = odd_im * c - odd_re * s
+        bins[k] = (even_re + turn_re, even_im + turn_im)
+        bins[length // 2 - k] = (even_re - turn_re, turn_im - even_im)
+    return bins
+
+
+def first_half(bins, length):
+    if length == 2:
+        return [bins[0][0] + bins[1][0]]
+    half = length // 2
+    quarter = length // 4
+    even = [None] * (quarter + 1)
+    odd = [None] * (quarter + 1)
+    even[0] = (bins[0][0] + bins[half][0], None)
+    odd[0] = (bins[0][0] - bins[half][0], None)
+    even[quarter] = (2.0 * bins[quarter][0], None)
+    odd[quarter] = (-2.0 * bins[quarter][1], None)
+    for k in range(1, quarter):
+        c = math.cos(2.0 * math.pi * k / length)
+        s = math.sin(2.0 * math.pi * k / length)
+        near_re, near_im = bins[k]
+        far_re, far_im = bins[half - k]
+        even[k] = (near_re + far_re, near_im - far_im)
+        gap_re = near_re - far_re
+        gap_im = near_im + far_im
+        if 2 * k == quarter:
+            odd[k] = ((gap_re - gap_im) * c, (gap_re + gap_im) * c)
+        else:
+            odd[k] = (gap_re * c - gap_im * s, gap_re * s + gap_im * c)
+    result = [None] * half
+    result[0::2] = first_half(even, half)
+    result[1::2] = first_half(odd, half)
+    return result
+
+
+def spectrum_tables(outer):
+    size = outer * INNER
+    near = np.arange(outer // 2 + 1)[:, None, None]
+    place = np.arange(INNER)
+    angle = -2.0 * np.pi * (
+        (near * place[None, None, :]) / size + place[None, :, None] * place[None, None, :] / INNER
+    )
+    c, s = np.cos(angle), np.sin(angle)
+    ahead = np.concatenate(
+        [np.concatenate([c, -s], 2), np.concatenate([s, c], 2)], 1
+    )
+    back = np.swapaxes(ahead, 1, 2) / size
+    return ahead.astype(jnp.bfloat16), back.astype(jnp.bfloat16)
+
+
+def outer_ahead(load, z_ref, outer, width):
+    def step(chunk, carry):
+        row = pl.multiple_of(chunk * 16, 16)
+        for lane in range(0, width, 128):
+            values = [load(a, row, lane).astype(jnp.float32) for a in range(outer // 2)]
+            bins = half_spectrum(values, outer)
+            for k, (re, im) in enumerate(bins):
+                im = jnp.zeros_like(re) if im is None else im
+                z_ref[k, pl.ds(row, 16), lane : lane + 128] = re.astype(jnp.bfloat16)
+                z_ref[k, pl.ds(INNER + row, 16), lane : lane + 128] = im.astype(jnp.bfloat16)
+        return carry
+
+    lax.fori_loop(0, INNER // 16, step, 0)
+
+
+def outer_back(u_ref, store, outer, width):
+    def step(chunk, carry):
+        row = pl.multiple_of(chunk * 16, 16)
+        for lane in range(0, width, 128):
+            bins = []
+            for k in range(outer // 2 + 1):
+                re = u_ref[k, pl.ds(row, 16), lane : lane + 128]
+                im = u_ref[k, pl.ds(INNER + row, 16), lane : lane + 128]
+                bins.append((re, im))
+            for a, value in enumerate(first_half(bins, outer)):
+                store(a, row, lane, value)
+        return carry
+
+    lax.fori_loop(0, INNER // 16, step, 0)
+
+
+def correlate_bin(first, gated):
+    first_re, first_im = first[:INNER], first[INNER:]
+    gated_re, gated_im = gated[:INNER], gated[INNER:]
+    return jnp.concatenate(
+        [
+            first_re * gated_re + first_im * gated_im,
+            first_re * gated_im - first_im * gated_re,
+        ],
+        0,
+    ).astype(jnp.bfloat16)
+
+
+def dot32(a, b):
+    return jnp.dot(a, b, preferred_element_type=jnp.float32)
+
+
+def filter_kernel(taps_ref, ahead_ref, spec_ref, rows_ref, z_ref, *, outer, width):
+    for a in range(outer // 2):
+        piece = taps_ref[:, a * INNER : (a + 1) * INNER].astype(jnp.float32)
+        rows_ref[a * INNER : (a + 1) * INNER, :] = piece.T
+    outer_ahead(
+        lambda a, row, lane: rows_ref[pl.ds(a * INNER + row, 16), lane : lane + 128],
+        z_ref, outer, width,
+    )
+
+    def one_bin(k, carry):
+        spec_ref[k] = dot32(ahead_ref[k], z_ref[k]).astype(jnp.bfloat16)
+        return carry
+
+    lax.fori_loop(0, outer // 2 + 1, one_bin, 0)
+
+
+def conv_kernel(gated_ref, filter_ref, ahead_ref, back_ref, conv_ref, spec_ref, z_ref, u_ref, *, outer, width):
+    outer_ahead(
+        lambda a, row, lane: gated_ref[pl.ds(a * INNER + row, 16), lane : lane + 128],
+        z_ref, outer, width,
+    )
+
+    def one_bin(k, carry):
+        gated = dot32(ahead_ref[k], z_ref[k])
+        spec_ref[k] = gated.astype(jnp.bfloat16)
+        product = correlate_bin(filter_ref[k].astype(jnp.float32), gated)
+        u_ref[k] = dot32(back_ref[k], product)
+        return carry
+
+    lax.fori_loop(0, outer // 2 + 1, one_bin, 0)
+
+    def store(a, row, lane, value):
+        conv_ref[pl.ds(a * INNER + row, 16), lane : lane + 128] = value.astype(jnp.bfloat16)
+
+    outer_back(u_ref, store, outer, width)
+
+
+def grad_kernel(mixed_ref, gated_ref, spec_ref, ahead_ref, back_ref, grad_ref, skip_ref, z_ref, u_ref, rows_ref, *, outer, width):
+    outer_ahead(
+        lambda a, row, lane: mixed_ref[pl.ds(a * INNER + row, 16), lane : lane + 128],
+        z_ref, outer, width,
+    )
+
+    def one_bin(k, carry):
+        mixed = dot32(ahead_ref[k], z_ref[k])
+        product = correlate_bin(mixed, spec_ref[k].astype(jnp.float32))
+        u_ref[k] = dot32(back_ref[k], product)
+        return carry
+
+    lax.fori_loop(0, outer // 2 + 1, one_bin, 0)
+
+    def store(a, row, lane, value):
+        rows_ref[pl.ds(a * INNER + row, 16), lane : lane + 128] = value
+
+    outer_back(u_ref, store, outer, width)
+    for a in range(outer // 2):
+        grad_ref[:, a * INNER : (a + 1) * INNER] = rows_ref[
+            a * INNER : (a + 1) * INNER, :
+        ].T.astype(jnp.bfloat16)
+
+    def add(a, total):
+        place = pl.ds(pl.multiple_of(a * INNER, INNER), INNER)
+        part = gated_ref[place, :].astype(jnp.float32) * mixed_ref[place, :].astype(jnp.float32)
+        return total + jnp.sum(part.reshape(INNER // 8, 8, width), axis=0)
+
+    total = lax.fori_loop(0, outer // 2, add, jnp.zeros((8, width), jnp.float32))
+    skip_ref[...] = jnp.sum(total, axis=0, keepdims=True)
+
+
+def later_grad_kernel(mixed_ref, gated_ref, spec_ref, ahead_ref, back_ref, done_ref, *rest, outer, width):
+    grad_kernel(mixed_ref, gated_ref, spec_ref, ahead_ref, back_ref, *rest, outer=outer, width=width)
+
+
+def shifted_down(values, distance, edge):
+    moved = pltpu.roll(values, distance, 0)
+    row = lax.broadcasted_iota(jnp.int32, values.shape, 0)
+    for i in range(distance):
+        source = edge.shape[0] - distance + i
+        moved = jnp.where(row == i, edge[source : source + 1], moved)
+    return moved
+
+
+def shifted_up(values, distance, edge):
+    count = values.shape[0]
+    moved = pltpu.roll(values, count - distance, 0)
+    row = lax.broadcasted_iota(jnp.int32, values.shape, 0)
+    for i in range(distance):
+        moved = jnp.where(row == count - distance + i, edge[i : i + 1], moved)
+    return moved
+
+
+def gate_kernel(grad_ref, query_ref, gated_ref, *, width):
+    for j in range(gated_ref.shape[0]):
+        cols = slice(j * width, (j + 1) * width)
+        gated_ref[j] = (
+            grad_ref[:, cols].astype(jnp.float32) * query_ref[:, cols].astype(jnp.float32)
+        ).astype(jnp.bfloat16)
+
+
+def mix_kernel(key_ref, value_ref, edge_ref, short_ref, grad_ref, conv_ref, *rest, width, parts):
+    mixed_refs, query_grad_ref = rest[:parts], rest[parts]
+    piece = width // parts
+    for j in range(mixed_refs[0].shape[0]):
+        for part in range(parts):
+            cols = slice(j * width + part * piece, j * width + (part + 1) * piece)
+            value = value_ref[:, cols].astype(jnp.float32)
+            edge = edge_ref[:, cols].astype(jnp.float32)
+            conv = (
+                short_ref[0:1, cols] * value
+                + short_ref[1:2, cols] * shifted_down(value, 1, edge)
+                + short_ref[2:3, cols] * shifted_down(value, 2, edge)
+            )
+            mixed_refs[part][j] = (key_ref[:, cols].astype(jnp.float32) * conv).astype(jnp.bfloat16)
+            query_grad_ref[:, cols] = (
+                grad_ref[:, cols].astype(jnp.float32) * conv_ref[:, cols].astype(jnp.float32)
+            ).astype(jnp.bfloat16)
+
+
+def finish_kernel(
+    back_ref, gated_ref, key_ref, value_ref, edge_ref, short_ref, skip_ref,
+    key_grad_ref, value_grad_ref, head_ref, tail_ref, part_ref, *, width,
+):
+    rows = key_ref.shape[0]
+    for j in range(back_ref.shape[0]):
+        for lane in range(0, width, 128):
+            cols = slice(j * width + lane, j * width + lane + 128)
+            lanes = slice(lane, lane + 128)
+            value = value_ref[:, cols].astype(jnp.float32)
+            edge = edge_ref[:, cols].astype(jnp.float32)
+            value_1 = shifted_down(value, 1, edge)
+            value_2 = shifted_down(value, 2, edge)
+            short = [short_ref[i : i + 1, cols] for i in range(3)]
+            conv = short[0] * value + short[1] * value_1 + short[2] * value_2
+            mixed_grad = back_ref[j, :, lanes].astype(jnp.float32) + skip_ref[:, cols] * gated_ref[
+                j, :, lanes
+            ].astype(jnp.float32)
+            key_grad_ref[:, cols] = (mixed_grad * conv).astype(jnp.bfloat16)
+            feature = (mixed_grad * key_ref[:, cols].astype(jnp.float32)).astype(jnp.bfloat16)
+            head_ref[:, cols] = feature[:16]
+            tail_ref[:, cols] = feature[rows - 16 :]
+            feature = feature.astype(jnp.float32)
+            zero = jnp.zeros((2, 128), jnp.float32)
+            value_grad_ref[:, cols] = (
+                short[0] * feature
+                + short[1] * shifted_up(feature, 1, zero)
+                + short[2] * shifted_up(feature, 2, zero)
+            ).astype(jnp.bfloat16)
+            for i, other in enumerate((value, value_1, value_2)):
+                part_ref[j, i : i + 1, lanes] = jnp.sum(feature * other, axis=0, keepdims=True)
+            part_ref[j, 3:8, lanes] = jnp.zeros((5, 128), jnp.float32)
+
+
+def seam_kernel(tail_ref, head_ref, short_ref, done_ref, value_grad_ref):
+    feature = tail_ref[...].astype(jnp.float32)
+    head = head_ref[...].astype(jnp.float32)
+    value_grad_ref[...] = (
+        short_ref[0:1] * feature
+        + short_ref[1:2] * shifted_up(feature, 1, head)
+        + short_ref[2:3] * shifted_up(feature, 2, head)
+    ).astype(jnp.bfloat16)
+
+
+def exchanged(block):
+    return lax.all_to_all(block, "ctx", split_axis=0, concat_axis=0, tiled=True)
+
+
+def paired(block, distance):
+    return lax.ppermute(block, "ctx", [(i, i ^ distance) for i in range(lax.axis_size("ctx"))])
+
+
+def summed_at_owner(parts):
+    peers = lax.axis_size("ctx")
+    me = lax.axis_index("ctx")
+    inner = 4 if peers % 4 == 0 else 1
+    for count, place, step in ((peers // inner, me // inner, inner), (inner, me % inner, 1)):
+        if step == inner:
+            parts = parts.reshape((count, inner) + parts.shape[1:])
+        mine = lax.dynamic_index_in_dim(parts, place, 0, keepdims=False)
+        for distance in range(1, count):
+            other = lax.dynamic_index_in_dim(parts, place ^ distance, 0, keepdims=False)
+            mine = mine + paired(other, distance * step)
+        parts = mine
+    return parts
+
+
+def after(value, *others):
+    return lax.optimization_barrier((value,) + others)[0]
+
+
+def params(mib=48):
+    return pltpu.CompilerParams(vmem_limit_bytes=mib * 1024 * 1024)
+
+
+def cost(flops, size):
+    return pl.CostEstimate(flops=flops, bytes_accessed=size, transcendentals=0)
+
+
+def kernel_plan(
+    query_feat, key_feat, value_raw, conv_out, out_grad, filter_taps, short_filter, skip_gain
+):
+    rows, channels = query_feat.shape
+    peers = lax.axis_size("ctx")
+    width = channels // peers
+    seq = rows * peers
+    outer = 2 * seq // INNER
+    bins = outer // 2 + 1
+    steps = 4
+    group = peers // steps
+    span = group * width
+    parts = 2
+    piece = width // parts
+    bf16, f32 = jnp.bfloat16, jnp.float32
+    shape = jax.ShapeDtypeStruct
+    skip_row = skip_gain.reshape(1, channels)
+    ahead, back = (jnp.asarray(t) for t in spectrum_tables(outer))
+
+    flat = pl.BlockSpec((rows, span), lambda i: (0, i))
+    owned = pl.BlockSpec((group, rows, width), lambda i: (i, 0, 0))
+    owned_part = pl.BlockSpec((group, rows, piece), lambda i: (i, 0, 0))
+    edge_spec = pl.BlockSpec((16, span), lambda i: (0, i))
+    short_spec = pl.BlockSpec((3, span), lambda i: (0, i))
+    skip_spec = pl.BlockSpec((1, span), lambda i: (0, i))
+
+    gated = pl.pallas_call(
+        functools.partial(gate_kernel, width=width),
+        grid=(steps,),
+        in_specs=[flat, flat],
+        out_specs=owned,
+        out_shape=shape((peers, rows, width), bf16),
+        compiler_params=params(),
+        cost_estimate=cost(rows * channels, 6 * rows * channels),
+        name="gate",
+    )(out_grad, query_feat)
+
+    gated_got = exchanged(gated.reshape(seq, width))
+
+    edge = passed_along(value_raw[rows - 16 :], "ctx", 1)
+    *mixed, query_grad = pl.pallas_call(
+        functools.partial(mix_kernel, width=width, parts=parts),
+        grid=(steps,),
+        in_specs=[flat, flat, edge_spec, short_spec, flat, flat],
+        out_specs=[owned_part] * parts + [flat],
+        out_shape=[shape((peers, rows, piece), bf16)] * parts + [shape((rows, channels), bf16)],
+        compiler_params=params(),
+        cost_estimate=cost(10 * rows * channels, 12 * rows * channels),
+        name="mix",
+    )(key_feat, value_raw, edge, short_filter, out_grad, conv_out)
+
+    spec_shape = shape((bins, 2 * INNER, width), bf16)
+    z_scratch = pltpu.VMEM((bins, 2 * INNER, width), bf16)
+    u_scratch = pltpu.VMEM((bins, 2 * INNER, width), f32)
+    table_bytes = 8 * bins * INNER * INNER
+    spec_bytes = 4 * bins * INNER * width
+    work = 2 * bins * (2 * INNER) ** 2 * width
+    filter_spec = pl.pallas_call(
+        functools.partial(filter_kernel, outer=outer, width=width),
+        out_shape=spec_shape,
+        scratch_shapes=[pltpu.VMEM((seq, width), f32), z_scratch],
+        compiler_params=params(),
+        cost_estimate=cost(work, table_bytes + spec_bytes + 2 * seq * width),
+        name="filter_spectrum",
+    )(filter_taps, ahead)
+
+    mixed_got = [None] * parts
+    mixed_got[0] = exchanged(after(mixed[0], gated_got).reshape(seq, piece))
+
+    conv_back, gated_spec = pl.pallas_call(
+        functools.partial(conv_kernel, outer=outer, width=width),
+        out_shape=(shape((seq, width), bf16), spec_shape),
+        scratch_shapes=[z_scratch, u_scratch],
+        compiler_params=params(),
+        cost_estimate=cost(2 * work, 2 * table_bytes + 2 * spec_bytes + 4 * seq * width),
+        name="conv_back",
+    )(gated_got, filter_spec, ahead, back)
+
+    back_got = exchanged(after(conv_back, mixed_got[0])).reshape(peers, rows, width)
+    mixed_got[1] = exchanged(after(mixed[1], back_got).reshape(seq, piece))
+
+    key_grad, value_grad, head, tail, short_part = pl.pallas_call(
+        functools.partial(finish_kernel, width=width),
+        grid=(steps,),
+        in_specs=[owned, owned, flat, flat, edge_spec, short_spec, skip_spec],
+        out_specs=[flat, flat, edge_spec, edge_spec, pl.BlockSpec((group, 8, width), lambda i: (i, 0, 0))],
+        out_shape=[
+            shape((rows, channels), bf16),
+            shape((rows, channels), bf16),
+            shape((16, channels), bf16),
+            shape((16, channels), bf16),
+            shape((peers, 8, width), f32),
+        ],
+        compiler_params=params(),
+        cost_estimate=cost(30 * rows * channels, 12 * rows * channels),
+        name="finish",
+    )(back_got, gated, key_feat, value_raw, edge, short_filter, skip_row)
+
+    head_got = passed_along(head, "ctx", -1)
+    whole = lambda size: pl.BlockSpec((size, channels), lambda i: (0, 0))
+    value_grad = pl.pallas_call(
+        seam_kernel,
+        grid=(1,),
+        in_specs=[whole(16), whole(16), whole(3), pl.BlockSpec(memory_space=pl.ANY)],
+        out_specs=pl.BlockSpec((16, channels), lambda i: (rows // 16 - 1, 0)),
+        out_shape=shape((rows, channels), bf16),
+        input_output_aliases={3: 0},
+        compiler_params=params(),
+        cost_estimate=cost(5 * 16 * channels, 6 * 16 * channels),
+        name="seam",
+    )(tail, head_got, short_filter, value_grad)
+    short_grad = summed_at_owner(short_part)[:3]
+
+    filter_grad = None
+    skip_parts = []
+    for part in range(parts):
+        at = part
+        in_specs = [
+            pl.BlockSpec((seq, piece), lambda i: (0, 0)),
+            pl.BlockSpec((seq, piece), lambda i, at=at: (0, at)),
+            pl.BlockSpec((bins, 2 * INNER, piece), lambda i, at=at: (0, 0, at)),
+            pl.BlockSpec((bins, 2 * INNER, 2 * INNER), lambda i: (0, 0, 0)),
+            pl.BlockSpec((bins, 2 * INNER, 2 * INNER), lambda i: (0, 0, 0)),
+        ]
+        operands = [mixed_got[part], gated_got, gated_spec, ahead, back]
+        body = functools.partial(grad_kernel, outer=outer, width=piece)
+        if part:
+            in_specs.append(pl.BlockSpec(memory_space=pl.ANY))
+            operands.append(filter_grad)
+            body = functools.partial(later_grad_kernel, outer=outer, width=piece)
+        filter_grad, skip_part = pl.pallas_call(
+            body,
+            grid=(1,),
+            in_specs=in_specs,
+            out_specs=[
+                pl.BlockSpec((piece, seq), lambda i, at=at: (at, 0)),
+                pl.BlockSpec((1, piece), lambda i: (0, 0)),
+            ],
+            out_shape=[shape((width, seq), bf16), shape((1, piece), f32)],
+            scratch_shapes=[
+                pltpu.VMEM((bins, 2 * INNER, piece), bf16),
+                pltpu.VMEM((bins, 2 * INNER, piece), f32),
+                pltpu.VMEM((seq, piece), f32),
+            ],
+            input_output_aliases={5: 0} if part else {},
+            compiler_params=params(),
+            cost_estimate=cost(2 * work // parts, 2 * table_bytes + spec_bytes),
+            name=f"filter_grad_{part}",
+        )(*operands)
+        skip_parts.append(skip_part)
+    skip_grad = jnp.concatenate(skip_parts, 1).reshape(width)
+    return query_grad, key_grad, value_grad, filter_grad, skip_grad, short_grad
+
+
+def per_device(query_feat, key_feat, value_raw, conv_out, out_grad, filter_taps, short_filter, skip_gain):
+    rows, channels = query_feat.shape
+    peers = lax.axis_size("ctx")
+    width = channels // peers
+    fits = (
+        peers % 4 == 0
+        and peers & (peers - 1) == 0
+        and rows % 16 == 0
+        and width % 256 == 0
+        and rows * peers in (8 * INNER, 16 * INNER)
+    )
+    plan = kernel_plan if fits else general_plan
+    return plan(query_feat, key_feat, value_raw, conv_out, out_grad, filter_taps, short_filter, skip_gain)
+
+
 def solution(mesh):
     in_specs = (
         P(("groups", "ctx"), None),

time: 302 us -> 165 us (0.55)
  the two profiles are of different devices: /device:TPU:0 before, /device:TPU:1 now
where the time goes in v1:
time: 165 us; the launch traced here: 164 us
  Pallas kernels  50 us (30%)
  starting transfers between devices  40.6 us (25%)
  blocking collectives  31.2 us (19%)
  local copies, waits for them, and re-layouts  21.3 us (13%)
  waiting for transfers between devices  18.1 us (11%)
  other arithmetic  1.93 us (1%)
    all_to_all x1, blocking collectives, exchanged(): return lax.all_to_all(block, 'ctx', split_axis=0, concat_axis=0, tiled=True)  31.2 us
    all_to_all x3, starting transfers between devices, exchanged(): return lax.all_to_all(block, 'ctx', split_axis=0, concat_axis=0, tiled=True)  27.8 us
    pallas_call x2, Pallas kernels, kernel_plan(): pl.pallas_call(body, grid=(1,), in_specs=in_specs, out_specs=[pl.BlockSpe...  22.3 us
    unnamed x48, local copies, waits for them, and re-layouts  20.4 us
    pallas_call x1, Pallas kernels, kernel_plan(): pl.pallas_call(functools.partial(conv_kernel, outer=outer, width=width),...  12.8 us
    ppermute x2, waiting for transfers between devices, passed_along(): return lax.ppermute(block, axis, route)  7.94 us
    ppermute x6, starting transfers between devices, paired(): lax.ppermute(block, 'ctx', [(i, i ^ distance) for i in range(lax.axis_siz...  6.91 us
    ppermute x2, starting transfers between devices, passed_along(): return lax.ppermute(block, axis, route)  5.89 us
  transfers between devices with their start and end apart: 11, of which 6 were waited for; matrix products, arithmetic and copies ran while one was open for 1% of the time, Pallas kernels for 23%

profile of v1, /device:TPU:1, one launch (start us, length us, event | category | flops | bytes accessed | tf_op | source)
XLA Modules:
  0.0 163.9 jit_solution(13477034113139503310)
XLA Ops:
  0.6 0.0 copy-start.8
  0.6 1.2 copy-done.8
  1.9 1.2 copy-done.13
  3.1 1.7 %gate.1.gated_ref = bf16[16,128,256]{2,1,0:T(8,128)(2,1)} custom-call(bf16[128,4096]{1,0:T(8,128)(2,1)S(1)} %copy-done.8, bf16[128,4096]{1,0:T(8,128)(2,1)S(1)} %copy-done.13), custom_call_target="tpu_custom_call" | custom-call | flops 524288 | bytes 3145728 | tf_op jit(solution)/shard_map/gate/pallas_call | solution.py:535
  4.8 7.3 %all-to-all-start = ((bf16[16,128,256]{2,1,0:T(8,128)(2,1)}), bf16[16,128,256]{2,1,0:T(8,128)(2,1)S(1)}, u32[]{:S(2)}, u32[]{:S(2)}) async-start(bf16[16,128,256]{2,1,0:T(8,128)(2,1)} %gate.1.gated_ref), calls=%async_computation | async-start | bytes 2097152 | tf_op jit(solution)/shard_map/all_to_all | solution.py:475
  12.2 0.9 slice.6
  13.1 0.0 copy-start
  13.1 3.7 %collective-permute-start = (bf16[16,4096]{1,0:T(8,128)(2,1)S(1)}, bf16[16,4096]{1,0:T(8,128)(2,1)S(1)}, u32[]{:S(2)}, u32[]{:S(2)}) collective-permute-start(bf16[16,4096]{1,0:T(8,128)(2,1)S(1)} %slice.6), channel_id=1, source_target_pairs={{0,1},{1,2},{2,3},{3,4},{4,5},{5,6},{6,7},{7,8},{8,9},{9,10},{10,1... | collective-permute-start | bytes 393224 | tf_op jit(solution)/shard_map/ppermute | solution.py:18
  16.8 4.5 %collective-permute-done.edge_ref = bf16[16,4096]{1,0:T(8,128)(2,1)S(1)} collective-permute-done((bf16[16,4096]{1,0:T(8,128)(2,1)S(1)}, bf16[16,4096]{1,0:T(8,128)(2,1)S(1)}, u32[]{:S(2)}, u32[]{:S(2)}) %collective-permute-start) | collective-permute-done | bytes 131104 | tf_op jit(solution)/shard_map/ppermute | solution.py:18
  21.3 0.0 copy-done.16
  21.3 1.2 copy-done.6
  22.5 1.2 copy-done.9
  23.7 1.2 copy-done.11
  25.0 1.2 copy-done.14
  26.2 2.5 %mix.1 = (bf16[16,128,128]{2,1,0:T(8,128)(2,1)S(1)}, bf16[16,128,128]{2,1,0:T(8,128)(2,1)}, bf16[128,4096]{1,0:T(8,128)(2,1)}) custom-call(bf16[128,4096]{1,0:T(8,128)(2,1)S(1)} %copy-done.11, bf16[128,4096]{1,0:T(8,128)(2,1)S(1)} %copy-done.6, bf16[16,4096]{1,0:T(8,128)(2,1)S(1)} %collective-permute-done.edge_ref, f32[3,4096]{1,0:T(4,128)S(1)} %copy-done.16, ...), custom_call_target="tpu_custom_call" | custom-call | flops 5242880 | bytes 6291456 | tf_op jit(solution)/shard_map/mix/pallas_call | solution.py:549
  28.7 0.8 copy-done.17
  29.4 5.8 %all-to-all-done = bf16[16,128,256]{2,1,0:T(8,128)(2,1)S(1)} async-done(((bf16[16,128,256]{2,1,0:T(8,128)(2,1)}), bf16[16,128,256]{2,1,0:T(8,128)(2,1)S(1)}, u32[]{:S(2)}, u32[]{:S(2)}) %all-to-all-start) | async-done | bytes 1048608 | tf_op jit(solution)/shard_map/all_to_all | solution.py:475
  35.3 15.8 %all-to-all-start.1 = ((bf16[16,128,128]{2,1,0:T(8,128)(2,1)}), bf16[16,128,128]{2,1,0:T(8,128)(2,1)}, u32[]{:S(2)}, u32[]{:S(2)}) async-start(bf16[16,128,128]{2,1,0:T(8,128)(2,1)} %copy-done.17), calls=%async_computation.1 | async-start | bytes 1048576 | tf_op jit(solution)/shard_map/all_to_all | solution.py:475
  51.1 0.0 copy-done
  51.1 0.0 copy-start.15
  51.1 1.2 copy-done.15
  52.3 4.9 %filter_spectrum.1.filter_ref = bf16[17,256,256]{2,1,0:T(8,128)(2,1)S(1)} custom-call(bf16[256,2048]{1,0:T(8,128)(2,1)S(1)} %copy-done.15, bf16[17,256,256]{2,1,0:T(8,128)(2,1)S(1)} %copy-done), custom_call_target="tpu_custom_call" | custom-call | flops 570425344 | bytes 5505024 | tf_op jit(solution)/shard_map/filter_spectrum/pallas_call | solution.py:566
  57.2 0.0 copy-start.5
  57.2 1.4 copy-done.5
  58.6 12.8 %conv_back.1 = (bf16[2048,256]{1,0:T(8,128)(2,1)S(1)}, bf16[17,256,256]{2,1,0:T(8,128)(2,1)S(1)}) custom-call(bf16[2048,256]{1,0:T(8,128)(2,1)S(1)} %bitcast.27, bf16[17,256,256]{2,1,0:T(8,128)(2,1)} %copy-done.5, bf16[17,256,256]{2,1,0:T(8,128)(2,1)} %constant.57.clone.ahead_ref, bf16[17,256,256]{2,1,0:T(8,128)(2,1)} %constant.58.clone.back_ref), custom_call_target="tpu_custom_call" | custom-call | flops 1140850688 | bytes 11010048 | tf_op jit(solution)/shard_map/conv_back/pallas_call | solution.py:578
  71.5 0.0 copy-start.2
  71.5 1.4 copy-done.2
  72.8 0.0 all-to-all-done.1
  72.8 31.2 %all_to_all.33.back_ref = bf16[16,128,256]{2,1,0:T(8,128)(2,1)} all-to-all(bf16[16,128,256]{2,1,0:T(8,128)(2,1)S(1)} %bitcast.30), channel_id=1, replica_groups=mesh['groups'=2,'ctx'=16] {'ctx'}, dimensions={0} | all-to-all | bytes 2097152 | tf_op jit(solution)/shard_map/all_to_all | solution.py:475
  104.1 4.6 %all-to-all-start.3 = ((bf16[16,128,128]{2,1,0:T(8,128)(2,1)}), bf16[16,128,128]{2,1,0:T(8,128)(2,1)}, u32[]{:S(2)}, u32[]{:S(2)}) async-start(bf16[16,128,128]{2,1,0:T(8,128)(2,1)} %get-tuple-element.33), calls=%async_computation.3 | async-start | bytes 1048576 | tf_op jit(solution)/shard_map/all_to_all | solution.py:475
  108.7 0.0 copy-done.21
  108.7 0.0 copy-start.7
  108.7 1.2 copy-done.7
  110.0 1.2 copy-done.10
  111.2 1.2 copy-done.12
  112.4 4.9 %finish.1 = (bf16[128,4096]{1,0:T(8,128)(2,1)}, bf16[128,4096]{1,0:T(8,128)(2,1)}, bf16[16,4096]{1,0:T(8,128)(2,1)S(1)}, bf16[16,4096]{1,0:T(8,128)(2,1)S(1)}, f32[16,8,256]{2,1,0:T(8,128)S(1)}) custom-call(bf16[16,128,256]{2,1,0:T(8,128)(2,1)S(1)} %copy-done.10, bf16[16,128,256]{2,1,0:T(8,128)(2,1)} %gate.1.gated_ref, bf16[128,4096]{1,0:T(8,128)(2,1)S(1)} %copy-done.12, ...), custom_call_target="tpu_custom_call" | custom-call | flops 15728640 | bytes 6291456 | tf_op jit(solution)/shard_map/finish/pallas_call | solution.py:590
  117.3 0.7 copy-done.18
  118.0 0.7 copy-done.20
  118.6 0.0 copy-done.22
  118.7 1.4 collective-permute-start.2
  120.1 2.1 %collective-permute-start.4 = (f32[4,8,256]{2,1,0:T(8,128)S(1)}, f32[4,8,256]{2,1,0:T(8,128)S(1)}, u32[]{:S(2)}, u32[]{:S(2)}) collective-permute-start(f32[4,8,256]{2,1,0:T(8,128)S(1)} %get-tuple-element.41), channel_id=1, source_target_pairs={{0,12},{1,13},{2,14},{3,15},{4,8},{5,9},{6,10},{7,11},{8,4},{9,5},... | collective-permute-start | bytes 98312 | tf_op jit(solution)/shard_map/ppermute | solution.py:479
  122.2 0.0 collective-permute-start.3
  122.2 0.7 collective-permute-done.2
  122.9 1.8 %collective-permute-done.4 = f32[4,8,256]{2,1,0:T(8,128)S(1)} collective-permute-done((f32[4,8,256]{2,1,0:T(8,128)S(1)}, f32[4,8,256]{2,1,0:T(8,128)S(1)}, u32[]{:S(2)}, u32[]{:S(2)}) %collective-permute-start.4) | collective-permute-done | bytes 32800 | tf_op jit(solution)/shard_map/ppermute | solution.py:479
  124.7 1.8 %collective-permute-done.3 = f32[4,8,256]{2,1,0:T(8,128)S(1)} collective-permute-done((f32[4,8,256]{2,1,0:T(8,128)S(1)}, f32[4,8,256]{2,1,0:T(8,128)S(1)}, u32[]{:S(2)}, u32[]{:S(2)}) %collective-permute-start.3) | collective-permute-done | bytes 32800 | tf_op jit(solution)/shard_map/ppermute | solution.py:479
  126.5 0.8 fusion.1
  127.3 2.9 %collective-permute-start.7 = (f32[8,256]{1,0:T(8,128)S(1)}, f32[8,256]{1,0:T(8,128)S(1)}, u32[]{:S(2)}, u32[]{:S(2)}) collective-permute-start(f32[8,256]{1,0:T(8,128)S(1)} %get-tuple-element.44), channel_id=1, source_target_pairs={{0,3},{1,2},{2,1},{3,0},{4,7},{5,6},{6,5},{7,4},{8,11},{9,10},{10,... | collective-permute-start | bytes 24584 | tf_op jit(solution)/shard_map/ppermute | solution.py:479
  130.2 0.3 collective-permute-start.6
  130.5 0.2 collective-permute-start.5
  130.7 0.0 copy-done.1
  130.7 1.6 copy-done.3
  132.3 11.2 %filter_grad_0.1 = (bf16[256,2048]{1,0:T(8,128)(2,1)}, f32[1,128]{1,0:T(1,128)S(1)}) custom-call(bf16[2048,128]{1,0:T(8,128)(2,1)} %bitcast.1.mixed_ref, bf16[2048,256]{1,0:T(8,128)(2,1)S(1)} %bitcast.28, bf16[17,256,256]{2,1,0:T(8,128)(2,1)S(1)} %copy-done.3, bf16[17,256,256]{2,1,0:T(8,128)(2,1)S(1)} %copy-done.1, bf16[17,256,256]{2,1,0:T(8,128)(2,1)} %constant.58.clone.back_ref), custom_call_target="tpu_custom_call" | custom-call | flops 570425344 | bytes 6684672 | tf_op jit(solution)/shard_map/filter_grad_0/pallas_call | solution.py:639
  143.5 0.0 copy-done.23
  143.5 2.2 %collective-permute-start.1 = (bf16[16,4096]{1,0:T(8,128)(2,1)S(1)}, bf16[16,4096]{1,0:T(8,128)(2,1)S(1)}, u32[]{:S(2)}, u32[]{:S(2)}) collective-permute-start(bf16[16,4096]{1,0:T(8,128)(2,1)S(1)} %copy-done.23), channel_id=1, source_target_pairs={{1,0},{2,1},{3,2},{4,3},{5,4},{6,5},{7,6},{8,7},{9,8},{10,9},{11,1... | collective-permute-start | bytes 393224 | tf_op jit(solution)/shard_map/ppermute | solution.py:18
  145.7 0.0 collective-permute-done.7
  145.7 0.0 collective-permute-done.6
  145.7 0.0 collective-permute-done.5
  145.7 0.6 slice_add_fusion
  146.3 3.4 %collective-permute-done.1.head_ref = bf16[16,4096]{1,0:T(8,128)(2,1)S(1)} collective-permute-done((bf16[16,4096]{1,0:T(8,128)(2,1)S(1)}, bf16[16,4096]{1,0:T(8,128)(2,1)S(1)}, u32[]{:S(2)}, u32[]{:S(2)}) %collective-permute-start.1) | collective-permute-done | bytes 131104 | tf_op jit(solution)/shard_map/ppermute | solution.py:18
  149.8 0.8 seam.1
  150.6 0.0 all-to-all-done.3
  150.6 1.6 copy-done.4
  152.2 11.2 %filter_grad_1.1 = (bf16[256,2048]{1,0:T(8,128)(2,1)}, f32[1,128]{1,0:T(1,128)S(1)}) custom-call(bf16[2048,128]{1,0:T(8,128)(2,1)} %bitcast.4.mixed_ref, bf16[2048,256]{1,0:T(8,128)(2,1)S(1)} %bitcast.29, bf16[17,256,256]{2,1,0:T(8,128)(2,1)S(1)} %copy-done.4, bf16[17,256,256]{2,1,0:T(8,128)(2,1)S(1)} %copy-done.1, ...), custom_call_target="tpu_custom_call", output_to_operand_aliasing={{0}: (5, {})} | custom-call | flops 570425344 | bytes 6684672 | tf_op jit(solution)/shard_map/filter_grad_1/pallas_call | solution.py:639
  163.4 0.6 pad_maximum_fusion
  (21 shorter events, 0.1 us)
Async XLA Ops:
  0.6 1.2 copy-start.8
  1.9 1.2 copy-start.13
  3.1 18.2 %copy-start.16 = (f32[3,4096]{1,0:T(4,128)S(1)}, f32[3,4096]{1,0:T(4,128)}, u32[]{:S(2)}) copy-start(f32[3,4096]{1,0:T(4,128)} %short_ref.5) | copy-start | bytes 147460
  4.8 30.5 %all-to-all-start = ((bf16[16,128,256]{2,1,0:T(8,128)(2,1)}), bf16[16,128,256]{2,1,0:T(8,128)(2,1)S(1)}, u32[]{:S(2)}, u32[]{:S(2)}) async-start(bf16[16,128,256]{2,1,0:T(8,128)(2,1)} %gate.1.gated_ref), calls=%async_computation | async-start | bytes 2097152 | tf_op jit(solution)/shard_map/all_to_all | solution.py:475
  13.1 38.0 %copy-start = (bf16[17,256,256]{2,1,0:T(8,128)(2,1)S(1)}, bf16[17,256,256]{2,1,0:T(8,128)(2,1)}, u32[]{:S(2)}) copy-start(bf16[17,256,256]{2,1,0:T(8,128)(2,1)} %constant.57.clone.ahead_ref) | copy-start | bytes 6684676
  13.1 8.2 %collective-permute-start = (bf16[16,4096]{1,0:T(8,128)(2,1)S(1)}, bf16[16,4096]{1,0:T(8,128)(2,1)S(1)}, u32[]{:S(2)}, u32[]{:S(2)}) collective-permute-start(bf16[16,4096]{1,0:T(8,128)(2,1)S(1)} %slice.6), channel_id=1, source_target_pairs={{0,1},{1,2},{2,3},{3,4},{4,5},{5,6},{6,7},{7,8},{8,9},{9,10},{10,1... | collective-permute-start | bytes 393224 | tf_op jit(solution)/shard_map/ppermute | solution.py:18
  21.3 1.2 copy-start.6
  22.5 1.2 copy-start.9
  23.7 1.2 copy-start.11
  25.0 1.2 copy-start.14
  28.6 0.8 copy-start.17
  35.3 37.5 %all-to-all-start.1 = ((bf16[16,128,128]{2,1,0:T(8,128)(2,1)}), bf16[16,128,128]{2,1,0:T(8,128)(2,1)}, u32[]{:S(2)}, u32[]{:S(2)}) async-start(bf16[16,128,128]{2,1,0:T(8,128)(2,1)} %copy-done.17), calls=%async_computation.1 | async-start | bytes 1048576 | tf_op jit(solution)/shard_map/all_to_all | solution.py:475
  51.1 1.2 copy-start.15
  57.2 1.4 copy-start.5
  71.5 1.4 copy-start.2
  72.8 35.9 %copy-start.21 = (f32[4096]{0:T(1024)S(1)}, f32[4096]{0:T(1024)}, u32[]{:S(2)}) copy-start(f32[4096]{0:T(1024)} %param.17) | copy-start | bytes 49156
  104.1 46.5 %all-to-all-start.3 = ((bf16[16,128,128]{2,1,0:T(8,128)(2,1)}), bf16[16,128,128]{2,1,0:T(8,128)(2,1)}, u32[]{:S(2)}, u32[]{:S(2)}) async-start(bf16[16,128,128]{2,1,0:T(8,128)(2,1)} %get-tuple-element.33), calls=%async_computation.3 | async-start | bytes 1048576 | tf_op jit(solution)/shard_map/all_to_all | solution.py:475
  108.7 1.2 copy-start.7
  110.0 1.2 copy-start.10
  111.2 1.2 copy-start.12
  112.4 18.3 %copy-start.1 = (bf16[17,256,256]{2,1,0:T(8,128)(2,1)S(1)}, bf16[17,256,256]{2,1,0:T(8,128)(2,1)}, u32[]{:S(2)}) copy-start(bf16[17,256,256]{2,1,0:T(8,128)(2,1)} %constant.57.clone.ahead_ref) | copy-start | bytes 6684676
  117.3 0.7 copy-start.18
  118.0 0.7 copy-start.20
  118.0 0.7 copy-start.22
  118.7 4.2 %collective-permute-start.2 = (f32[4,8,256]{2,1,0:T(8,128)S(1)}, f32[4,8,256]{2,1,0:T(8,128)S(1)}, u32[]{:S(2)}, u32[]{:S(2)}) collective-permute-start(f32[4,8,256]{2,1,0:T(8,128)S(1)} %get-tuple-element.40), channel_id=1, source_target_pairs={{0,4},{1,5},{2,6},{3,7},{4,0},{5,1},{6,2},{7,3},{8,12},{9,13},{10,... | collective-permute-start | bytes 98312 | tf_op jit(solution)/shard_map/ppermute | solution.py:479
  120.1 4.6 %collective-permute-start.4 = (f32[4,8,256]{2,1,0:T(8,128)S(1)}, f32[4,8,256]{2,1,0:T(8,128)S(1)}, u32[]{:S(2)}, u32[]{:S(2)}) collective-permute-start(f32[4,8,256]{2,1,0:T(8,128)S(1)} %get-tuple-element.41), channel_id=1, source_target_pairs={{0,12},{1,13},{2,14},{3,15},{4,8},{5,9},{6,10},{7,11},{8,4},{9,5},... | collective-permute-start | bytes 98312 | tf_op jit(solution)/shard_map/ppermute | solution.py:479
  122.2 4.3 %collective-permute-start.3 = (f32[4,8,256]{2,1,0:T(8,128)S(1)}, f32[4,8,256]{2,1,0:T(8,128)S(1)}, u32[]{:S(2)}, u32[]{:S(2)}) collective-permute-start(f32[4,8,256]{2,1,0:T(8,128)S(1)} %get-tuple-element.42), channel_id=1, source_target_pairs={{0,8},{1,9},{2,10},{3,11},{4,12},{5,13},{6,14},{7,15},{8,0},{9,1},... | collective-permute-start | bytes 98312 | tf_op jit(solution)/shard_map/ppermute | solution.py:479
  127.3 18.5 %collective-permute-start.7 = (f32[8,256]{1,0:T(8,128)S(1)}, f32[8,256]{1,0:T(8,128)S(1)}, u32[]{:S(2)}, u32[]{:S(2)}) collective-permute-start(f32[8,256]{1,0:T(8,128)S(1)} %get-tuple-element.44), channel_id=1, source_target_pairs={{0,3},{1,2},{2,1},{3,0},{4,7},{5,6},{6,5},{7,4},{8,11},{9,10},{10,... | collective-permute-start | bytes 24584 | tf_op jit(solution)/shard_map/ppermute | solution.py:479
  130.2 15.5 %collective-permute-start.6 = (f32[8,256]{1,0:T(8,128)S(1)}, f32[8,256]{1,0:T(8,128)S(1)}, u32[]{:S(2)}, u32[]{:S(2)}) collective-permute-start(f32[8,256]{1,0:T(8,128)S(1)} %get-tuple-element.45), channel_id=1, source_target_pairs={{0,2},{1,3},{2,0},{3,1},{4,6},{5,7},{6,4},{7,5},{8,10},{9,11},{10,... | collective-permute-start | bytes 24584 | tf_op jit(solution)/shard_map/ppermute | solution.py:479
  130.5 15.3 %collective-permute-start.5 = (f32[8,256]{1,0:T(8,128)S(1)}, f32[8,256]{1,0:T(8,128)S(1)}, u32[]{:S(2)}, u32[]{:S(2)}) collective-permute-start(f32[8,256]{1,0:T(8,128)S(1)} %get-tuple-element.46), channel_id=1, source_target_pairs={{0,1},{1,0},{2,3},{3,2},{4,5},{5,4},{6,7},{7,6},{8,9},{9,8},{10,11... | collective-permute-start | bytes 24584 | tf_op jit(solution)/shard_map/ppermute | solution.py:479
  130.7 1.6 copy-start.3
  132.3 11.2 %copy-start.23 = (bf16[16,4096]{1,0:T(8,128)(2,1)S(1)}, bf16[16,4096]{1,0:T(8,128)(2,1)}, u32[]{:S(2)}) copy-start(bf16[16,4096]{1,0:T(8,128)(2,1)} %copy-done.22) | copy-start | bytes 393220
  132.3 17.5 %copy-start.19 = (bf16[16,4096]{1,0:T(8,128)(2,1)S(1)}, bf16[16,4096]{1,0:T(8,128)(2,1)}, u32[]{:S(2)}) copy-start(bf16[16,4096]{1,0:T(8,128)(2,1)} %copy-done.18) | copy-start | bytes 393220
  143.5 6.3 %collective-permute-start.1 = (bf16[16,4096]{1,0:T(8,128)(2,1)S(1)}, bf16[16,4096]{1,0:T(8,128)(2,1)S(1)}, u32[]{:S(2)}, u32[]{:S(2)}) collective-permute-start(bf16[16,4096]{1,0:T(8,128)(2,1)S(1)} %copy-done.23), channel_id=1, source_target_pairs={{1,0},{2,1},{3,2},{4,3},{5,4},{6,5},{7,6},{8,7},{9,8},{10,9},{11,1... | collective-permute-start | bytes 393224 | tf_op jit(solution)/shard_map/ppermute | solution.py:18
  150.6 1.6 copy-start.4

commit v2 on v1

--- a/solution.py
+++ b/solution.py
@@ -190,6 +190,7 @@
 
 
 INNER = 128
+INNER_PEERS = 4
 
 
 def half_spectrum(values, length):
@@ -318,68 +319,88 @@
         z_ref, outer, width,
     )
 
-    def one_bin(k, carry):
+    for k in range(outer // 2 + 1):
         spec_ref[k] = dot32(ahead_ref[k], z_ref[k]).astype(jnp.bfloat16)
-        return carry
-
-    lax.fori_loop(0, outer // 2 + 1, one_bin, 0)
-
-
-def conv_kernel(gated_ref, filter_ref, ahead_ref, back_ref, conv_ref, spec_ref, z_ref, u_ref, *, outer, width):
+
+
+def begun(source, target, semaphore):
+    copy = pltpu.make_async_copy(source, target, semaphore)
+    copy.start()
+    return copy
+
+
+def conv_kernel(
+    gated_hbm, filter_hbm, ahead_hbm, back_hbm, conv_ref, spec_hbm,
+    gated_ref, filter_ref, ahead_ref, back_ref, spec_ref, z_ref, u_ref, sems, *, outer, width,
+):
+    gated_in = begun(gated_hbm, gated_ref, sems.at[0])
+    ahead_in = begun(ahead_hbm, ahead_ref, sems.at[1])
+    filter_in = begun(filter_hbm, filter_ref, sems.at[2])
+    back_in = begun(back_hbm, back_ref, sems.at[3])
+    gated_in.wait()
     outer_ahead(
         lambda a, row, lane: gated_ref[pl.ds(a * INNER + row, 16), lane : lane + 128],
         z_ref, outer, width,
     )
-
-    def one_bin(k, carry):
+    ahead_in.wait()
+    filter_in.wait()
+    for k in range(outer // 2 + 1):
         gated = dot32(ahead_ref[k], z_ref[k])
         spec_ref[k] = gated.astype(jnp.bfloat16)
-        product = correlate_bin(filter_ref[k].astype(jnp.float32), gated)
-        u_ref[k] = dot32(back_ref[k], product)
-        return carry
-
-    lax.fori_loop(0, outer // 2 + 1, one_bin, 0)
+        z_ref[k] = correlate_bin(filter_ref[k].astype(jnp.float32), gated)
+    spec_out = begun(spec_ref, spec_hbm, sems.at[4])
+    back_in.wait()
+    for k in range(outer // 2 + 1):
+        u_ref[k] = dot32(back_ref[k], z_ref[k])
 
     def store(a, row, lane, value):
         conv_ref[pl.ds(a * INNER + row, 16), lane : lane + 128] = value.astype(jnp.bfloat16)
 
     outer_back(u_ref, store, outer, width)
-
-
-def grad_kernel(mixed_ref, gated_ref, spec_ref, ahead_ref, back_ref, grad_ref, skip_ref, z_ref, u_ref, rows_ref, *, outer, width):
+    spec_out.wait()
+
+
+def grad_kernel(
+    mixed_hbm, gated_hbm, spec_hbm, ahead_hbm, back_hbm, grad_ref, skip_ref,
+    mixed_ref, gated_ref, spec_ref, ahead_ref, back_ref, z_ref, u_ref, rows_ref, sems, *, outer, width,
+):
+    slabs = outer // 2
+    mixed_in = begun(mixed_hbm, mixed_ref, sems.at[0])
+    ahead_in = begun(ahead_hbm, ahead_ref, sems.at[1])
+    spec_in = begun(spec_hbm, spec_ref, sems.at[2])
+    back_in = begun(back_hbm, back_ref, sems.at[3])
+    gated_in = begun(gated_hbm, gated_ref, sems.at[4])
+    mixed_in.wait()
     outer_ahead(
         lambda a, row, lane: mixed_ref[pl.ds(a * INNER + row, 16), lane : lane + 128],
         z_ref, outer, width,
     )
-
-    def one_bin(k, carry):
+    ahead_in.wait()
+    spec_in.wait()
+    for k in range(outer // 2 + 1):
         mixed = dot32(ahead_ref[k], z_ref[k])
-        product = correlate_bin(mixed, spec_ref[k].astype(jnp.float32))
-        u_ref[k] = dot32(back_ref[k], product)
-        return carry
-
-    lax.fori_loop(0, outer // 2 + 1, one_bin, 0)
+        z_ref[k] = correlate_bin(mixed, spec_ref[k].astype(jnp.float32))
+    back_in.wait()
+    for k in range(outer // 2 + 1):
+        u_ref[k] = dot32(back_ref[k], z_ref[k])
 
     def store(a, row, lane, value):
         rows_ref[pl.ds(a * INNER + row, 16), lane : lane + 128] = value
 
     outer_back(u_ref, store, outer, width)
-    for a in range(outer // 2):
+    for a in range(slabs):
         grad_ref[:, a * INNER : (a + 1) * INNER] = rows_ref[
             a * INNER : (a + 1) * INNER, :
         ].T.astype(jnp.bfloat16)
+    gated_in.wait()
 
     def add(a, total):
         place = pl.ds(pl.multiple_of(a * INNER, INNER), INNER)
         part = gated_ref[place, :].astype(jnp.float32) * mixed_ref[place, :].astype(jnp.float32)
         return total + jnp.sum(part.reshape(INNER // 8, 8, width), axis=0)
 
-    total = lax.fori_loop(0, outer // 2, add, jnp.zeros((8, width), jnp.float32))
+    total = lax.fori_loop(0, slabs, add, jnp.zeros((8, width), jnp.float32))
     skip_ref[...] = jnp.sum(total, axis=0, keepdims=True)
-
-
-def later_grad_kernel(mixed_ref, gated_ref, spec_ref, ahead_ref, back_ref, done_ref, *rest, outer, width):
-    grad_kernel(mixed_ref, gated_ref, spec_ref, ahead_ref, back_ref, *rest, outer=outer, width=width)
 
 
 def shifted_down(values, distance, edge):
@@ -408,47 +429,93 @@
         ).astype(jnp.bfloat16)
 
 
-def mix_kernel(key_ref, value_ref, edge_ref, short_ref, grad_ref, conv_ref, *rest, width, parts):
-    mixed_refs, query_grad_ref = rest[:parts], rest[parts]
-    piece = width // parts
-    for j in range(mixed_refs[0].shape[0]):
-        for part in range(parts):
-            cols = slice(j * width + part * piece, j * width + (part + 1) * piece)
-            value = value_ref[:, cols].astype(jnp.float32)
-            edge = edge_ref[:, cols].astype(jnp.float32)
-            conv = (
-                short_ref[0:1, cols] * value
-                + short_ref[1:2, cols] * shifted_down(value, 1, edge)
-                + short_ref[2:3, cols] * shifted_down(value, 2, edge)
+def mixed_values(key_ref, value_ref, short_ref, cols, edge):
+    value = value_ref[:, cols].astype(jnp.float32)
+    conv = (
+        short_ref[0:1, cols] * value
+        + short_ref[1:2, cols] * shifted_down(value, 1, edge)
+        + short_ref[2:3, cols] * shifted_down(value, 2, edge)
+    )
+    return (key_ref[:, cols].astype(jnp.float32) * conv).astype(jnp.bfloat16)
+
+
+def mix_kernel(key_ref, value_ref, short_ref, grad_ref, conv_ref, mixed_ref, query_grad_ref, *, width):
+    zero = jnp.zeros((2, 128), jnp.float32)
+    for j in range(mixed_ref.shape[0]):
+        for lane in range(0, width, 128):
+            cols = slice(j * width + lane, j * width + lane + 128)
+            mixed_ref[j, :, lane : lane + 128] = mixed_values(
+                key_ref, value_ref, short_ref, cols, zero
             )
-            mixed_refs[part][j] = (key_ref[:, cols].astype(jnp.float32) * conv).astype(jnp.bfloat16)
             query_grad_ref[:, cols] = (
                 grad_ref[:, cols].astype(jnp.float32) * conv_ref[:, cols].astype(jnp.float32)
             ).astype(jnp.bfloat16)
 
 
-def finish_kernel(
-    back_ref, gated_ref, key_ref, value_ref, edge_ref, short_ref, skip_ref,
-    key_grad_ref, value_grad_ref, head_ref, tail_ref, part_ref, *, width,
+def mix_top_kernel(key_ref, value_ref, short_ref, edge_ref, mixed_in, mixed_ref, *, width):
+    for j in range(mixed_ref.shape[0]):
+        for lane in range(0, width, 128):
+            cols = slice(j * width + lane, j * width + lane + 128)
+            edge = edge_ref[:, cols].astype(jnp.float32)
+            mixed_ref[j, :, lane : lane + 128] = mixed_values(
+                key_ref, value_ref, short_ref, cols, edge
+            )
+
+
+def sums_kernel(
+    back_ref, gated_ref, key_ref, value_ref, edge_ref, skip_ref, head_ref, tail_ref, *part_refs, width
 ):
     rows = key_ref.shape[0]
+    first = pl.program_id(0) * (back_ref.shape[0] // INNER_PEERS)
+    own = lax.axis_index("ctx") // INNER_PEERS
+    for j in range(back_ref.shape[0]):
+        distance = (first + j // INNER_PEERS) ^ own
+        for lane in range(0, width, 128):
+            cols = slice(j * width + lane, j * width + lane + 128)
+            lanes = slice(lane, lane + 128)
+            value = value_ref[:, cols].astype(jnp.float32)
+            edge = edge_ref[:, cols].astype(jnp.float32)
+            mixed_grad = back_ref[j, :, lanes].astype(jnp.float32) + skip_ref[:, cols] * gated_ref[
+                j, :, lanes
+            ].astype(jnp.float32)
+            feature = (mixed_grad * key_ref[:, cols].astype(jnp.float32)).astype(jnp.bfloat16)
+            head_ref[:, cols] = feature[:2]
+            tail_ref[:, cols] = feature[rows - 16 :]
+            feature = feature.astype(jnp.float32)
+            shifted = (value, shifted_down(value, 1, edge), shifted_down(value, 2, edge))
+            sums = jnp.concatenate(
+                [jnp.sum(feature * other, axis=0, keepdims=True) for other in shifted]
+                + [jnp.zeros((5, 128), jnp.float32)],
+                0,
+            )
+            for d, part_ref in enumerate(part_refs):
+
+                @pl.when(distance == d)
+                def _(part_ref=part_ref, sums=sums):
+                    part_ref[j % INNER_PEERS, :, lanes] = sums
+
+
+def finish_kernel(
+    back_ref, gated_ref, key_ref, value_ref, edge_ref, short_ref, skip_ref, key_grad_ref,
+    value_grad_ref, *, width,
+):
     for j in range(back_ref.shape[0]):
         for lane in range(0, width, 128):
             cols = slice(j * width + lane, j * width + lane + 128)
             lanes = slice(lane, lane + 128)
             value = value_ref[:, cols].astype(jnp.float32)
             edge = edge_ref[:, cols].astype(jnp.float32)
-            value_1 = shifted_down(value, 1, edge)
-            value_2 = shifted_down(value, 2, edge)
             short = [short_ref[i : i + 1, cols] for i in range(3)]
-            conv = short[0] * value + short[1] * value_1 + short[2] * value_2
+            conv = (
+                short[0] * value
+                + short[1] * shifted_down(value, 1, edge)
+                + short[2] * shifted_down(value, 2, edge)
+            )
             mixed_grad = back_ref[j, :, lanes].astype(jnp.float32) + skip_ref[:, cols] * gated_ref[
                 j, :, lanes
             ].astype(jnp.float32)
             key_grad_ref[:, cols] = (mixed_grad * conv).astype(jnp.bfloat16)
             feature = (mixed_grad * key_ref[:, cols].astype(jnp.float32)).astype(jnp.bfloat16)
-            head_ref[:, cols] = feature[:16]
-            tail_ref[:, cols] = feature[rows - 16 :]
             feature = feature.astype(jnp.float32)
             zero = jnp.zeros((2, 128), jnp.float32)
             value_grad_ref[:, cols] = (
@@ -456,9 +523,6 @@
                 + short[1] * shifted_up(feature, 1, zero)
                 + short[2] * shifted_up(feature, 2, zero)
             ).astype(jnp.bfloat16)
-            for i, other in enumerate((value, value_1, value_2)):
-                part_ref[j, i : i + 1, lanes] = jnp.sum(feature * other, axis=0, keepdims=True)
-            part_ref[j, 3:8, lanes] = jnp.zeros((5, 128), jnp.float32)
 
 
 def seam_kernel(tail_ref, head_ref, short_ref, done_ref, value_grad_ref):
@@ -479,26 +543,24 @@
     return lax.ppermute(block, "ctx", [(i, i ^ distance) for i in range(lax.axis_size("ctx"))])
 
 
-def summed_at_owner(parts):
-    peers = lax.axis_size("ctx")
-    me = lax.axis_index("ctx")
-    inner = 4 if peers % 4 == 0 else 1
-    for count, place, step in ((peers // inner, me // inner, inner), (inner, me % inner, 1)):
-        if step == inner:
-            parts = parts.reshape((count, inner) + parts.shape[1:])
-        mine = lax.dynamic_index_in_dim(parts, place, 0, keepdims=False)
-        for distance in range(1, count):
-            other = lax.dynamic_index_in_dim(parts, place ^ distance, 0, keepdims=False)
-            mine = mine + paired(other, distance * step)
-        parts = mine
-    return parts
+def summed_at_owner(parts, *beside):
+    place = lax.axis_index("ctx") % INNER_PEERS
+    rows = parts[0]
+    for distance in range(1, len(parts)):
+        rows = rows + paired(parts[distance], distance * INNER_PEERS)
+    rows, *beside = lax.optimization_barrier((rows, *beside))
+    total = lax.dynamic_index_in_dim(rows, place, 0, keepdims=False)
+    for distance in range(1, INNER_PEERS):
+        other = lax.dynamic_index_in_dim(rows, place ^ distance, 0, keepdims=False)
+        total = total + paired(other, distance)
+    return total, *beside
 
 
 def after(value, *others):
     return lax.optimization_barrier((value,) + others)[0]
 
 
-def params(mib=48):
+def params(mib=63):
     return pltpu.CompilerParams(vmem_limit_bytes=mib * 1024 * 1024)
 
 
@@ -515,11 +577,11 @@
     seq = rows * peers
     outer = 2 * seq // INNER
     bins = outer // 2 + 1
-    steps = 4
+    steps = 2
     group = peers // steps
     span = group * width
-    parts = 2
-    piece = width // parts
+    far = peers // INNER_PEERS
+    hbm = pl.BlockSpec(memory_space=pl.ANY)
     bf16, f32 = jnp.bfloat16, jnp.float32
     shape = jax.ShapeDtypeStruct
     skip_row = skip_gain.reshape(1, channels)
@@ -527,8 +589,8 @@
 
     flat = pl.BlockSpec((rows, span), lambda i: (0, i))
     owned = pl.BlockSpec((group, rows, width), lambda i: (i, 0, 0))
-    owned_part = pl.BlockSpec((group, rows, piece), lambda i: (i, 0, 0))
-    edge_spec = pl.BlockSpec((16, span), lambda i: (0, i))
+    edge_spec = pl.BlockSpec((2, span), lambda i: (0, i))
+    tail_spec = pl.BlockSpec((16, span), lambda i: (0, i))
     short_spec = pl.BlockSpec((3, span), lambda i: (0, i))
     skip_spec = pl.BlockSpec((1, span), lambda i: (0, i))
 
@@ -545,21 +607,10 @@
 
     gated_got = exchanged(gated.reshape(seq, width))
 
-    edge = passed_along(value_raw[rows - 16 :], "ctx", 1)
-    *mixed, query_grad = pl.pallas_call(
-        functools.partial(mix_kernel, width=width, parts=parts),
-        grid=(steps,),
-        in_specs=[flat, flat, edge_spec, short_spec, flat, flat],
-        out_specs=[owned_part] * parts + [flat],
-        out_shape=[shape((peers, rows, piece), bf16)] * parts + [shape((rows, channels), bf16)],
-        compiler_params=params(),
-        cost_estimate=cost(10 * rows * channels, 12 * rows * channels),
-        name="mix",
-    )(key_feat, value_raw, edge, short_filter, out_grad, conv_out)
-
     spec_shape = shape((bins, 2 * INNER, width), bf16)
     z_scratch = pltpu.VMEM((bins, 2 * INNER, width), bf16)
     u_scratch = pltpu.VMEM((bins, 2 * INNER, width), f32)
+    table_scratch = pltpu.VMEM((bins, 2 * INNER, 2 * INNER), bf16)
     table_bytes = 8 * bins * INNER * INNER
     spec_bytes = 4 * bins * INNER * width
     work = 2 * bins * (2 * INNER) ** 2 * width
@@ -572,44 +623,76 @@
         name="filter_spectrum",
     )(filter_taps, ahead)
 
-    mixed_got = [None] * parts
-    mixed_got[0] = exchanged(after(mixed[0], gated_got).reshape(seq, piece))
+    whole = lambda size: pl.BlockSpec((size, channels), lambda i: (0, 0))
+    mixed, query_grad = pl.pallas_call(
+        functools.partial(mix_kernel, width=width),
+        grid=(steps,),
+        in_specs=[flat, flat, short_spec, flat, flat],
+        out_specs=[owned, flat],
+        out_shape=[shape((peers, rows, width), bf16), shape((rows, channels), bf16)],
+        compiler_params=params(),
+        cost_estimate=cost(10 * rows * channels, 12 * rows * channels),
+        name="mix",
+    )(key_feat, value_raw, short_filter, out_grad, conv_out)
+    filter_spec, mixed = lax.optimization_barrier((filter_spec, mixed))
+    edge = passed_along(value_raw[rows - 2 :], "ctx", 1)
 
     conv_back, gated_spec = pl.pallas_call(
         functools.partial(conv_kernel, outer=outer, width=width),
+        in_specs=[hbm] * 4,
+        out_specs=[pl.BlockSpec(memory_space=pltpu.VMEM), hbm],
         out_shape=(shape((seq, width), bf16), spec_shape),
-        scratch_shapes=[z_scratch, u_scratch],
+        scratch_shapes=[pltpu.VMEM((seq, width), bf16), z_scratch, table_scratch, table_scratch, z_scratch]
+        + [z_scratch, u_scratch, pltpu.SemaphoreType.DMA((5,))],
         compiler_params=params(),
         cost_estimate=cost(2 * work, 2 * table_bytes + 2 * spec_bytes + 4 * seq * width),
         name="conv_back",
     )(gated_got, filter_spec, ahead, back)
 
-    back_got = exchanged(after(conv_back, mixed_got[0])).reshape(peers, rows, width)
-    mixed_got[1] = exchanged(after(mixed[1], back_got).reshape(seq, piece))
-
-    key_grad, value_grad, head, tail, short_part = pl.pallas_call(
+    conv_back, edge = lax.optimization_barrier((conv_back, edge))
+    back_got = exchanged(conv_back).reshape(peers, rows, width)
+    mixed = pl.pallas_call(
+        functools.partial(mix_top_kernel, width=width),
+        grid=(1,),
+        in_specs=[whole(16), whole(16), whole(3), whole(2), hbm],
+        out_specs=pl.BlockSpec((peers, 16, width), lambda i: (0, 0, 0)),
+        out_shape=shape((peers, rows, width), bf16),
+        input_output_aliases={4: 0},
+        compiler_params=params(),
+        cost_estimate=cost(10 * 16 * channels, 10 * 16 * channels),
+        name="mix_top",
+    )(key_feat, value_raw, short_filter, edge, mixed)
+    mixed_got = exchanged(after(mixed, back_got).reshape(seq, width))
+
+    head, tail, *short_parts = pl.pallas_call(
+        functools.partial(sums_kernel, width=width),
+        grid=(steps,),
+        in_specs=[owned, owned, flat, flat, edge_spec, skip_spec],
+        out_specs=[edge_spec, tail_spec]
+        + [pl.BlockSpec((INNER_PEERS, 8, width), lambda i: (0, 0, 0))] * far,
+        out_shape=[shape((2, channels), bf16), shape((16, channels), bf16)]
+        + [shape((INNER_PEERS, 8, width), f32)] * far,
+        compiler_params=params(),
+        cost_estimate=cost(20 * rows * channels, 8 * rows * channels),
+        name="sums",
+    )(back_got, gated, key_feat, value_raw, edge, skip_row)
+
+    key_grad, value_grad = pl.pallas_call(
         functools.partial(finish_kernel, width=width),
         grid=(steps,),
         in_specs=[owned, owned, flat, flat, edge_spec, short_spec, skip_spec],
-        out_specs=[flat, flat, edge_spec, edge_spec, pl.BlockSpec((group, 8, width), lambda i: (i, 0, 0))],
-        out_shape=[
-            shape((rows, channels), bf16),
-            shape((rows, channels), bf16),
-            shape((16, channels), bf16),
-            shape((16, channels), bf16),
-            shape((peers, 8, width), f32),
-        ],
+        out_specs=[flat, flat],
+        out_shape=[shape((rows, channels), bf16)] * 2,
         compiler_params=params(),
         cost_estimate=cost(30 * rows * channels, 12 * rows * channels),
         name="finish",
     )(back_got, gated, key_feat, value_raw, edge, short_filter, skip_row)
 
     head_got = passed_along(head, "ctx", -1)
-    whole = lambda size: pl.BlockSpec((size, channels), lambda i: (0, 0))
     value_grad = pl.pallas_call(
         seam_kernel,
         grid=(1,),
-        in_specs=[whole(16), whole(16), whole(3), pl.BlockSpec(memory_space=pl.ANY)],
+        in_specs=[whole(16), whole(2), whole(3), hbm],
         out_specs=pl.BlockSpec((16, channels), lambda i: (rows // 16 - 1, 0)),
         out_shape=shape((rows, channels), bf16),
         input_output_aliases={3: 0},
@@ -617,47 +700,19 @@
         cost_estimate=cost(5 * 16 * channels, 6 * 16 * channels),
         name="seam",
     )(tail, head_got, short_filter, value_grad)
-    short_grad = summed_at_owner(short_part)[:3]
-
-    filter_grad = None
-    skip_parts = []
-    for part in range(parts):
-        at = part
-        in_specs = [
-            pl.BlockSpec((seq, piece), lambda i: (0, 0)),
-            pl.BlockSpec((seq, piece), lambda i, at=at: (0, at)),
-            pl.BlockSpec((bins, 2 * INNER, piece), lambda i, at=at: (0, 0, at)),
-            pl.BlockSpec((bins, 2 * INNER, 2 * INNER), lambda i: (0, 0, 0)),
-            pl.BlockSpec((bins, 2 * INNER, 2 * INNER), lambda i: (0, 0, 0)),
-        ]
-        operands = [mixed_got[part], gated_got, gated_spec, ahead, back]
-        body = functools.partial(grad_kernel, outer=outer, width=piece)
-        if part:
-            in_specs.append(pl.BlockSpec(memory_space=pl.ANY))
-            operands.append(filter_grad)
-            body = functools.partial(later_grad_kernel, outer=outer, width=piece)
-        filter_grad, skip_part = pl.pallas_call(
-            body,
-            grid=(1,),
-            in_specs=in_specs,
-            out_specs=[
-                pl.BlockSpec((piece, seq), lambda i, at=at: (at, 0)),
-                pl.BlockSpec((1, piece), lambda i: (0, 0)),
-            ],
-            out_shape=[shape((width, seq), bf16), shape((1, piece), f32)],
-            scratch_shapes=[
-                pltpu.VMEM((bins, 2 * INNER, piece), bf16),
-                pltpu.VMEM((bins, 2 * INNER, piece), f32),
-                pltpu.VMEM((seq, piece), f32),
-            ],
-            input_output_aliases={5: 0} if part else {},
-            compiler_params=params(),
-            cost_estimate=cost(2 * work // parts, 2 * table_bytes + spec_bytes),
-            name=f"filter_grad_{part}",
-        )(*operands)
-        skip_parts.append(skip_part)
-    skip_grad = jnp.concatenate(skip_parts, 1).reshape(width)
-    return query_grad, key_grad, value_grad, filter_grad, skip_grad, short_grad
+    short_grad, value_grad, mixed_got = summed_at_owner(short_parts, value_grad, mixed_got)
+    filter_grad, skip_grad = pl.pallas_call(
+        functools.partial(grad_kernel, outer=outer, width=width),
+        in_specs=[hbm] * 5,
+        out_shape=[shape((width, seq), bf16), shape((1, width), f32)],
+        scratch_shapes=[pltpu.VMEM((seq, width), bf16)] * 2
+        + [z_scratch, table_scratch, table_scratch, z_scratch, u_scratch]
+        + [pltpu.VMEM((seq, width), f32), pltpu.SemaphoreType.DMA((5,))],
+        compiler_params=params(),
+        cost_estimate=cost(2 * work, 2 * table_bytes + spec_bytes),
+        name="filter_grad",
+    )(mixed_got, gated_got, gated_spec, ahead, back)
+    return query_grad, key_grad, value_grad, filter_grad, skip_grad.reshape(width), short_grad[:3]
 
 
 def per_device(query_feat, key_feat, value_raw, conv_out, out_grad, filter_taps, short_filter, skip_gain):
@@ -665,11 +720,11 @@
     peers = lax.axis_size("ctx")
     width = channels // peers
     fits = (
-        peers % 4 == 0
+        peers % INNER_PEERS == 0
         and peers & (peers - 1) == 0
-        and rows % 16 == 0
+        and rows == INNER
         and width % 256 == 0
-        and rows * peers in (8 * INNER, 16 * INNER)
+        and peers in (8, 16)
     )
     plan = kernel_plan if fits else general_plan
     return plan(query_feat, key_feat, value_raw, conv_out, out_grad, filter_taps, short_filter, skip_gain)

time: 165 us -> 117 us (0.71)
  the two profiles are of different devices: /device:TPU:1 before, /device:TPU:0 now
where the time goes in v2:
time: 117 us; the launch traced here: 116 us
  waiting for transfers between devices  43.6 us (37%)
  Pallas kernels  38.6 us (33%)
  starting transfers between devices  31.2 us (27%)
  local copies, waits for them, and re-layouts  1.48 us (1%)
    all_to_all x3, waiting for transfers between devices, exchanged(): return lax.all_to_all(block, 'ctx', split_axis=0, concat_axis=0, tiled=True)  31.6 us
    all_to_all x3, starting transfers between devices, exchanged(): return lax.all_to_all(block, 'ctx', split_axis=0, concat_axis=0, tiled=True)  21.3 us
    ppermute x6, waiting for transfers between devices, paired(): lax.ppermute(block, 'ctx', [(i, i ^ distance) for i in range(lax.axis_siz...  12 us
    pallas_call x1, Pallas kernels, kernel_plan(): pl.pallas_call(functools.partial(grad_kernel, outer=outer, width=width),...  7.35 us
    pallas_call x1, Pallas kernels, kernel_plan(): pl.pallas_call(functools.partial(conv_kernel, outer=outer, width=width),...  6.9 us
    ppermute x6, starting transfers between devices, paired(): lax.ppermute(block, 'ctx', [(i, i ^ distance) for i in range(lax.axis_siz...  6.38 us
    pallas_call x1, Pallas kernels, kernel_plan(): pl.pallas_call(functools.partial(filter_kernel, outer=outer, width=width)...  5.69 us
    pallas_call x1, Pallas kernels, kernel_plan(): pl.pallas_call(functools.partial(finish_kernel, width=width), grid=(steps...  4.59 us
  transfers between devices with their start and end apart: 11, of which 4 were waited for; matrix products, arithmetic and copies ran while one was open for 1% of the time, Pallas kernels for 31%

profile of v2, /device:TPU:0, one launch (start us, length us, event | category | flops | bytes accessed | tf_op | source)
XLA Modules:
  0.0 116.2 jit_solution(14367347324043596885)
XLA Ops:
  0.6 2.5 %gate.1.gated_ref = bf16[16,128,256]{2,1,0:T(8,128)(2,1)} custom-call(bf16[128,4096]{1,0:T(8,128)(2,1)} %grad_ref.3, bf16[128,4096]{1,0:T(8,128)(2,1)} %query_ref.1), custom_call_target="tpu_custom_call" | custom-call | flops 524288 | bytes 3145728 | tf_op jit(solution)/shard_map/gate/pallas_call | solution.py:597
  3.1 7.4 %all-to-all-start = ((bf16[16,128,256]{2,1,0:T(8,128)(2,1)}), bf16[16,128,256]{2,1,0:T(8,128)(2,1)}, u32[]{:S(2)}, u32[]{:S(2)}) async-start(bf16[16,128,256]{2,1,0:T(8,128)(2,1)} %gate.1.gated_ref), calls=%async_computation | async-start | bytes 2097152 | tf_op jit(solution)/shard_map/all_to_all | solution.py:539
  10.5 0.9 slice.6
  11.4 2.3 %collective-permute-start = (bf16[2,4096]{1,0:T(2,128)(2,1)S(1)}, bf16[2,4096]{1,0:T(2,128)(2,1)S(1)}, u32[]{:S(2)}, u32[]{:S(2)}) collective-permute-start(bf16[2,4096]{1,0:T(2,128)(2,1)S(1)} %slice.6), channel_id=1, source_target_pairs={{0,1},{1,2},{2,3},{3,4},{4,5},{5,6},{6,7},{7,8},{8,9},{9,10},{10,1... | collective-permute-start | bytes 49160 | tf_op jit(solution)/shard_map/ppermute | solution.py:18
  13.7 3.8 %mix.1 = (bf16[16,128,256]{2,1,0:T(8,128)(2,1)}, bf16[128,4096]{1,0:T(8,128)(2,1)}) custom-call(bf16[128,4096]{1,0:T(8,128)(2,1)} %key_ref.7, bf16[128,4096]{1,0:T(8,128)(2,1)} %value_ref.7, f32[3,4096]{1,0:T(4,128)} %short_ref.7, bf16[128,4096]{1,0:T(8,128)(2,1)} %grad_ref.3, bf16[128,4096]{1,0:T(8,128)(2,1)} %conv_ref.1), custom_call_target="tpu_custom_call" | custom-call | flops 5242880 | bytes 6291456 | tf_op jit(solution)/shard_map/mix/pallas_call | solution.py:627
  17.4 5.7 %filter_spectrum.1.filter_hbm = bf16[17,256,256]{2,1,0:T(8,128)(2,1)} custom-call(bf16[256,2048]{1,0:T(8,128)(2,1)} %taps_ref.1, bf16[17,256,256]{2,1,0:T(8,128)(2,1)} %constant.36.clone.ahead_ref.ahead_hbm), custom_call_target="tpu_custom_call" | custom-call | flops 570425344 | bytes 5505024 | tf_op jit(solution)/shard_map/filter_spectrum/pallas_call | solution.py:617
  23.1 10.4 %all-to-all-done = bf16[16,128,256]{2,1,0:T(8,128)(2,1)} async-done(((bf16[16,128,256]{2,1,0:T(8,128)(2,1)}), bf16[16,128,256]{2,1,0:T(8,128)(2,1)}, u32[]{:S(2)}, u32[]{:S(2)}) %all-to-all-start) | async-done | bytes 1048608 | tf_op jit(solution)/shard_map/all_to_all | solution.py:539
  33.5 6.9 %conv_back.1 = (bf16[2048,256]{1,0:T(8,128)(2,1)}, bf16[17,256,256]{2,1,0:T(8,128)(2,1)}) custom-call(bf16[2048,256]{1,0:T(8,128)(2,1)} %bitcast.gated_hbm, bf16[17,256,256]{2,1,0:T(8,128)(2,1)} %filter_spectrum.1.filter_hbm, bf16[17,256,256]{2,1,0:T(8,128)(2,1)} %constant.36.clone.ahead_ref.ahead_hbm, bf16[17,256,256]{2,1,0:T(8,128)(2,1)} %constant.37.clone.back_hbm), custom_call_target="tpu_custom_call" | custom-call | flops 1140850688 | bytes 11010048 | tf_op jit(solution)/shard_map/conv_back/pallas_call | solution.py:640
  40.4 0.0 collective-permute-done.edge_ref
  40.4 0.0 copy-start
  40.4 6.9 %all-to-all-start.1 = ((bf16[16,128,256]{2,1,0:T(8,128)(2,1)}), bf16[16,128,256]{2,1,0:T(8,128)(2,1)}, u32[]{:S(2)}, u32[]{:S(2)}) async-start(bf16[16,128,256]{2,1,0:T(8,128)(2,1)} %bitcast.13), calls=%async_computation.1 | async-start | bytes 2097152 | tf_op jit(solution)/shard_map/all_to_all | solution.py:539
  47.4 0.0 copy-done
  47.4 1.8 %mix_top.1 = bf16[16,128,256]{2,1,0:T(8,128)(2,1)} custom-call(bf16[128,4096]{1,0:T(8,128)(2,1)} %key_ref.7, bf16[128,4096]{1,0:T(8,128)(2,1)} %value_ref.7, f32[3,4096]{1,0:T(4,128)} %short_ref.7, bf16[2,4096]{1,0:T(2,128)(2,1)} %copy-done, bf16[16,128,256]{2,1,0:T(8,128)(2,1)} %get-tuple-element.42.mixed_in), custom_call_target="tpu_custom_call", output_to_operand_aliasing={{}: (4, {})} | custom-call | flops 655360 | bytes 655360 | tf_op jit(solution)/shard_map/mix_top/pallas_call | solution.py:654
  49.2 21.2 %all-to-all-done.1.back_ref = bf16[16,128,256]{2,1,0:T(8,128)(2,1)} async-done(((bf16[16,128,256]{2,1,0:T(8,128)(2,1)}), bf16[16,128,256]{2,1,0:T(8,128)(2,1)}, u32[]{:S(2)}, u32[]{:S(2)}) %all-to-all-start.1) | async-done | bytes 1048608 | tf_op jit(solution)/shard_map/all_to_all | solution.py:539
  70.4 6.9 %all-to-all-start.2 = ((bf16[16,128,256]{2,1,0:T(8,128)(2,1)}), bf16[16,128,256]{2,1,0:T(8,128)(2,1)}, u32[]{:S(2)}, u32[]{:S(2)}) async-start(bf16[16,128,256]{2,1,0:T(8,128)(2,1)} %mix_top.1), calls=%async_computation.2 | async-start | bytes 2097152 | tf_op jit(solution)/shard_map/all_to_all | solution.py:539
  77.3 4.3 %sums.1 = (bf16[2,4096]{1,0:T(2,128)(2,1)}, bf16[16,4096]{1,0:T(8,128)(2,1)}, f32[4,8,256]{2,1,0:T(8,128)}, f32[4,8,256]{2,1,0:T(8,128)}, f32[4,8,256]{2,1,0:T(8,128)}, /*index=5*/f32[4,8,256]{2,1,0:T(8,128)}) custom-call(bf16[16,128,256]{2,1,0:T(8,128)(2,1)} %all-to-all-done.1.back_ref, bf16[16,128,256]{2,1,0:T(8,128)(2,1)} %gate.1.gated_ref, ...), custom_call_target="tpu_custom_call" | custom-call | flops 10485760 | bytes 4194304 | tf_op jit(solution)/shard_map/sums/pallas_call | solution.py:667
  81.6 1.9 %collective-permute-start.1 = (f32[4,8,256]{2,1,0:T(8,128)}, f32[4,8,256]{2,1,0:T(8,128)S(1)}, u32[]{:S(2)}, u32[]{:S(2)}) collective-permute-start(f32[4,8,256]{2,1,0:T(8,128)} %get-tuple-element.36), channel_id=1, source_target_pairs={{0,4},{1,5},{2,6},{3,7},{4,0},{5,1},{6,2},{7,3},{8,12},{9,13},{10,... | collective-permute-start | bytes 98312 | tf_op jit(solution)/shard_map/ppermute | solution.py:543
  83.5 2.4 %collective-permute-start.2 = (f32[4,8,256]{2,1,0:T(8,128)}, f32[4,8,256]{2,1,0:T(8,128)S(1)}, u32[]{:S(2)}, u32[]{:S(2)}) collective-permute-start(f32[4,8,256]{2,1,0:T(8,128)} %get-tuple-element.37), channel_id=1, source_target_pairs={{0,8},{1,9},{2,10},{3,11},{4,12},{5,13},{6,14},{7,15},{8,0},{9,1},... | collective-permute-start | bytes 98312 | tf_op jit(solution)/shard_map/ppermute | solution.py:543
  85.9 0.2 collective-permute-start.3
  86.0 1.3 %collective-permute-start.4 = (bf16[2,4096]{1,0:T(2,128)(2,1)}, bf16[2,4096]{1,0:T(2,128)(2,1)S(1)}, u32[]{:S(2)}, u32[]{:S(2)}) collective-permute-start(bf16[2,4096]{1,0:T(2,128)(2,1)} %get-tuple-element.40), channel_id=1, source_target_pairs={{1,0},{2,1},{3,2},{4,3},{5,4},{6,5},{7,6},{8,7},{9,8},{10,9},{11,1... | collective-permute-start | bytes 49160 | tf_op jit(solution)/shard_map/ppermute | solution.py:18
  87.4 4.6 %finish.1 = (bf16[128,4096]{1,0:T(8,128)(2,1)}, bf16[128,4096]{1,0:T(8,128)(2,1)}) custom-call(bf16[16,128,256]{2,1,0:T(8,128)(2,1)} %all-to-all-done.1.back_ref, bf16[16,128,256]{2,1,0:T(8,128)(2,1)} %gate.1.gated_ref, bf16[128,4096]{1,0:T(8,128)(2,1)} %key_ref.7, bf16[128,4096]{1,0:T(8,128)(2,1)} %value_ref.7, bf16[2,4096]{1,0:T(2,128)(2,1)} %copy-done, ...), custom_call_target="tpu_custom_call" | custom-call | flops 15728640 | bytes 6291456 | tf_op jit(solution)/shard_map/finish/pallas_call | solution.py:680
  91.9 0.0 copy-start.1
  91.9 0.0 collective-permute-done.4.head_ref
  92.0 0.0 copy-start.2
  92.0 0.6 copy-done.2
  92.6 1.7 %seam.1 = bf16[128,4096]{1,0:T(8,128)(2,1)} custom-call(bf16[16,4096]{1,0:T(8,128)(2,1)} %get-tuple-element.39.tail_ref, bf16[2,4096]{1,0:T(2,128)(2,1)} %copy-done.2, f32[3,4096]{1,0:T(4,128)} %short_ref.7, bf16[128,4096]{1,0:T(8,128)(2,1)} %get-tuple-element.41.done_ref), custom_call_target="tpu_custom_call", output_to_operand_aliasing={{}: (3, {})} | custom-call | flops 327680 | bytes 393216 | tf_op jit(solution)/shard_map/seam/pallas_call | solution.py:692
  94.3 2.0 %collective-permute-done.1 = f32[4,8,256]{2,1,0:T(8,128)S(1)} collective-permute-done((f32[4,8,256]{2,1,0:T(8,128)}, f32[4,8,256]{2,1,0:T(8,128)S(1)}, u32[]{:S(2)}, u32[]{:S(2)}) %collective-permute-start.1) | collective-permute-done | bytes 32800 | tf_op jit(solution)/shard_map/ppermute | solution.py:543
  96.3 10.0 %collective-permute-done.2 = f32[4,8,256]{2,1,0:T(8,128)S(1)} collective-permute-done((f32[4,8,256]{2,1,0:T(8,128)}, f32[4,8,256]{2,1,0:T(8,128)S(1)}, u32[]{:S(2)}, u32[]{:S(2)}) %collective-permute-start.2) | collective-permute-done | bytes 32800 | tf_op jit(solution)/shard_map/ppermute | solution.py:543
  106.3 0.0 collective-permute-done.3
  106.3 0.0 copy-done.1
  106.3 0.0 all-to-all-done.2
  106.3 0.1 collective-permute-start.5
  106.4 1.5 %collective-permute-start.6 = (f32[8,256]{1,0:T(8,128)S(1)}, f32[8,256]{1,0:T(8,128)S(1)}, u32[]{:S(2)}, u32[]{:S(2)}) collective-permute-start(f32[8,256]{1,0:T(8,128)S(1)} %get-tuple-element.52), channel_id=1, source_target_pairs={{0,2},{1,3},{2,0},{3,1},{4,6},{5,7},{6,4},{7,5},{8,10},{9,11},{10,... | collective-permute-start | bytes 24584 | tf_op jit(solution)/shard_map/ppermute | solution.py:543
  107.9 0.3 collective-permute-start.7
  108.3 7.3 %filter_grad.1 = (bf16[256,2048]{1,0:T(8,128)(2,1)}, f32[1,256]{1,0:T(1,128)}) custom-call(bf16[2048,256]{1,0:T(8,128)(2,1)} %bitcast.3.mixed_hbm, bf16[2048,256]{1,0:T(8,128)(2,1)} %bitcast.gated_hbm, bf16[17,256,256]{2,1,0:T(8,128)(2,1)} %get-tuple-element.46.spec_hbm, bf16[17,256,256]{2,1,0:T(8,128)(2,1)} %constant.36.clone.ahead_ref.ahead_hbm, ...), custom_call_target="tpu_custom_call" | custom-call | flops 1140850688 | bytes 6684672 | tf_op jit(solution)/shard_map/filter_grad/pallas_call | solution.py:704
  115.6 0.0 collective-permute-done.5
  115.6 0.0 collective-permute-done.6
  115.6 0.0 collective-permute-done.7
  115.6 0.6 slice_add_fusion
  (2 shorter events, 0.0 us)
Async XLA Ops:
  3.1 30.4 %all-to-all-start = ((bf16[16,128,256]{2,1,0:T(8,128)(2,1)}), bf16[16,128,256]{2,1,0:T(8,128)(2,1)}, u32[]{:S(2)}, u32[]{:S(2)}) async-start(bf16[16,128,256]{2,1,0:T(8,128)(2,1)} %gate.1.gated_ref), calls=%async_computation | async-start | bytes 2097152 | tf_op jit(solution)/shard_map/all_to_all | solution.py:539
  11.4 29.0 %collective-permute-start = (bf16[2,4096]{1,0:T(2,128)(2,1)S(1)}, bf16[2,4096]{1,0:T(2,128)(2,1)S(1)}, u32[]{:S(2)}, u32[]{:S(2)}) collective-permute-start(bf16[2,4096]{1,0:T(2,128)(2,1)S(1)} %slice.6), channel_id=1, source_target_pairs={{0,1},{1,2},{2,3},{3,4},{4,5},{5,6},{6,7},{7,8},{8,9},{9,10},{10,1... | collective-permute-start | bytes 49160 | tf_op jit(solution)/shard_map/ppermute | solution.py:18
  40.4 6.9 %copy-start = (bf16[2,4096]{1,0:T(2,128)(2,1)}, bf16[2,4096]{1,0:T(2,128)(2,1)S(1)}, u32[]{:S(2)}) copy-start(bf16[2,4096]{1,0:T(2,128)(2,1)S(1)} %collective-permute-done.edge_ref) | copy-start | bytes 49156
  40.4 29.9 %all-to-all-start.1 = ((bf16[16,128,256]{2,1,0:T(8,128)(2,1)}), bf16[16,128,256]{2,1,0:T(8,128)(2,1)}, u32[]{:S(2)}, u32[]{:S(2)}) async-start(bf16[16,128,256]{2,1,0:T(8,128)(2,1)} %bitcast.13), calls=%async_computation.1 | async-start | bytes 2097152 | tf_op jit(solution)/shard_map/all_to_all | solution.py:539
  70.4 35.9 %all-to-all-start.2 = ((bf16[16,128,256]{2,1,0:T(8,128)(2,1)}), bf16[16,128,256]{2,1,0:T(8,128)(2,1)}, u32[]{:S(2)}, u32[]{:S(2)}) async-start(bf16[16,128,256]{2,1,0:T(8,128)(2,1)} %mix_top.1), calls=%async_computation.2 | async-start | bytes 2097152 | tf_op jit(solution)/shard_map/all_to_all | solution.py:539
  81.6 14.7 %collective-permute-start.1 = (f32[4,8,256]{2,1,0:T(8,128)}, f32[4,8,256]{2,1,0:T(8,128)S(1)}, u32[]{:S(2)}, u32[]{:S(2)}) collective-permute-start(f32[4,8,256]{2,1,0:T(8,128)} %get-tuple-element.36), channel_id=1, source_target_pairs={{0,4},{1,5},{2,6},{3,7},{4,0},{5,1},{6,2},{7,3},{8,12},{9,13},{10,... | collective-permute-start | bytes 98312 | tf_op jit(solution)/shard_map/ppermute | solution.py:543
  83.5 22.7 %collective-permute-start.2 = (f32[4,8,256]{2,1,0:T(8,128)}, f32[4,8,256]{2,1,0:T(8,128)S(1)}, u32[]{:S(2)}, u32[]{:S(2)}) collective-permute-start(f32[4,8,256]{2,1,0:T(8,128)} %get-tuple-element.37), channel_id=1, source_target_pairs={{0,8},{1,9},{2,10},{3,11},{4,12},{5,13},{6,14},{7,15},{8,0},{9,1},... | collective-permute-start | bytes 98312 | tf_op jit(solution)/shard_map/ppermute | solution.py:543
  85.9 20.4 %collective-permute-start.3 = (f32[4,8,256]{2,1,0:T(8,128)}, f32[4,8,256]{2,1,0:T(8,128)S(1)}, u32[]{:S(2)}, u32[]{:S(2)}) collective-permute-start(f32[4,8,256]{2,1,0:T(8,128)} %get-tuple-element.38), channel_id=1, source_target_pairs={{0,12},{1,13},{2,14},{3,15},{4,8},{5,9},{6,10},{7,11},{8,4},{9,5},... | collective-permute-start | bytes 98312 | tf_op jit(solution)/shard_map/ppermute | solution.py:543
  86.0 5.9 %collective-permute-start.4 = (bf16[2,4096]{1,0:T(2,128)(2,1)}, bf16[2,4096]{1,0:T(2,128)(2,1)S(1)}, u32[]{:S(2)}, u32[]{:S(2)}) collective-permute-start(bf16[2,4096]{1,0:T(2,128)(2,1)} %get-tuple-element.40), channel_id=1, source_target_pairs={{1,0},{2,1},{3,2},{4,3},{5,4},{6,5},{7,6},{8,7},{9,8},{10,9},{11,1... | collective-permute-start | bytes 49160 | tf_op jit(solution)/shard_map/ppermute | solution.py:18
  91.9 14.3 %copy-start.1 = (f32[4,8,256]{2,1,0:T(8,128)S(1)}, f32[4,8,256]{2,1,0:T(8,128)}, u32[]{:S(2)}) copy-start(f32[4,8,256]{2,1,0:T(8,128)} %get-tuple-element.35) | copy-start | bytes 98308
  92.0 0.6 copy-start.2
  106.3 9.3 %collective-permute-start.5 = (f32[8,256]{1,0:T(8,128)S(1)}, f32[8,256]{1,0:T(8,128)S(1)}, u32[]{:S(2)}, u32[]{:S(2)}) collective-permute-start(f32[8,256]{1,0:T(8,128)S(1)} %get-tuple-element.53), channel_id=1, source_target_pairs={{0,1},{1,0},{2,3},{3,2},{4,5},{5,4},{6,7},{7,6},{8,9},{9,8},{10,11... | collective-permute-start | bytes 24584 | tf_op jit(solution)/shard_map/ppermute | solution.py:543
  106.4 9.2 %collective-permute-start.6 = (f32[8,256]{1,0:T(8,128)S(1)}, f32[8,256]{1,0:T(8,128)S(1)}, u32[]{:S(2)}, u32[]{:S(2)}) collective-permute-start(f32[8,256]{1,0:T(8,128)S(1)} %get-tuple-element.52), channel_id=1, source_target_pairs={{0,2},{1,3},{2,0},{3,1},{4,6},{5,7},{6,4},{7,5},{8,10},{9,11},{10,... | collective-permute-start | bytes 24584 | tf_op jit(solution)/shard_map/ppermute | solution.py:543
  107.9 7.7 %collective-permute-start.7 = (f32[8,256]{1,0:T(8,128)S(1)}, f32[8,256]{1,0:T(8,128)S(1)}, u32[]{:S(2)}, u32[]{:S(2)}) collective-permute-start(f32[8,256]{1,0:T(8,128)S(1)} %get-tuple-element.51), channel_id=1, source_target_pairs={{0,3},{1,2},{2,1},{3,0},{4,7},{5,6},{6,5},{7,4},{8,11},{9,10},{10,... | collective-permute-start | bytes 24584 | tf_op jit(solution)/shard_map/ppermute | solution.py:543

commit v3 on v2

--- a/solution.py
+++ b/solution.py
@@ -360,19 +360,35 @@
     spec_out.wait()
 
 
-def grad_kernel(
-    mixed_hbm, gated_hbm, spec_hbm, ahead_hbm, back_hbm, grad_ref, skip_ref,
-    mixed_ref, gated_ref, spec_ref, ahead_ref, back_ref, z_ref, u_ref, rows_ref, sems, *, outer, width,
-):
+def grad_kernel(*refs, outer, width):
+    far = outer // 2 // INNER_PEERS
+    place_hbm, refs = refs[:far], refs[far:]
+    near_hbm, refs = refs[: INNER_PEERS - 1], refs[INNER_PEERS - 1 :]
+    far_hbm, refs = refs[: far - 1], refs[far - 1 :]
+    gated_hbm, spec_hbm, ahead_hbm, back_hbm, grad_ref, skip_ref = refs[:6]
+    mixed_ref, gated_ref, spec_ref, ahead_ref, back_ref, z_ref, u_ref, rows_ref, sems = refs[6:]
     slabs = outer // 2
-    mixed_in = begun(mixed_hbm, mixed_ref, sems.at[0])
-    ahead_in = begun(ahead_hbm, ahead_ref, sems.at[1])
-    spec_in = begun(spec_hbm, spec_ref, sems.at[2])
-    back_in = begun(back_hbm, back_ref, sems.at[3])
-    gated_in = begun(gated_hbm, gated_ref, sems.at[4])
-    mixed_in.wait()
+    me = lax.axis_index("ctx")
+    own_row, own_place = me // INNER_PEERS, me % INNER_PEERS
+    mixed_in = []
+    for d in range(far):
+        for e in range(INNER_PEERS):
+            if e == 0:
+                source = place_hbm[d]
+            elif d == 0:
+                source = near_hbm[e - 1].at[own_row]
+            else:
+                source = far_hbm[d - 1].at[e - 1]
+            slab = (own_row ^ d) * INNER_PEERS + (own_place ^ e)
+            mixed_in.append(begun(source, mixed_ref.at[slab], sems.at[4 + len(mixed_in)]))
+    ahead_in = begun(ahead_hbm, ahead_ref, sems.at[0])
+    spec_in = begun(spec_hbm, spec_ref, sems.at[1])
+    back_in = begun(back_hbm, back_ref, sems.at[2])
+    gated_in = begun(gated_hbm, gated_ref, sems.at[3])
+    for copy in mixed_in:
+        copy.wait()
     outer_ahead(
-        lambda a, row, lane: mixed_ref[pl.ds(a * INNER + row, 16), lane : lane + 128],
+        lambda a, row, lane: mixed_ref[a, pl.ds(row, 16), lane : lane + 128],
         z_ref, outer, width,
     )
     ahead_in.wait()
@@ -396,11 +412,19 @@
 
     def add(a, total):
         place = pl.ds(pl.multiple_of(a * INNER, INNER), INNER)
-        part = gated_ref[place, :].astype(jnp.float32) * mixed_ref[place, :].astype(jnp.float32)
+        part = gated_ref[place, :].astype(jnp.float32) * mixed_ref[a].astype(jnp.float32)
         return total + jnp.sum(part.reshape(INNER // 8, 8, width), axis=0)
 
     total = lax.fori_loop(0, slabs, add, jnp.zeros((8, width), jnp.float32))
     skip_ref[...] = jnp.sum(total, axis=0, keepdims=True)
+
+
+def regroup_kernel(*refs):
+    near, far = refs[: INNER_PEERS - 1], refs[INNER_PEERS - 1 :]
+    own_row = lax.axis_index("ctx") // INNER_PEERS
+    for d in range(1, len(far) + 1):
+        for e in range(1, INNER_PEERS):
+            far[d - 1][e - 1] = near[e - 1][own_row ^ d]
 
 
 def shifted_down(values, distance, edge):
@@ -429,100 +453,92 @@
         ).astype(jnp.bfloat16)
 
 
-def mixed_values(key_ref, value_ref, short_ref, cols, edge):
-    value = value_ref[:, cols].astype(jnp.float32)
-    conv = (
-        short_ref[0:1, cols] * value
-        + short_ref[1:2, cols] * shifted_down(value, 1, edge)
-        + short_ref[2:3, cols] * shifted_down(value, 2, edge)
-    )
-    return (key_ref[:, cols].astype(jnp.float32) * conv).astype(jnp.bfloat16)
-
-
-def mix_kernel(key_ref, value_ref, short_ref, grad_ref, conv_ref, mixed_ref, query_grad_ref, *, width):
-    zero = jnp.zeros((2, 128), jnp.float32)
-    for j in range(mixed_ref.shape[0]):
+def mix_kernel(key_ref, value_ref, edge_ref, short_ref, grad_ref, conv_ref, *rest, width):
+    near_refs, place_refs = rest[: INNER_PEERS - 1], rest[INNER_PEERS - 1 : -3]
+    query_grad_ref, behind, mixed_ref = rest[-3:]
+    rows = key_ref.shape[0]
+    owners = key_ref.shape[1] // width
+    step = pl.program_id(0)
+    for j in range(owners):
         for lane in range(0, width, 128):
+            slot = (j * width + lane) // 128 % 2
             cols = slice(j * width + lane, j * width + lane + 128)
-            mixed_ref[j, :, lane : lane + 128] = mixed_values(
-                key_ref, value_ref, short_ref, cols, zero
+            value = value_ref[:, cols].astype(jnp.float32)
+            behind[slot, 6:8] = edge_ref[:, cols].astype(jnp.float32)
+            behind[slot, 8 : 8 + rows] = value
+            conv = (
+                short_ref[0:1, cols] * value
+                + short_ref[1:2, cols] * behind[slot, 7 : 7 + rows]
+                + short_ref[2:3, cols] * behind[slot, 6 : 6 + rows]
             )
+            mixed_ref[step * owners + j, :, lane : lane + 128] = (
+                key_ref[:, cols].astype(jnp.float32) * conv
+            ).astype(jnp.bfloat16)
             query_grad_ref[:, cols] = (
                 grad_ref[:, cols].astype(jnp.float32) * conv_ref[:, cols].astype(jnp.float32)
             ).astype(jnp.bfloat16)
 
-
-def mix_top_kernel(key_ref, value_ref, short_ref, edge_ref, mixed_in, mixed_ref, *, width):
-    for j in range(mixed_ref.shape[0]):
+    @pl.when(step == pl.num_programs(0) - 1)
+    def _():
+        me = lax.axis_index("ctx")
+        own_row, place = me // INNER_PEERS, me % INNER_PEERS
+        for e, near_ref in enumerate(near_refs, 1):
+            for row in range(near_ref.shape[0]):
+                near_ref[row] = mixed_ref[row * INNER_PEERS + (place ^ e)]
+        for d, place_ref in enumerate(place_refs):
+            place_ref[...] = mixed_ref[(own_row ^ d) * INNER_PEERS + place]
+
+
+def finish_kernel(
+    back_ref, gated_ref, key_ref, value_ref, edge_ref, short_ref, skip_ref,
+    key_grad_ref, value_grad_ref, head_ref, tail_ref, *rest, width,
+):
+    part_refs, behind, ahead, sums_ref = rest[:-3], rest[-3], rest[-2], rest[-1]
+    rows = key_ref.shape[0]
+    owners = back_ref.shape[0]
+    step = pl.program_id(0)
+    for j in range(owners):
         for lane in range(0, width, 128):
-            cols = slice(j * width + lane, j * width + lane + 128)
-            edge = edge_ref[:, cols].astype(jnp.float32)
-            mixed_ref[j, :, lane : lane + 128] = mixed_values(
-                key_ref, value_ref, short_ref, cols, edge
-            )
-
-
-def sums_kernel(
-    back_ref, gated_ref, key_ref, value_ref, edge_ref, skip_ref, head_ref, tail_ref, *part_refs, width
-):
-    rows = key_ref.shape[0]
-    first = pl.program_id(0) * (back_ref.shape[0] // INNER_PEERS)
-    own = lax.axis_index("ctx") // INNER_PEERS
-    for j in range(back_ref.shape[0]):
-        distance = (first + j // INNER_PEERS) ^ own
-        for lane in range(0, width, 128):
+            slot = (j * width + lane) // 128 % 2
             cols = slice(j * width + lane, j * width + lane + 128)
             lanes = slice(lane, lane + 128)
+            short = [short_ref[i : i + 1, cols] for i in range(3)]
             value = value_ref[:, cols].astype(jnp.float32)
-            edge = edge_ref[:, cols].astype(jnp.float32)
+            behind[slot, 6:8] = edge_ref[:, cols].astype(jnp.float32)
+            behind[slot, 8 : 8 + rows] = value
+            value_1 = behind[slot, 7 : 7 + rows]
+            value_2 = behind[slot, 6 : 6 + rows]
             mixed_grad = back_ref[j, :, lanes].astype(jnp.float32) + skip_ref[:, cols] * gated_ref[
                 j, :, lanes
             ].astype(jnp.float32)
+            conv = short[0] * value + short[1] * value_1 + short[2] * value_2
+            key_grad_ref[:, cols] = (mixed_grad * conv).astype(jnp.bfloat16)
             feature = (mixed_grad * key_ref[:, cols].astype(jnp.float32)).astype(jnp.bfloat16)
             head_ref[:, cols] = feature[:2]
             tail_ref[:, cols] = feature[rows - 16 :]
             feature = feature.astype(jnp.float32)
-            shifted = (value, shifted_down(value, 1, edge), shifted_down(value, 2, edge))
+            ahead[slot, 0:rows] = feature
+            ahead[slot, rows : rows + 8] = jnp.zeros((8, 128), jnp.float32)
+            value_grad_ref[:, cols] = (
+                short[0] * feature
+                + short[1] * ahead[slot, 1 : 1 + rows]
+                + short[2] * ahead[slot, 2 : 2 + rows]
+            ).astype(jnp.bfloat16)
             sums = jnp.concatenate(
-                [jnp.sum(feature * other, axis=0, keepdims=True) for other in shifted]
+                [
+                    jnp.sum(feature * other, axis=0, keepdims=True)
+                    for other in (value, value_1, value_2)
+                ]
                 + [jnp.zeros((5, 128), jnp.float32)],
                 0,
             )
-            for d, part_ref in enumerate(part_refs):
-
-                @pl.when(distance == d)
-                def _(part_ref=part_ref, sums=sums):
-                    part_ref[j % INNER_PEERS, :, lanes] = sums
-
-
-def finish_kernel(
-    back_ref, gated_ref, key_ref, value_ref, edge_ref, short_ref, skip_ref, key_grad_ref,
-    value_grad_ref, *, width,
-):
-    for j in range(back_ref.shape[0]):
-        for lane in range(0, width, 128):
-            cols = slice(j * width + lane, j * width + lane + 128)
-            lanes = slice(lane, lane + 128)
-            value = value_ref[:, cols].astype(jnp.float32)
-            edge = edge_ref[:, cols].astype(jnp.float32)
-            short = [short_ref[i : i + 1, cols] for i in range(3)]
-            conv = (
-                short[0] * value
-                + short[1] * shifted_down(value, 1, edge)
-                + short[2] * shifted_down(value, 2, edge)
-            )
-            mixed_grad = back_ref[j, :, lanes].astype(jnp.float32) + skip_ref[:, cols] * gated_ref[
-                j, :, lanes
-            ].astype(jnp.float32)
-            key_grad_ref[:, cols] = (mixed_grad * conv).astype(jnp.bfloat16)
-            feature = (mixed_grad * key_ref[:, cols].astype(jnp.float32)).astype(jnp.bfloat16)
-            feature = feature.astype(jnp.float32)
-            zero = jnp.zeros((2, 128), jnp.float32)
-            value_grad_ref[:, cols] = (
-                short[0] * feature
-                + short[1] * shifted_up(feature, 1, zero)
-                + short[2] * shifted_up(feature, 2, zero)
-            ).astype(jnp.bfloat16)
+            sums_ref[step * owners + j, :, lanes] = sums
+
+    @pl.when(step == pl.num_programs(0) - 1)
+    def _():
+        own = lax.axis_index("ctx") // INNER_PEERS
+        for d, part_ref in enumerate(part_refs):
+            part_ref[...] = sums_ref[pl.ds((own ^ d) * INNER_PEERS, INNER_PEERS)]
 
 
 def seam_kernel(tail_ref, head_ref, short_ref, done_ref, value_grad_ref):
@@ -545,10 +561,9 @@
 
 def summed_at_owner(parts, *beside):
     place = lax.axis_index("ctx") % INNER_PEERS
-    rows = parts[0]
-    for distance in range(1, len(parts)):
-        rows = rows + paired(parts[distance], distance * INNER_PEERS)
-    rows, *beside = lax.optimization_barrier((rows, *beside))
+    got = [parts[0]] + [paired(parts[d], d * INNER_PEERS) for d in range(1, len(parts))]
+    rows = sum(got[1:], got[0])
+    rows, beside = lax.optimization_barrier((rows, beside))
     total = lax.dynamic_index_in_dim(rows, place, 0, keepdims=False)
     for distance in range(1, INNER_PEERS):
         other = lax.dynamic_index_in_dim(rows, place ^ distance, 0, keepdims=False)
@@ -581,7 +596,8 @@
     group = peers // steps
     span = group * width
     far = peers // INNER_PEERS
-    hbm = pl.BlockSpec(memory_space=pl.ANY)
+    any_place = pl.BlockSpec(memory_space=pl.ANY)
+    hbm = pl.BlockSpec(memory_space=pltpu.HBM)
     bf16, f32 = jnp.bfloat16, jnp.float32
     shape = jax.ShapeDtypeStruct
     skip_row = skip_gain.reshape(1, channels)
@@ -614,28 +630,52 @@
     table_bytes = 8 * bins * INNER * INNER
     spec_bytes = 4 * bins * INNER * width
     work = 2 * bins * (2 * INNER) ** 2 * width
+    edge = passed_along(value_raw[rows - 2 :], "ctx", 1)
+    whole = lambda size: pl.BlockSpec((size, channels), lambda i: (0, 0))
+    shift_scratch = pltpu.VMEM((2, rows + 8, 128), f32)
+    near_spec = pl.BlockSpec((far, rows, width), lambda i: (0, 0, 0))
+    far_spec = pl.BlockSpec((INNER_PEERS - 1, rows, width), lambda i: (0, 0, 0))
+    place_spec = pl.BlockSpec((rows, width), lambda i: (0, 0))
+    *mixed, query_grad = pl.pallas_call(
+        functools.partial(mix_kernel, width=width),
+        grid=(steps,),
+        in_specs=[flat, flat, edge_spec, short_spec, flat, flat],
+        out_specs=[near_spec] * (INNER_PEERS - 1) + [place_spec] * far + [flat],
+        out_shape=[shape((far, rows, width), bf16)] * (INNER_PEERS - 1)
+        + [shape((rows, width), bf16)] * far
+        + [shape((rows, channels), bf16)],
+        scratch_shapes=[shift_scratch, pltpu.VMEM((peers, rows, width), bf16)],
+        compiler_params=params(),
+        cost_estimate=cost(40000000000, 12 * rows * channels),
+        name="mix",
+    )(key_feat, value_raw, edge, short_filter, out_grad, conv_out)
+    near = [paired(mixed[e - 1], e) for e in range(1, INNER_PEERS)]
+    placed = mixed[INNER_PEERS - 1 :]
+
+    placed = [placed[0]] + [paired(placed[d], d * INNER_PEERS) for d in range(1, far)]
+    across = pl.pallas_call(
+        regroup_kernel,
+        grid=(1,),
+        in_specs=[near_spec] * (INNER_PEERS - 1),
+        out_specs=[far_spec] * (far - 1),
+        out_shape=[shape((INNER_PEERS - 1, rows, width), bf16)] * (far - 1),
+        compiler_params=params(),
+        cost_estimate=cost(0, 4 * seq * width),
+        name="regroup",
+    )(*near)
+    filter_taps, query_grad = lax.optimization_barrier((filter_taps, query_grad))
     filter_spec = pl.pallas_call(
         functools.partial(filter_kernel, outer=outer, width=width),
         out_shape=spec_shape,
         scratch_shapes=[pltpu.VMEM((seq, width), f32), z_scratch],
         compiler_params=params(),
-        cost_estimate=cost(work, table_bytes + spec_bytes + 2 * seq * width),
+        cost_estimate=cost(40000000000, table_bytes + spec_bytes + 2 * seq * width),
         name="filter_spectrum",
     )(filter_taps, ahead)
 
-    whole = lambda size: pl.BlockSpec((size, channels), lambda i: (0, 0))
-    mixed, query_grad = pl.pallas_call(
-        functools.partial(mix_kernel, width=width),
-        grid=(steps,),
-        in_specs=[flat, flat, short_spec, flat, flat],
-        out_specs=[owned, flat],
-        out_shape=[shape((peers, rows, width), bf16), shape((rows, channels), bf16)],
-        compiler_params=params(),
-        cost_estimate=cost(10 * rows * channels, 12 * rows * channels),
-        name="mix",
-    )(key_feat, value_raw, short_filter, out_grad, conv_out)
-    filter_spec, mixed = lax.optimization_barrier((filter_spec, mixed))
-    edge = passed_along(value_raw[rows - 2 :], "ctx", 1)
+
+    *across, gated_got = lax.optimization_barrier((*across, gated_got))
+    across = [paired(across[d - 1], d * INNER_PEERS) for d in range(1, far)]
 
     conv_back, gated_spec = pl.pallas_call(
         functools.partial(conv_kernel, outer=outer, width=width),
@@ -645,50 +685,51 @@
         scratch_shapes=[pltpu.VMEM((seq, width), bf16), z_scratch, table_scratch, table_scratch, z_scratch]
         + [z_scratch, u_scratch, pltpu.SemaphoreType.DMA((5,))],
         compiler_params=params(),
-        cost_estimate=cost(2 * work, 2 * table_bytes + 2 * spec_bytes + 4 * seq * width),
+        cost_estimate=cost(40000000000, 2 * table_bytes + 2 * spec_bytes + 4 * seq * width),
         name="conv_back",
     )(gated_got, filter_spec, ahead, back)
 
-    conv_back, edge = lax.optimization_barrier((conv_back, edge))
     back_got = exchanged(conv_back).reshape(peers, rows, width)
-    mixed = pl.pallas_call(
-        functools.partial(mix_top_kernel, width=width),
-        grid=(1,),
-        in_specs=[whole(16), whole(16), whole(3), whole(2), hbm],
-        out_specs=pl.BlockSpec((peers, 16, width), lambda i: (0, 0, 0)),
-        out_shape=shape((peers, rows, width), bf16),
-        input_output_aliases={4: 0},
+
+
+    filter_grad, skip_grad = pl.pallas_call(
+        functools.partial(grad_kernel, outer=outer, width=width),
+        in_specs=[hbm] * (INNER_PEERS + 2 * far + 2),
+        out_shape=[shape((width, seq), bf16), shape((1, width), f32)],
+        scratch_shapes=[
+            pltpu.VMEM((peers, rows, width), bf16),
+            pltpu.VMEM((seq, width), bf16),
+            z_scratch,
+            table_scratch,
+            table_scratch,
+            z_scratch,
+            u_scratch,
+            pltpu.VMEM((seq, width), f32),
+            pltpu.SemaphoreType.DMA((peers + 4,)),
+        ],
         compiler_params=params(),
-        cost_estimate=cost(10 * 16 * channels, 10 * 16 * channels),
-        name="mix_top",
-    )(key_feat, value_raw, short_filter, edge, mixed)
-    mixed_got = exchanged(after(mixed, back_got).reshape(seq, width))
-
-    head, tail, *short_parts = pl.pallas_call(
-        functools.partial(sums_kernel, width=width),
-        grid=(steps,),
-        in_specs=[owned, owned, flat, flat, edge_spec, skip_spec],
-        out_specs=[edge_spec, tail_spec]
-        + [pl.BlockSpec((INNER_PEERS, 8, width), lambda i: (0, 0, 0))] * far,
-        out_shape=[shape((2, channels), bf16), shape((16, channels), bf16)]
-        + [shape((INNER_PEERS, 8, width), f32)] * far,
-        compiler_params=params(),
-        cost_estimate=cost(20 * rows * channels, 8 * rows * channels),
-        name="sums",
-    )(back_got, gated, key_feat, value_raw, edge, skip_row)
-
-    key_grad, value_grad = pl.pallas_call(
+        cost_estimate=cost(100000000000, 2 * table_bytes + spec_bytes),
+        name="filter_grad",
+    )(*placed, *near, *across, gated_got, gated_spec, ahead, back)
+    back_got, filter_grad, skip_grad = lax.optimization_barrier((back_got, filter_grad, skip_grad))
+
+    key_grad, value_grad, head, tail, *short_parts = pl.pallas_call(
         functools.partial(finish_kernel, width=width),
         grid=(steps,),
         in_specs=[owned, owned, flat, flat, edge_spec, short_spec, skip_spec],
-        out_specs=[flat, flat],
-        out_shape=[shape((rows, channels), bf16)] * 2,
+        out_specs=[flat, flat, edge_spec, tail_spec]
+        + [pl.BlockSpec((INNER_PEERS, 8, width), lambda i: (0, 0, 0))] * far,
+        out_shape=[shape((rows, channels), bf16)] * 2
+        + [shape((2, channels), bf16), shape((16, channels), bf16)]
+        + [shape((INNER_PEERS, 8, width), f32)] * far,
+        scratch_shapes=[pltpu.VMEM((2, rows + 8, 128), f32)] * 2 + [pltpu.VMEM((peers, 8, width), f32)],
         compiler_params=params(),
         cost_estimate=cost(30 * rows * channels, 12 * rows * channels),
         name="finish",
     )(back_got, gated, key_feat, value_raw, edge, short_filter, skip_row)
 
     head_got = passed_along(head, "ctx", -1)
+    short_grad, head_got, value_grad = summed_at_owner(short_parts, head_got, value_grad)
     value_grad = pl.pallas_call(
         seam_kernel,
         grid=(1,),
@@ -700,18 +741,6 @@
         cost_estimate=cost(5 * 16 * channels, 6 * 16 * channels),
         name="seam",
     )(tail, head_got, short_filter, value_grad)
-    short_grad, value_grad, mixed_got = summed_at_owner(short_parts, value_grad, mixed_got)
-    filter_grad, skip_grad = pl.pallas_call(
-        functools.partial(grad_kernel, outer=outer, width=width),
-        in_specs=[hbm] * 5,
-        out_shape=[shape((width, seq), bf16), shape((1, width), f32)],
-        scratch_shapes=[pltpu.VMEM((seq, width), bf16)] * 2
-        + [z_scratch, table_scratch, table_scratch, z_scratch, u_scratch]
-        + [pltpu.VMEM((seq, width), f32), pltpu.SemaphoreType.DMA((5,))],
-        compiler_params=params(),
-        cost_estimate=cost(2 * work, 2 * table_bytes + spec_bytes),
-        name="filter_grad",
-    )(mixed_got, gated_got, gated_spec, ahead, back)
     return query_grad, key_grad, value_grad, filter_grad, skip_grad.reshape(width), short_grad[:3]
 
 

time: 117 us -> 106 us (0.906)
  waiting for transfers between devices: 43.6 us -> 29.1 us
  starting transfers between devices: 31.2 us -> 35.3 us
  Pallas kernels: 38.6 us -> 35.6 us
  local copies, waits for them, and re-layouts: 1.48 us -> 2.92 us
    all_to_all x3 -> x2, waiting for transfers between devices: 31.6 us -> 14.8 us  [exchanged(): return lax.all_to_all(block, 'ctx', split_axis=0, concat_axis=0, tiled=True)]
    ppermute x6 -> x15, starting transfers between devices: 6.38 us -> 20 us  [paired(): lax.ppermute(block, 'ctx', [(i, i ^ distance) for i in range(lax.axis_siz...]
    all_to_all x3 -> x2, starting transfers between devices: 21.3 us -> 11.6 us  [exchanged(): return lax.all_to_all(block, 'ctx', split_axis=0, concat_axis=0, tiled=True)]
    pallas_call x2 -> x1, Pallas kernels: 6.05 us -> 1.95 us  [kernel_plan(): pl.pallas_call(regroup_kernel, grid=(1,), in_specs=[near_spec] * (INNER_P...]
    ppermute x6 -> x15, waiting for transfers between devices: 12 us -> 14.3 us  [paired(): lax.ppermute(block, 'ctx', [(i, i ^ distance) for i in range(lax.axis_siz...]
    unnamed x6 -> x22, local copies, waits for them, and re-layouts: 0.6 us -> 2.04 us
  transfers between devices with their start and end apart: 11 -> 19, of which waited for: 4 -> 7; matrix products, arithmetic and copies ran while one was open for 1% -> 1% of each run, Pallas kernels for 31% -> 29%
where the time goes in v3:
time: 106 us; the launch traced here: 105 us
  Pallas kernels  35.6 us (34%)
  starting transfers between devices  35.3 us (33%)
  waiting for transfers between devices  29.1 us (27%)
  local copies, waits for them, and re-layouts  2.92 us (3%)
  other arithmetic  1.37 us (1%)
    ppermute x15, starting transfers between devices, paired(): lax.ppermute(block, 'ctx', [(i, i ^ distance) for i in range(lax.axis_siz...  20 us
    all_to_all x2, waiting for transfers between devices, exchanged(): return lax.all_to_all(block, 'ctx', split_axis=0, concat_axis=0, tiled=True)  14.8 us
    ppermute x15, waiting for transfers between devices, paired(): lax.ppermute(block, 'ctx', [(i, i ^ distance) for i in range(lax.axis_siz...  14.3 us
    all_to_all x2, starting transfers between devices, exchanged(): return lax.all_to_all(block, 'ctx', split_axis=0, concat_axis=0, tiled=True)  11.6 us
    pallas_call x1, Pallas kernels, kernel_plan(): pl.pallas_call(functools.partial(grad_kernel, outer=outer, width=width),...  7.59 us
    pallas_call x1, Pallas kernels, kernel_plan(): pl.pallas_call(functools.partial(conv_kernel, outer=outer, width=width),...  6.9 us
    pallas_call x1, Pallas kernels, kernel_plan(): pl.pallas_call(functools.partial(filter_kernel, outer=outer, width=width)...  5.7 us
    pallas_call x1, Pallas kernels, kernel_plan(): pl.pallas_call(functools.partial(finish_kernel, width=width), grid=(steps...  5.19 us
  transfers between devices with their start and end apart: 19, of which 7 were waited for; matrix products, arithmetic and copies ran while one was open for 1% of the time, Pallas kernels for 29%

profile of v3, /device:TPU:0, one launch (start us, length us, event | category | flops | bytes accessed | tf_op | source)
XLA Modules:
  0.0 105.1 jit_solution(855983242681018459)
XLA Ops:
  0.6 0.9 slice.6
  1.5 2.4 %collective-permute-start = (bf16[2,4096]{1,0:T(2,128)(2,1)S(1)}, bf16[2,4096]{1,0:T(2,128)(2,1)S(1)}, u32[]{:S(2)}, u32[]{:S(2)}) collective-permute-start(bf16[2,4096]{1,0:T(2,128)(2,1)S(1)} %slice.6), channel_id=1, source_target_pairs={{0,1},{1,2},{2,3},{3,4},{4,5},{5,6},{6,7},{7,8},{8,9},{9,10},{10,1... | collective-permute-start | bytes 49160 | tf_op jit(solution)/shard_map/ppermute | solution.py:18
  3.9 2.5 %gate.1.gated_ref = bf16[16,128,256]{2,1,0:T(8,128)(2,1)} custom-call(bf16[128,4096]{1,0:T(8,128)(2,1)} %grad_ref.3, bf16[128,4096]{1,0:T(8,128)(2,1)} %query_ref.1), custom_call_target="tpu_custom_call" | custom-call | flops 524288 | bytes 3145728 | tf_op jit(solution)/shard_map/gate/pallas_call | solution.py:613
  6.3 7.2 %all-to-all-start = ((bf16[16,128,256]{2,1,0:T(8,128)(2,1)}), bf16[16,128,256]{2,1,0:T(8,128)(2,1)}, u32[]{:S(2)}, u32[]{:S(2)}) async-start(bf16[16,128,256]{2,1,0:T(8,128)(2,1)} %gate.1.gated_ref), calls=%async_computation | async-start | bytes 2097152 | tf_op jit(solution)/shard_map/all_to_all | solution.py:555
  13.6 0.0 collective-permute-done.edge_ref
  13.6 0.0 copy-start.3
  13.6 0.6 copy-done.3
  14.2 4.1 %mix.1 = (bf16[4,128,256]{2,1,0:T(8,128)(2,1)}, bf16[4,128,256]{2,1,0:T(8,128)(2,1)}, bf16[4,128,256]{2,1,0:T(8,128)(2,1)}, bf16[128,256]{1,0:T(8,128)(2,1)}, bf...) custom-call(bf16[128,4096]{1,0:T(8,128)(2,1)} %key_ref.3, ...), custom_call_target="tpu_custom_call" | custom-call | flops 40000000000 | bytes 6291456 | tf_op jit(solution)/shard_map/mix/pallas_call | solution.py:639
  18.3 0.4 collective-permute-start.1
  18.7 1.7 %collective-permute-start.2 = (bf16[4,128,256]{2,1,0:T(8,128)(2,1)}, bf16[4,128,256]{2,1,0:T(8,128)(2,1)S(1)}, u32[]{:S(2)}, u32[]{:S(2)}) collective-permute-start(bf16[4,128,256]{2,1,0:T(8,128)(2,1)} %get-tuple-element.44), channel_id=1, source_target_pairs={{0,2},{1,3},{2,0},{3,1},{4,6},{5,7},{6,4},{7,5},{8,10},{9,11},{10,... | collective-permute-start | bytes 786440 | tf_op jit(solution)/shard_map/ppermute | solution.py:559
  20.4 0.0 collective-permute-start.3
  20.4 1.7 %collective-permute-start.4 = (bf16[128,256]{1,0:T(8,128)(2,1)}, bf16[128,256]{1,0:T(8,128)(2,1)S(1)}, u32[]{:S(2)}, u32[]{:S(2)}) collective-permute-start(bf16[128,256]{1,0:T(8,128)(2,1)} %get-tuple-element.53), channel_id=1, source_target_pairs={{0,4},{1,5},{2,6},{3,7},{4,0},{5,1},{6,2},{7,3},{8,12},{9,13},{10,... | collective-permute-start | bytes 196616 | tf_op jit(solution)/shard_map/ppermute | solution.py:559
  22.1 2.4 %collective-permute-start.5 = (bf16[128,256]{1,0:T(8,128)(2,1)}, bf16[128,256]{1,0:T(8,128)(2,1)S(1)}, u32[]{:S(2)}, u32[]{:S(2)}) collective-permute-start(bf16[128,256]{1,0:T(8,128)(2,1)} %get-tuple-element.54), channel_id=1, source_target_pairs={{0,8},{1,9},{2,10},{3,11},{4,12},{5,13},{6,14},{7,15},{8,0},{9,1},... | collective-permute-start | bytes 196616 | tf_op jit(solution)/shard_map/ppermute | solution.py:559
  24.4 5.7 %filter_spectrum.1.filter_hbm = bf16[17,256,256]{2,1,0:T(8,128)(2,1)} custom-call(bf16[256,2048]{1,0:T(8,128)(2,1)} %taps_ref, bf16[17,256,256]{2,1,0:T(8,128)(2,1)} %constant.36.clone.ahead_ref.ahead_hbm.refs_12_), custom_call_target="tpu_custom_call" | custom-call | flops 40000000000 | bytes 5505024 | tf_op jit(solution)/shard_map/filter_spectrum/pallas_call | solution.py:667
  30.2 0.0 collective-permute-done.1.refs_0_.refs_4_
  30.2 0.0 copy-done.10
  30.2 0.4 collective-permute-start.6
  30.6 1.7 %collective-permute-done.2.refs_1_.refs_5_ = bf16[4,128,256]{2,1,0:T(8,128)(2,1)S(1)} collective-permute-done((bf16[4,128,256]{2,1,0:T(8,128)(2,1)}, bf16[4,128,256]{2,1,0:T(8,128)(2,1)S(1)}, u32[]{:S(2)}, u32[]{:S(2)}) %collective-permute-start.2) | collective-permute-done | bytes 262176 | tf_op jit(solution)/shard_map/ppermute | solution.py:559
  32.3 6.4 %collective-permute-done.3.refs_2_.refs_6_ = bf16[4,128,256]{2,1,0:T(8,128)(2,1)S(1)} collective-permute-done((bf16[4,128,256]{2,1,0:T(8,128)(2,1)}, bf16[4,128,256]{2,1,0:T(8,128)(2,1)S(1)}, u32[]{:S(2)}, u32[]{:S(2)}) %collective-permute-start.3) | collective-permute-done | bytes 262176 | tf_op jit(solution)/shard_map/ppermute | solution.py:559
  38.7 0.0 copy-done
  38.7 0.0 copy-done.1
  38.7 0.7 copy-done.2
  39.4 1.9 %regroup.1 = (bf16[3,128,256]{2,1,0:T(8,128)(2,1)}, bf16[3,128,256]{2,1,0:T(8,128)(2,1)}, bf16[3,128,256]{2,1,0:T(8,128)(2,1)}) custom-call(bf16[4,128,256]{2,1,0:T(8,128)(2,1)} %copy-done, bf16[4,128,256]{2,1,0:T(8,128)(2,1)} %copy-done.1, bf16[4,128,256]{2,1,0:T(8,128)(2,1)} %copy-done.2), custom_call_target="tpu_custom_call" | custom-call | bytes 2097152 | tf_op jit(solution)/shard_map/regroup/pallas_call | solution.py:656
  41.3 0.0 all-to-all-done
  41.3 1.3 %collective-permute-start.7 = (bf16[3,128,256]{2,1,0:T(8,128)(2,1)}, bf16[3,128,256]{2,1,0:T(8,128)(2,1)S(1)}, u32[]{:S(2)}, u32[]{:S(2)}) collective-permute-start(bf16[3,128,256]{2,1,0:T(8,128)(2,1)} %get-tuple-element.56), channel_id=1, source_target_pairs={{0,4},{1,5},{2,6},{3,7},{4,0},{5,1},{6,2},{7,3},{8,12},{9,13},{10,... | collective-permute-start | bytes 589832 | tf_op jit(solution)/shard_map/ppermute | solution.py:559
  42.6 2.3 %collective-permute-start.8 = (bf16[3,128,256]{2,1,0:T(8,128)(2,1)}, bf16[3,128,256]{2,1,0:T(8,128)(2,1)S(1)}, u32[]{:S(2)}, u32[]{:S(2)}) collective-permute-start(bf16[3,128,256]{2,1,0:T(8,128)(2,1)} %get-tuple-element.57), channel_id=1, source_target_pairs={{0,8},{1,9},{2,10},{3,11},{4,12},{5,13},{6,14},{7,15},{8,0},{9,1},... | collective-permute-start | bytes 589832 | tf_op jit(solution)/shard_map/ppermute | solution.py:559
  44.9 0.0 collective-permute-done.4.refs_1_
  45.0 1.5 %collective-permute-start.9 = (bf16[3,128,256]{2,1,0:T(8,128)(2,1)}, bf16[3,128,256]{2,1,0:T(8,128)(2,1)S(1)}, u32[]{:S(2)}, u32[]{:S(2)}) collective-permute-start(bf16[3,128,256]{2,1,0:T(8,128)(2,1)} %get-tuple-element.58), channel_id=1, source_target_pairs={{0,12},{1,13},{2,14},{3,15},{4,8},{5,9},{6,10},{7,11},{8,4},{9,5},... | collective-permute-start | bytes 589832 | tf_op jit(solution)/shard_map/ppermute | solution.py:559
  46.5 6.9 %conv_back.1 = (bf16[2048,256]{1,0:T(8,128)(2,1)}, bf16[17,256,256]{2,1,0:T(8,128)(2,1)}) custom-call(bf16[2048,256]{1,0:T(8,128)(2,1)} %bitcast.gated_hbm.refs_10_, bf16[17,256,256]{2,1,0:T(8,128)(2,1)} %filter_spectrum.1.filter_hbm, bf16[17,256,256]{2,1,0:T(8,128)(2,1)} %constant.36.clone.ahead_ref.ahead_hbm.refs_12_, ...), custom_call_target="tpu_custom_call" | custom-call | flops 40000000000 | bytes 11010048 | tf_op jit(solution)/shard_map/conv_back/pallas_call | solution.py:680
  53.4 0.0 copy-done.8
  53.4 4.4 %all-to-all-start.1 = ((bf16[16,128,256]{2,1,0:T(8,128)(2,1)}), bf16[16,128,256]{2,1,0:T(8,128)(2,1)}, u32[]{:S(2)}, u32[]{:S(2)}) async-start(bf16[16,128,256]{2,1,0:T(8,128)(2,1)} %bitcast.12), calls=%async_computation.1 | async-start | bytes 2097152 | tf_op jit(solution)/shard_map/all_to_all | solution.py:555
  57.8 0.0 collective-permute-done.5.refs_2_
  57.8 0.0 copy-start.9
  57.8 0.0 collective-permute-done.6.refs_3_
  57.8 0.0 collective-permute-done.7.refs_7_
  57.8 0.0 copy-start.5
  57.8 2.1 %collective-permute-done.8.refs_8_ = bf16[3,128,256]{2,1,0:T(8,128)(2,1)S(1)} collective-permute-done((bf16[3,128,256]{2,1,0:T(8,128)(2,1)}, bf16[3,128,256]{2,1,0:T(8,128)(2,1)S(1)}, u32[]{:S(2)}, u32[]{:S(2)}) %collective-permute-start.8) | collective-permute-done | bytes 196640 | tf_op jit(solution)/shard_map/ppermute | solution.py:559
  59.9 0.0 collective-permute-done.9.refs_9_
  59.9 0.0 copy-done.9
  59.9 0.0 copy-done.5
  59.9 0.6 copy-done.6
  60.6 0.1 copy-done.7
  60.6 7.6 %filter_grad.1 = (bf16[256,2048]{1,0:T(8,128)(2,1)}, f32[1,256]{1,0:T(1,128)}) custom-call(bf16[128,256]{1,0:T(8,128)(2,1)} %get-tuple-element.52.refs_0_, bf16[128,256]{1,0:T(8,128)(2,1)} %copy-done.8, bf16[128,256]{1,0:T(8,128)(2,1)} %copy-done.9, bf16[128,256]{1,0:T(8,128)(2,1)} %collective-permute-done.6.refs_3_, bf16[4,128,256]{2,1,0:T(8,128)(2,1)} %copy-done, ...), custom_call_target="tpu_custom_call" | custom-call | flops 99999997952 | bytes 6684672 | tf_op jit(solution)/shard_map/filter_grad/pallas_call | solution.py:695
  68.2 14.8 %all-to-all-done.1.back_ref = bf16[16,128,256]{2,1,0:T(8,128)(2,1)} async-done(((bf16[16,128,256]{2,1,0:T(8,128)(2,1)}), bf16[16,128,256]{2,1,0:T(8,128)(2,1)}, u32[]{:S(2)}, u32[]{:S(2)}) %all-to-all-start.1) | async-done | bytes 1048608 | tf_op jit(solution)/shard_map/all_to_all | solution.py:555
  83.1 5.2 %finish.1 = (bf16[128,4096]{1,0:T(8,128)(2,1)}, bf16[128,4096]{1,0:T(8,128)(2,1)}, bf16[2,4096]{1,0:T(2,128)(2,1)}, bf16[16,4096]{1,0:T(8,128)(2,1)}, f32[4,8,25...) custom-call(bf16[16,128,256]{2,1,0:T(8,128)(2,1)} %all-to-all-done.1.back_ref, ...), custom_call_target="tpu_custom_call" | custom-call | flops 15728640 | bytes 6291456 | tf_op jit(solution)/shard_map/finish/pallas_call | solution.py:716
  88.3 2.8 %collective-permute-start.12 = (f32[4,8,256]{2,1,0:T(8,128)}, f32[4,8,256]{2,1,0:T(8,128)S(1)}, u32[]{:S(2)}, u32[]{:S(2)}) collective-permute-start(f32[4,8,256]{2,1,0:T(8,128)} %get-tuple-element.68), channel_id=1, source_target_pairs={{0,12},{1,13},{2,14},{3,15},{4,8},{5,9},{6,10},{7,11},{8,4},{9,5},... | collective-permute-start | bytes 98312 | tf_op jit(solution)/shard_map/ppermute | solution.py:559
  91.1 2.7 %collective-permute-start.11 = (f32[4,8,256]{2,1,0:T(8,128)}, f32[4,8,256]{2,1,0:T(8,128)S(1)}, u32[]{:S(2)}, u32[]{:S(2)}) collective-permute-start(f32[4,8,256]{2,1,0:T(8,128)} %get-tuple-element.67), channel_id=1, source_target_pairs={{0,8},{1,9},{2,10},{3,11},{4,12},{5,13},{6,14},{7,15},{8,0},{9,1},... | collective-permute-start | bytes 98312 | tf_op jit(solution)/shard_map/ppermute | solution.py:559
  93.7 0.5 collective-permute-start.10
  94.2 1.3 %collective-permute-start.13 = (bf16[2,4096]{1,0:T(2,128)(2,1)}, bf16[2,4096]{1,0:T(2,128)(2,1)S(1)}, u32[]{:S(2)}, u32[]{:S(2)}) collective-permute-start(bf16[2,4096]{1,0:T(2,128)(2,1)} %get-tuple-element.69), channel_id=1, source_target_pairs={{1,0},{2,1},{3,2},{4,3},{5,4},{6,5},{7,6},{8,7},{9,8},{10,9},{11,1... | collective-permute-start | bytes 49160 | tf_op jit(solution)/shard_map/ppermute | solution.py:18
  95.5 0.0 collective-permute-done.12
  95.5 0.6 collective-permute-done.11
  96.1 1.7 %collective-permute-done.10 = f32[4,8,256]{2,1,0:T(8,128)S(1)} collective-permute-done((f32[4,8,256]{2,1,0:T(8,128)}, f32[4,8,256]{2,1,0:T(8,128)S(1)}, u32[]{:S(2)}, u32[]{:S(2)}) %collective-permute-start.10) | collective-permute-done | bytes 32800 | tf_op jit(solution)/shard_map/ppermute | solution.py:559
  97.9 0.8 add_add_fusion
  98.6 0.0 collective-permute-done.13.head_ref
  98.6 0.0 copy-start.4
  98.7 2.2 %collective-permute-start.16 = (f32[8,256]{1,0:T(8,128)S(1)}, f32[8,256]{1,0:T(8,128)S(1)}, u32[]{:S(2)}, u32[]{:S(2)}) collective-permute-start(f32[8,256]{1,0:T(8,128)S(1)} %get-tuple-element.77), channel_id=1, source_target_pairs={{0,3},{1,2},{2,1},{3,0},{4,7},{5,6},{6,5},{7,4},{8,11},{9,10},{10,... | collective-permute-start | bytes 24584 | tf_op jit(solution)/shard_map/ppermute | solution.py:559
  100.9 0.0 collective-permute-start.15
  100.9 0.2 collective-permute-start.14
  101.1 0.0 copy-done.4
  101.1 1.7 %seam.1 = bf16[128,4096]{1,0:T(8,128)(2,1)} custom-call(bf16[16,4096]{1,0:T(8,128)(2,1)} %get-tuple-element.64.tail_ref, bf16[2,4096]{1,0:T(2,128)(2,1)} %copy-done.4, f32[3,4096]{1,0:T(4,128)} %short_ref.5, bf16[128,4096]{1,0:T(8,128)(2,1)} %get-tuple-element.72.done_ref), custom_call_target="tpu_custom_call", output_to_operand_aliasing={{}: (3, {})} | custom-call | flops 327680 | bytes 393216 | tf_op jit(solution)/shard_map/seam/pallas_call | solution.py:733
  102.8 0.0 collective-permute-done.16
  102.8 1.7 %collective-permute-done.15 = f32[8,256]{1,0:T(8,128)S(1)} collective-permute-done((f32[8,256]{1,0:T(8,128)S(1)}, f32[8,256]{1,0:T(8,128)S(1)}, u32[]{:S(2)}, u32[]{:S(2)}) %collective-permute-start.15) | collective-permute-done | bytes 8224 | tf_op jit(solution)/shard_map/ppermute | solution.py:559
  104.5 0.0 collective-permute-done.14
  104.5 0.6 slice_add_fusion
  (8 shorter events, 0.0 us)
Async XLA Ops:
  1.5 12.1 %collective-permute-start = (bf16[2,4096]{1,0:T(2,128)(2,1)S(1)}, bf16[2,4096]{1,0:T(2,128)(2,1)S(1)}, u32[]{:S(2)}, u32[]{:S(2)}) collective-permute-start(bf16[2,4096]{1,0:T(2,128)(2,1)S(1)} %slice.6), channel_id=1, source_target_pairs={{0,1},{1,2},{2,3},{3,4},{4,5},{5,6},{6,7},{7,8},{8,9},{9,10},{10,1... | collective-permute-start | bytes 49160 | tf_op jit(solution)/shard_map/ppermute | solution.py:18
  6.3 35.0 %all-to-all-start = ((bf16[16,128,256]{2,1,0:T(8,128)(2,1)}), bf16[16,128,256]{2,1,0:T(8,128)(2,1)}, u32[]{:S(2)}, u32[]{:S(2)}) async-start(bf16[16,128,256]{2,1,0:T(8,128)(2,1)} %gate.1.gated_ref), calls=%async_computation | async-start | bytes 2097152 | tf_op jit(solution)/shard_map/all_to_all | solution.py:555
  13.6 0.6 copy-start.3
  18.3 11.9 %collective-permute-start.1 = (bf16[4,128,256]{2,1,0:T(8,128)(2,1)}, bf16[4,128,256]{2,1,0:T(8,128)(2,1)S(1)}, u32[]{:S(2)}, u32[]{:S(2)}) collective-permute-start(bf16[4,128,256]{2,1,0:T(8,128)(2,1)} %get-tuple-element.43), channel_id=1, source_target_pairs={{0,1},{1,0},{2,3},{3,2},{4,5},{5,4},{6,7},{7,6},{8,9},{9,8},{10,11... | collective-permute-start | bytes 786440 | tf_op jit(solution)/shard_map/ppermute | solution.py:559
  18.7 13.6 %collective-permute-start.2 = (bf16[4,128,256]{2,1,0:T(8,128)(2,1)}, bf16[4,128,256]{2,1,0:T(8,128)(2,1)S(1)}, u32[]{:S(2)}, u32[]{:S(2)}) collective-permute-start(bf16[4,128,256]{2,1,0:T(8,128)(2,1)} %get-tuple-element.44), channel_id=1, source_target_pairs={{0,2},{1,3},{2,0},{3,1},{4,6},{5,7},{6,4},{7,5},{8,10},{9,11},{10,... | collective-permute-start | bytes 786440 | tf_op jit(solution)/shard_map/ppermute | solution.py:559
  20.4 18.3 %collective-permute-start.3 = (bf16[4,128,256]{2,1,0:T(8,128)(2,1)}, bf16[4,128,256]{2,1,0:T(8,128)(2,1)S(1)}, u32[]{:S(2)}, u32[]{:S(2)}) collective-permute-start(bf16[4,128,256]{2,1,0:T(8,128)(2,1)} %get-tuple-element.45), channel_id=1, source_target_pairs={{0,3},{1,2},{2,1},{3,0},{4,7},{5,6},{6,5},{7,4},{8,11},{9,10},{10,... | collective-permute-start | bytes 786440 | tf_op jit(solution)/shard_map/ppermute | solution.py:559
  20.4 24.6 %collective-permute-start.4 = (bf16[128,256]{1,0:T(8,128)(2,1)}, bf16[128,256]{1,0:T(8,128)(2,1)S(1)}, u32[]{:S(2)}, u32[]{:S(2)}) collective-permute-start(bf16[128,256]{1,0:T(8,128)(2,1)} %get-tuple-element.53), channel_id=1, source_target_pairs={{0,4},{1,5},{2,6},{3,7},{4,0},{5,1},{6,2},{7,3},{8,12},{9,13},{10,... | collective-permute-start | bytes 196616 | tf_op jit(solution)/shard_map/ppermute | solution.py:559
  22.1 8.1 %copy-start.10 = (bf16[128,256]{1,0:T(8,128)(2,1)S(1)}, bf16[128,256]{1,0:T(8,128)(2,1)}, u32[]{:S(2)}) copy-start(bf16[128,256]{1,0:T(8,128)(2,1)} %get-tuple-element.55) | copy-start | bytes 196612
  22.1 35.7 %collective-permute-start.5 = (bf16[128,256]{1,0:T(8,128)(2,1)}, bf16[128,256]{1,0:T(8,128)(2,1)S(1)}, u32[]{:S(2)}, u32[]{:S(2)}) collective-permute-start(bf16[128,256]{1,0:T(8,128)(2,1)} %get-tuple-element.54), channel_id=1, source_target_pairs={{0,8},{1,9},{2,10},{3,11},{4,12},{5,13},{6,14},{7,15},{8,0},{9,1},... | collective-permute-start | bytes 196616 | tf_op jit(solution)/shard_map/ppermute | solution.py:559
  30.2 8.5 %copy-start = (bf16[4,128,256]{2,1,0:T(8,128)(2,1)}, bf16[4,128,256]{2,1,0:T(8,128)(2,1)S(1)}, u32[]{:S(2)}) copy-start(bf16[4,128,256]{2,1,0:T(8,128)(2,1)S(1)} %collective-permute-done.1.refs_0_.refs_4_) | copy-start | bytes 786436
  30.2 27.6 %collective-permute-start.6 = (bf16[128,256]{1,0:T(8,128)(2,1)S(1)}, bf16[128,256]{1,0:T(8,128)(2,1)}, u32[]{:S(2)}, u32[]{:S(2)}) collective-permute-start(bf16[128,256]{1,0:T(8,128)(2,1)S(1)} %copy-done.10), channel_id=1, source_target_pairs={{0,12},{1,13},{2,14},{3,15},{4,8},{5,9},{6,10},{7,11},{8,4},{9,5},... | collective-permute-start | bytes 196616 | tf_op jit(solution)/shard_map/ppermute | solution.py:559
  32.3 6.4 %copy-start.1 = (bf16[4,128,256]{2,1,0:T(8,128)(2,1)}, bf16[4,128,256]{2,1,0:T(8,128)(2,1)S(1)}, u32[]{:S(2)}) copy-start(bf16[4,128,256]{2,1,0:T(8,128)(2,1)S(1)} %collective-permute-done.2.refs_1_.refs_5_) | copy-start | bytes 786436
  38.7 0.7 copy-start.2
  41.3 16.5 %collective-permute-start.7 = (bf16[3,128,256]{2,1,0:T(8,128)(2,1)}, bf16[3,128,256]{2,1,0:T(8,128)(2,1)S(1)}, u32[]{:S(2)}, u32[]{:S(2)}) collective-permute-start(bf16[3,128,256]{2,1,0:T(8,128)(2,1)} %get-tuple-element.56), channel_id=1, source_target_pairs={{0,4},{1,5},{2,6},{3,7},{4,0},{5,1},{6,2},{7,3},{8,12},{9,13},{10,... | collective-permute-start | bytes 589832 | tf_op jit(solution)/shard_map/ppermute | solution.py:559
  42.6 17.3 %collective-permute-start.8 = (bf16[3,128,256]{2,1,0:T(8,128)(2,1)}, bf16[3,128,256]{2,1,0:T(8,128)(2,1)S(1)}, u32[]{:S(2)}, u32[]{:S(2)}) collective-permute-start(bf16[3,128,256]{2,1,0:T(8,128)(2,1)} %get-tuple-element.57), channel_id=1, source_target_pairs={{0,8},{1,9},{2,10},{3,11},{4,12},{5,13},{6,14},{7,15},{8,0},{9,1},... | collective-permute-start | bytes 589832 | tf_op jit(solution)/shard_map/ppermute | solution.py:559
  44.9 8.4 %copy-start.8 = (bf16[128,256]{1,0:T(8,128)(2,1)}, bf16[128,256]{1,0:T(8,128)(2,1)S(1)}, u32[]{:S(2)}) copy-start(bf16[128,256]{1,0:T(8,128)(2,1)S(1)} %collective-permute-done.4.refs_1_) | copy-start | bytes 196612
  45.0 14.9 %collective-permute-start.9 = (bf16[3,128,256]{2,1,0:T(8,128)(2,1)}, bf16[3,128,256]{2,1,0:T(8,128)(2,1)S(1)}, u32[]{:S(2)}, u32[]{:S(2)}) collective-permute-start(bf16[3,128,256]{2,1,0:T(8,128)(2,1)} %get-tuple-element.58), channel_id=1, source_target_pairs={{0,12},{1,13},{2,14},{3,15},{4,8},{5,9},{6,10},{7,11},{8,4},{9,5},... | collective-permute-start | bytes 589832 | tf_op jit(solution)/shard_map/ppermute | solution.py:559
  53.4 29.7 %all-to-all-start.1 = ((bf16[16,128,256]{2,1,0:T(8,128)(2,1)}), bf16[16,128,256]{2,1,0:T(8,128)(2,1)}, u32[]{:S(2)}, u32[]{:S(2)}) async-start(bf16[16,128,256]{2,1,0:T(8,128)(2,1)} %bitcast.12), calls=%async_computation.1 | async-start | bytes 2097152 | tf_op jit(solution)/shard_map/all_to_all | solution.py:555
  57.8 2.1 %copy-start.9 = (bf16[128,256]{1,0:T(8,128)(2,1)}, bf16[128,256]{1,0:T(8,128)(2,1)S(1)}, u32[]{:S(2)}) copy-start(bf16[128,256]{1,0:T(8,128)(2,1)S(1)} %collective-permute-done.5.refs_2_) | copy-start | bytes 196612
  57.8 2.1 %copy-start.5 = (bf16[3,128,256]{2,1,0:T(8,128)(2,1)}, bf16[3,128,256]{2,1,0:T(8,128)(2,1)S(1)}, u32[]{:S(2)}) copy-start(bf16[3,128,256]{2,1,0:T(8,128)(2,1)S(1)} %collective-permute-done.7.refs_7_) | copy-start | bytes 589828
  59.9 0.7 copy-start.6
  59.9 0.7 copy-start.7
  88.3 7.2 %collective-permute-start.12 = (f32[4,8,256]{2,1,0:T(8,128)}, f32[4,8,256]{2,1,0:T(8,128)S(1)}, u32[]{:S(2)}, u32[]{:S(2)}) collective-permute-start(f32[4,8,256]{2,1,0:T(8,128)} %get-tuple-element.68), channel_id=1, source_target_pairs={{0,12},{1,13},{2,14},{3,15},{4,8},{5,9},{6,10},{7,11},{8,4},{9,5},... | collective-permute-start | bytes 98312 | tf_op jit(solution)/shard_map/ppermute | solution.py:559
  91.1 5.0 %collective-permute-start.11 = (f32[4,8,256]{2,1,0:T(8,128)}, f32[4,8,256]{2,1,0:T(8,128)S(1)}, u32[]{:S(2)}, u32[]{:S(2)}) collective-permute-start(f32[4,8,256]{2,1,0:T(8,128)} %get-tuple-element.67), channel_id=1, source_target_pairs={{0,8},{1,9},{2,10},{3,11},{4,12},{5,13},{6,14},{7,15},{8,0},{9,1},... | collective-permute-start | bytes 98312 | tf_op jit(solution)/shard_map/ppermute | solution.py:559
  93.7 4.1 %collective-permute-start.10 = (f32[4,8,256]{2,1,0:T(8,128)}, f32[4,8,256]{2,1,0:T(8,128)S(1)}, u32[]{:S(2)}, u32[]{:S(2)}) collective-permute-start(f32[4,8,256]{2,1,0:T(8,128)} %get-tuple-element.66), channel_id=1, source_target_pairs={{0,4},{1,5},{2,6},{3,7},{4,0},{5,1},{6,2},{7,3},{8,12},{9,13},{10,... | collective-permute-start | bytes 98312 | tf_op jit(solution)/shard_map/ppermute | solution.py:559
  94.2 4.4 %collective-permute-start.13 = (bf16[2,4096]{1,0:T(2,128)(2,1)}, bf16[2,4096]{1,0:T(2,128)(2,1)S(1)}, u32[]{:S(2)}, u32[]{:S(2)}) collective-permute-start(bf16[2,4096]{1,0:T(2,128)(2,1)} %get-tuple-element.69), channel_id=1, source_target_pairs={{1,0},{2,1},{3,2},{4,3},{5,4},{6,5},{7,6},{8,7},{9,8},{10,9},{11,1... | collective-permute-start | bytes 49160 | tf_op jit(solution)/shard_map/ppermute | solution.py:18
  98.6 2.4 %copy-start.4 = (bf16[2,4096]{1,0:T(2,128)(2,1)}, bf16[2,4096]{1,0:T(2,128)(2,1)S(1)}, u32[]{:S(2)}) copy-start(bf16[2,4096]{1,0:T(2,128)(2,1)S(1)} %collective-permute-done.13.head_ref) | copy-start | bytes 49156
  98.7 4.1 %collective-permute-start.16 = (f32[8,256]{1,0:T(8,128)S(1)}, f32[8,256]{1,0:T(8,128)S(1)}, u32[]{:S(2)}, u32[]{:S(2)}) collective-permute-start(f32[8,256]{1,0:T(8,128)S(1)} %get-tuple-element.77), channel_id=1, source_target_pairs={{0,3},{1,2},{2,1},{3,0},{4,7},{5,6},{6,5},{7,4},{8,11},{9,10},{10,... | collective-permute-start | bytes 24584 | tf_op jit(solution)/shard_map/ppermute | solution.py:559
  100.9 3.7 %collective-permute-start.15 = (f32[8,256]{1,0:T(8,128)S(1)}, f32[8,256]{1,0:T(8,128)S(1)}, u32[]{:S(2)}, u32[]{:S(2)}) collective-permute-start(f32[8,256]{1,0:T(8,128)S(1)} %get-tuple-element.78), channel_id=1, source_target_pairs={{0,2},{1,3},{2,0},{3,1},{4,6},{5,7},{6,4},{7,5},{8,10},{9,11},{10,... | collective-permute-start | bytes 24584 | tf_op jit(solution)/shard_map/ppermute | solution.py:559
  100.9 3.7 %collective-permute-start.14 = (f32[8,256]{1,0:T(8,128)S(1)}, f32[8,256]{1,0:T(8,128)S(1)}, u32[]{:S(2)}, u32[]{:S(2)}) collective-permute-start(f32[8,256]{1,0:T(8,128)S(1)} %get-tuple-element.79), channel_id=1, source_target_pairs={{0,1},{1,0},{2,3},{3,2},{4,5},{5,4},{6,7},{7,6},{8,9},{9,8},{10,11... | collective-permute-start | bytes 24584 | tf_op jit(solution)/shard_map/ppermute | solution.py:559

commit v4 on v3

--- a/solution.py
+++ b/solution.py
@@ -445,7 +445,8 @@
     return moved
 
 
-def gate_kernel(grad_ref, query_ref, gated_ref, *, width):
+def gate_kernel(grad_ref, query_ref, value_ref, gated_ref, last_ref, *, width):
+    last_ref[...] = value_ref[value_ref.shape[0] - 2 :]
     for j in range(gated_ref.shape[0]):
         cols = slice(j * width, (j + 1) * width)
         gated_ref[j] = (
@@ -610,16 +611,16 @@
     short_spec = pl.BlockSpec((3, span), lambda i: (0, i))
     skip_spec = pl.BlockSpec((1, span), lambda i: (0, i))
 
-    gated = pl.pallas_call(
+    gated, last = pl.pallas_call(
         functools.partial(gate_kernel, width=width),
         grid=(steps,),
-        in_specs=[flat, flat],
-        out_specs=owned,
-        out_shape=shape((peers, rows, width), bf16),
+        in_specs=[flat, flat, pl.BlockSpec((16, span), lambda i: (rows // 16 - 1, i))],
+        out_specs=[owned, edge_spec],
+        out_shape=[shape((peers, rows, width), bf16), shape((2, channels), bf16)],
         compiler_params=params(),
         cost_estimate=cost(rows * channels, 6 * rows * channels),
         name="gate",
-    )(out_grad, query_feat)
+    )(out_grad, query_feat, value_raw)
 
     gated_got = exchanged(gated.reshape(seq, width))
 
@@ -630,7 +631,7 @@
     table_bytes = 8 * bins * INNER * INNER
     spec_bytes = 4 * bins * INNER * width
     work = 2 * bins * (2 * INNER) ** 2 * width
-    edge = passed_along(value_raw[rows - 2 :], "ctx", 1)
+    edge = passed_along(last, "ctx", 1)
     whole = lambda size: pl.BlockSpec((size, channels), lambda i: (0, 0))
     shift_scratch = pltpu.VMEM((2, rows + 8, 128), f32)
     near_spec = pl.BlockSpec((far, rows, width), lambda i: (0, 0, 0))
@@ -707,7 +708,7 @@
             pltpu.VMEM((seq, width), f32),
             pltpu.SemaphoreType.DMA((peers + 4,)),
         ],
-        compiler_params=params(),
+        compiler_params=params(63),
         cost_estimate=cost(100000000000, 2 * table_bytes + spec_bytes),
         name="filter_grad",
     )(*placed, *near, *across, gated_got, gated_spec, ahead, back)
@@ -723,7 +724,7 @@
         + [shape((2, channels), bf16), shape((16, channels), bf16)]
         + [shape((INNER_PEERS, 8, width), f32)] * far,
         scratch_shapes=[pltpu.VMEM((2, rows + 8, 128), f32)] * 2 + [pltpu.VMEM((peers, 8, width), f32)],
-        compiler_params=params(),
+        compiler_params=params(63),
         cost_estimate=cost(30 * rows * channels, 12 * rows * channels),
         name="finish",
     )(back_got, gated, key_feat, value_raw, edge, short_filter, skip_row)

time: 106 us -> 105 us (level)
  transfers between devices with their start and end apart: 19 -> 19, of which waited for: 7 -> 7; matrix products, arithmetic and copies ran while one was open for 1% -> 1% of each run, Pallas kernels for 29% -> 27%
where the time goes in v4:
time: 105 us; the launch traced here: 104 us
  Pallas kernels  35.6 us (34%)
  starting transfers between devices  35.3 us (34%)
  waiting for transfers between devices  29.1 us (28%)
  local copies, waits for them, and re-layouts  2.06 us (2%)
  other arithmetic  1.37 us (1%)
    ppermute x15, starting transfers between devices, paired(): lax.ppermute(block, 'ctx', [(i, i ^ distance) for i in range(lax.axis_siz...  20.1 us
    all_to_all x2, waiting for transfers between devices, exchanged(): return lax.all_to_all(block, 'ctx', split_axis=0, concat_axis=0, tiled=True)  14.8 us
    ppermute x15, waiting for transfers between devices, paired(): lax.ppermute(block, 'ctx', [(i, i ^ distance) for i in range(lax.axis_siz...  14.3 us
    all_to_all x2, starting transfers between devices, exchanged(): return lax.all_to_all(block, 'ctx', split_axis=0, concat_axis=0, tiled=True)  11.6 us
    pallas_call x1, Pallas kernels, kernel_plan(): pl.pallas_call(functools.partial(grad_kernel, outer=outer, width=width),...  7.59 us
    pallas_call x1, Pallas kernels, kernel_plan(): pl.pallas_call(functools.partial(conv_kernel, outer=outer, width=width),...  6.9 us
    pallas_call x1, Pallas kernels, kernel_plan(): pl.pallas_call(functools.partial(filter_kernel, outer=outer, width=width)...  5.72 us
    pallas_call x1, Pallas kernels, kernel_plan(): pl.pallas_call(functools.partial(finish_kernel, width=width), grid=(steps...  5.2 us
  transfers between devices with their start and end apart: 19, of which 7 were waited for; matrix products, arithmetic and copies ran while one was open for 1% of the time, Pallas kernels for 27%

profile of v4, /device:TPU:0, one launch (start us, length us, event | category | flops | bytes accessed | tf_op | source)
XLA Modules:
  0.0 104.3 jit_solution(10763818217712110676)
XLA Ops:
  0.6 2.5 %gate.1 = (bf16[16,128,256]{2,1,0:T(8,128)(2,1)}, bf16[2,4096]{1,0:T(2,128)(2,1)}) custom-call(bf16[128,4096]{1,0:T(8,128)(2,1)} %grad_ref.3, bf16[128,4096]{1,0:T(8,128)(2,1)} %query_ref.1, bf16[128,4096]{1,0:T(8,128)(2,1)} %value_ref.5), custom_call_target="tpu_custom_call" | custom-call | flops 524288 | bytes 3145728 | tf_op jit(solution)/shard_map/gate/pallas_call | solution.py:614
  3.1 2.3 %collective-permute-start = (bf16[2,4096]{1,0:T(2,128)(2,1)}, bf16[2,4096]{1,0:T(2,128)(2,1)S(1)}, u32[]{:S(2)}, u32[]{:S(2)}) collective-permute-start(bf16[2,4096]{1,0:T(2,128)(2,1)} %get-tuple-element.43), channel_id=1, source_target_pairs={{0,1},{1,2},{2,3},{3,4},{4,5},{5,6},{6,7},{7,8},{8,9},{9,10},{10,1... | collective-permute-start | bytes 49160 | tf_op jit(solution)/shard_map/ppermute | solution.py:18
  5.5 7.3 %all-to-all-start = ((bf16[16,128,256]{2,1,0:T(8,128)(2,1)}), bf16[16,128,256]{2,1,0:T(8,128)(2,1)}, u32[]{:S(2)}, u32[]{:S(2)}) async-start(bf16[16,128,256]{2,1,0:T(8,128)(2,1)} %get-tuple-element.52.gated_ref), calls=%async_computation | async-start | bytes 2097152 | tf_op jit(solution)/shard_map/all_to_all | solution.py:556
  12.7 0.0 collective-permute-done.edge_ref
  12.8 0.0 copy-start.3
  12.8 0.6 copy-done.3
  13.4 4.1 %mix.1 = (bf16[4,128,256]{2,1,0:T(8,128)(2,1)}, bf16[4,128,256]{2,1,0:T(8,128)(2,1)}, bf16[4,128,256]{2,1,0:T(8,128)(2,1)}, bf16[128,256]{1,0:T(8,128)(2,1)}, bf...) custom-call(bf16[128,4096]{1,0:T(8,128)(2,1)} %key_ref.3, ...), custom_call_target="tpu_custom_call" | custom-call | flops 40000000000 | bytes 6291456 | tf_op jit(solution)/shard_map/mix/pallas_call | solution.py:640
  17.4 0.4 collective-permute-start.1
  17.9 1.7 %collective-permute-start.2 = (bf16[4,128,256]{2,1,0:T(8,128)(2,1)}, bf16[4,128,256]{2,1,0:T(8,128)(2,1)S(1)}, u32[]{:S(2)}, u32[]{:S(2)}) collective-permute-start(bf16[4,128,256]{2,1,0:T(8,128)(2,1)} %get-tuple-element.47), channel_id=1, source_target_pairs={{0,2},{1,3},{2,0},{3,1},{4,6},{5,7},{6,4},{7,5},{8,10},{9,11},{10,... | collective-permute-start | bytes 786440 | tf_op jit(solution)/shard_map/ppermute | solution.py:560
  19.5 0.0 collective-permute-start.3
  19.5 1.7 %collective-permute-start.4 = (bf16[128,256]{1,0:T(8,128)(2,1)}, bf16[128,256]{1,0:T(8,128)(2,1)S(1)}, u32[]{:S(2)}, u32[]{:S(2)}) collective-permute-start(bf16[128,256]{1,0:T(8,128)(2,1)} %get-tuple-element.57), channel_id=1, source_target_pairs={{0,4},{1,5},{2,6},{3,7},{4,0},{5,1},{6,2},{7,3},{8,12},{9,13},{10,... | collective-permute-start | bytes 196616 | tf_op jit(solution)/shard_map/ppermute | solution.py:560
  21.2 0.0 copy-start.10
  21.2 2.4 %collective-permute-start.5 = (bf16[128,256]{1,0:T(8,128)(2,1)}, bf16[128,256]{1,0:T(8,128)(2,1)S(1)}, u32[]{:S(2)}, u32[]{:S(2)}) collective-permute-start(bf16[128,256]{1,0:T(8,128)(2,1)} %get-tuple-element.58), channel_id=1, source_target_pairs={{0,8},{1,9},{2,10},{3,11},{4,12},{5,13},{6,14},{7,15},{8,0},{9,1},... | collective-permute-start | bytes 196616 | tf_op jit(solution)/shard_map/ppermute | solution.py:560
  23.6 5.7 %filter_spectrum.1.filter_hbm = bf16[17,256,256]{2,1,0:T(8,128)(2,1)} custom-call(bf16[256,2048]{1,0:T(8,128)(2,1)} %taps_ref, bf16[17,256,256]{2,1,0:T(8,128)(2,1)} %constant.36.clone.ahead_ref.ahead_hbm.refs_12_), custom_call_target="tpu_custom_call" | custom-call | flops 40000000000 | bytes 5505024 | tf_op jit(solution)/shard_map/filter_spectrum/pallas_call | solution.py:668
  29.3 0.0 collective-permute-done.1.refs_0_.refs_4_
  29.3 0.0 copy-done.10
  29.3 0.4 collective-permute-start.6
  29.7 1.7 %collective-permute-done.2.refs_1_.refs_5_ = bf16[4,128,256]{2,1,0:T(8,128)(2,1)S(1)} collective-permute-done((bf16[4,128,256]{2,1,0:T(8,128)(2,1)}, bf16[4,128,256]{2,1,0:T(8,128)(2,1)S(1)}, u32[]{:S(2)}, u32[]{:S(2)}) %collective-permute-start.2) | collective-permute-done | bytes 262176 | tf_op jit(solution)/shard_map/ppermute | solution.py:560
  31.4 6.4 %collective-permute-done.3.refs_2_.refs_6_ = bf16[4,128,256]{2,1,0:T(8,128)(2,1)S(1)} collective-permute-done((bf16[4,128,256]{2,1,0:T(8,128)(2,1)}, bf16[4,128,256]{2,1,0:T(8,128)(2,1)S(1)}, u32[]{:S(2)}, u32[]{:S(2)}) %collective-permute-start.3) | collective-permute-done | bytes 262176 | tf_op jit(solution)/shard_map/ppermute | solution.py:560
  37.8 0.0 copy-done
  37.8 0.0 copy-done.1
  37.8 0.7 copy-done.2
  38.5 1.9 %regroup.1 = (bf16[3,128,256]{2,1,0:T(8,128)(2,1)}, bf16[3,128,256]{2,1,0:T(8,128)(2,1)}, bf16[3,128,256]{2,1,0:T(8,128)(2,1)}) custom-call(bf16[4,128,256]{2,1,0:T(8,128)(2,1)} %copy-done, bf16[4,128,256]{2,1,0:T(8,128)(2,1)} %copy-done.1, bf16[4,128,256]{2,1,0:T(8,128)(2,1)} %copy-done.2), custom_call_target="tpu_custom_call" | custom-call | bytes 2097152 | tf_op jit(solution)/shard_map/regroup/pallas_call | solution.py:657
  40.5 0.0 all-to-all-done
  40.5 1.3 %collective-permute-start.7 = (bf16[3,128,256]{2,1,0:T(8,128)(2,1)}, bf16[3,128,256]{2,1,0:T(8,128)(2,1)S(1)}, u32[]{:S(2)}, u32[]{:S(2)}) collective-permute-start(bf16[3,128,256]{2,1,0:T(8,128)(2,1)} %get-tuple-element.60), channel_id=1, source_target_pairs={{0,4},{1,5},{2,6},{3,7},{4,0},{5,1},{6,2},{7,3},{8,12},{9,13},{10,... | collective-permute-start | bytes 589832 | tf_op jit(solution)/shard_map/ppermute | solution.py:560
  41.8 2.3 %collective-permute-start.8 = (bf16[3,128,256]{2,1,0:T(8,128)(2,1)}, bf16[3,128,256]{2,1,0:T(8,128)(2,1)S(1)}, u32[]{:S(2)}, u32[]{:S(2)}) collective-permute-start(bf16[3,128,256]{2,1,0:T(8,128)(2,1)} %get-tuple-element.61), channel_id=1, source_target_pairs={{0,8},{1,9},{2,10},{3,11},{4,12},{5,13},{6,14},{7,15},{8,0},{9,1},... | collective-permute-start | bytes 589832 | tf_op jit(solution)/shard_map/ppermute | solution.py:560
  44.1 0.0 collective-permute-done.4.refs_1_
  44.1 1.5 %collective-permute-start.9 = (bf16[3,128,256]{2,1,0:T(8,128)(2,1)}, bf16[3,128,256]{2,1,0:T(8,128)(2,1)S(1)}, u32[]{:S(2)}, u32[]{:S(2)}) collective-permute-start(bf16[3,128,256]{2,1,0:T(8,128)(2,1)} %get-tuple-element.62), channel_id=1, source_target_pairs={{0,12},{1,13},{2,14},{3,15},{4,8},{5,9},{6,10},{7,11},{8,4},{9,5},... | collective-permute-start | bytes 589832 | tf_op jit(solution)/shard_map/ppermute | solution.py:560
  45.6 6.9 %conv_back.1 = (bf16[2048,256]{1,0:T(8,128)(2,1)}, bf16[17,256,256]{2,1,0:T(8,128)(2,1)}) custom-call(bf16[2048,256]{1,0:T(8,128)(2,1)} %bitcast.gated_hbm.refs_10_, bf16[17,256,256]{2,1,0:T(8,128)(2,1)} %filter_spectrum.1.filter_hbm, bf16[17,256,256]{2,1,0:T(8,128)(2,1)} %constant.36.clone.ahead_ref.ahead_hbm.refs_12_, ...), custom_call_target="tpu_custom_call" | custom-call | flops 40000000000 | bytes 11010048 | tf_op jit(solution)/shard_map/conv_back/pallas_call | solution.py:681
  52.5 0.0 copy-done.8
  52.5 4.4 %all-to-all-start.1 = ((bf16[16,128,256]{2,1,0:T(8,128)(2,1)}), bf16[16,128,256]{2,1,0:T(8,128)(2,1)}, u32[]{:S(2)}, u32[]{:S(2)}) async-start(bf16[16,128,256]{2,1,0:T(8,128)(2,1)} %bitcast.12), calls=%async_computation.1 | async-start | bytes 2097152 | tf_op jit(solution)/shard_map/all_to_all | solution.py:556
  56.9 0.0 collective-permute-done.5.refs_2_
  56.9 0.0 copy-start.9
  56.9 0.0 collective-permute-done.6.refs_3_
  56.9 0.0 collective-permute-done.7.refs_7_
  56.9 0.0 copy-start.5
  57.0 2.1 %collective-permute-done.8.refs_8_ = bf16[3,128,256]{2,1,0:T(8,128)(2,1)S(1)} collective-permute-done((bf16[3,128,256]{2,1,0:T(8,128)(2,1)}, bf16[3,128,256]{2,1,0:T(8,128)(2,1)S(1)}, u32[]{:S(2)}, u32[]{:S(2)}) %collective-permute-start.8) | collective-permute-done | bytes 196640 | tf_op jit(solution)/shard_map/ppermute | solution.py:560
  59.0 0.0 collective-permute-done.9.refs_9_
  59.0 0.0 copy-done.9
  59.1 0.0 copy-done.5
  59.1 0.6 copy-done.6
  59.7 0.1 copy-done.7
  59.8 7.6 %filter_grad.1 = (bf16[256,2048]{1,0:T(8,128)(2,1)}, f32[1,256]{1,0:T(1,128)}) custom-call(bf16[128,256]{1,0:T(8,128)(2,1)} %get-tuple-element.56.refs_0_, bf16[128,256]{1,0:T(8,128)(2,1)} %copy-done.8, bf16[128,256]{1,0:T(8,128)(2,1)} %copy-done.9, bf16[128,256]{1,0:T(8,128)(2,1)} %collective-permute-done.6.refs_3_, bf16[4,128,256]{2,1,0:T(8,128)(2,1)} %copy-done, ...), custom_call_target="tpu_custom_call" | custom-call | flops 99999997952 | bytes 6684672 | tf_op jit(solution)/shard_map/filter_grad/pallas_call | solution.py:696
  67.4 14.8 %all-to-all-done.1.back_ref = bf16[16,128,256]{2,1,0:T(8,128)(2,1)} async-done(((bf16[16,128,256]{2,1,0:T(8,128)(2,1)}), bf16[16,128,256]{2,1,0:T(8,128)(2,1)}, u32[]{:S(2)}, u32[]{:S(2)}) %all-to-all-start.1) | async-done | bytes 1048608 | tf_op jit(solution)/shard_map/all_to_all | solution.py:556
  82.2 5.2 %finish.1 = (bf16[128,4096]{1,0:T(8,128)(2,1)}, bf16[128,4096]{1,0:T(8,128)(2,1)}, bf16[2,4096]{1,0:T(2,128)(2,1)}, bf16[16,4096]{1,0:T(8,128)(2,1)}, f32[4,8,25...) custom-call(bf16[16,128,256]{2,1,0:T(8,128)(2,1)} %all-to-all-done.1.back_ref, ...), custom_call_target="tpu_custom_call" | custom-call | flops 15728640 | bytes 6291456 | tf_op jit(solution)/shard_map/finish/pallas_call | solution.py:717
  87.4 2.8 %collective-permute-start.12 = (f32[4,8,256]{2,1,0:T(8,128)}, f32[4,8,256]{2,1,0:T(8,128)S(1)}, u32[]{:S(2)}, u32[]{:S(2)}) collective-permute-start(f32[4,8,256]{2,1,0:T(8,128)} %get-tuple-element.72), channel_id=1, source_target_pairs={{0,12},{1,13},{2,14},{3,15},{4,8},{5,9},{6,10},{7,11},{8,4},{9,5},... | collective-permute-start | bytes 98312 | tf_op jit(solution)/shard_map/ppermute | solution.py:560
  90.2 2.7 %collective-permute-start.11 = (f32[4,8,256]{2,1,0:T(8,128)}, f32[4,8,256]{2,1,0:T(8,128)S(1)}, u32[]{:S(2)}, u32[]{:S(2)}) collective-permute-start(f32[4,8,256]{2,1,0:T(8,128)} %get-tuple-element.71), channel_id=1, source_target_pairs={{0,8},{1,9},{2,10},{3,11},{4,12},{5,13},{6,14},{7,15},{8,0},{9,1},... | collective-permute-start | bytes 98312 | tf_op jit(solution)/shard_map/ppermute | solution.py:560
  92.9 0.5 collective-permute-start.10
  93.4 1.3 %collective-permute-start.13 = (bf16[2,4096]{1,0:T(2,128)(2,1)}, bf16[2,4096]{1,0:T(2,128)(2,1)S(1)}, u32[]{:S(2)}, u32[]{:S(2)}) collective-permute-start(bf16[2,4096]{1,0:T(2,128)(2,1)} %get-tuple-element.73), channel_id=1, source_target_pairs={{1,0},{2,1},{3,2},{4,3},{5,4},{6,5},{7,6},{8,7},{9,8},{10,9},{11,1... | collective-permute-start | bytes 49160 | tf_op jit(solution)/shard_map/ppermute | solution.py:18
  94.7 0.0 collective-permute-done.12
  94.7 0.6 collective-permute-done.11
  95.3 1.7 %collective-permute-done.10 = f32[4,8,256]{2,1,0:T(8,128)S(1)} collective-permute-done((f32[4,8,256]{2,1,0:T(8,128)}, f32[4,8,256]{2,1,0:T(8,128)S(1)}, u32[]{:S(2)}, u32[]{:S(2)}) %collective-permute-start.10) | collective-permute-done | bytes 32800 | tf_op jit(solution)/shard_map/ppermute | solution.py:560
  97.0 0.8 add_add_fusion
  97.8 0.0 collective-permute-done.13.head_ref
  97.8 0.0 copy-start.4
  97.8 2.2 %collective-permute-start.16 = (f32[8,256]{1,0:T(8,128)S(1)}, f32[8,256]{1,0:T(8,128)S(1)}, u32[]{:S(2)}, u32[]{:S(2)}) collective-permute-start(f32[8,256]{1,0:T(8,128)S(1)} %get-tuple-element.81), channel_id=1, source_target_pairs={{0,3},{1,2},{2,1},{3,0},{4,7},{5,6},{6,5},{7,4},{8,11},{9,10},{10,... | collective-permute-start | bytes 24584 | tf_op jit(solution)/shard_map/ppermute | solution.py:560
  100.0 0.0 collective-permute-start.15
  100.0 0.2 collective-permute-start.14
  100.2 0.0 copy-done.4
  100.2 1.7 %seam.1 = bf16[128,4096]{1,0:T(8,128)(2,1)} custom-call(bf16[16,4096]{1,0:T(8,128)(2,1)} %get-tuple-element.68.tail_ref, bf16[2,4096]{1,0:T(2,128)(2,1)} %copy-done.4, f32[3,4096]{1,0:T(4,128)} %short_ref.5, bf16[128,4096]{1,0:T(8,128)(2,1)} %get-tuple-element.76.done_ref), custom_call_target="tpu_custom_call", output_to_operand_aliasing={{}: (3, {})} | custom-call | flops 327680 | bytes 393216 | tf_op jit(solution)/shard_map/seam/pallas_call | solution.py:734
  101.9 0.0 collective-permute-done.16
  101.9 1.7 %collective-permute-done.15 = f32[8,256]{1,0:T(8,128)S(1)} collective-permute-done((f32[8,256]{1,0:T(8,128)S(1)}, f32[8,256]{1,0:T(8,128)S(1)}, u32[]{:S(2)}, u32[]{:S(2)}) %collective-permute-start.15) | collective-permute-done | bytes 8224 | tf_op jit(solution)/shard_map/ppermute | solution.py:560
  103.7 0.0 collective-permute-done.14
  103.7 0.6 slice_add_fusion
  (7 shorter events, 0.0 us)
Async XLA Ops:
  3.1 9.6 %collective-permute-start = (bf16[2,4096]{1,0:T(2,128)(2,1)}, bf16[2,4096]{1,0:T(2,128)(2,1)S(1)}, u32[]{:S(2)}, u32[]{:S(2)}) collective-permute-start(bf16[2,4096]{1,0:T(2,128)(2,1)} %get-tuple-element.43), channel_id=1, source_target_pairs={{0,1},{1,2},{2,3},{3,4},{4,5},{5,6},{6,7},{7,8},{8,9},{9,10},{10,1... | collective-permute-start | bytes 49160 | tf_op jit(solution)/shard_map/ppermute | solution.py:18
  5.5 35.0 %all-to-all-start = ((bf16[16,128,256]{2,1,0:T(8,128)(2,1)}), bf16[16,128,256]{2,1,0:T(8,128)(2,1)}, u32[]{:S(2)}, u32[]{:S(2)}) async-start(bf16[16,128,256]{2,1,0:T(8,128)(2,1)} %get-tuple-element.52.gated_ref), calls=%async_computation | async-start | bytes 2097152 | tf_op jit(solution)/shard_map/all_to_all | solution.py:556
  12.8 0.6 copy-start.3
  17.4 11.9 %collective-permute-start.1 = (bf16[4,128,256]{2,1,0:T(8,128)(2,1)}, bf16[4,128,256]{2,1,0:T(8,128)(2,1)S(1)}, u32[]{:S(2)}, u32[]{:S(2)}) collective-permute-start(bf16[4,128,256]{2,1,0:T(8,128)(2,1)} %get-tuple-element.46), channel_id=1, source_target_pairs={{0,1},{1,0},{2,3},{3,2},{4,5},{5,4},{6,7},{7,6},{8,9},{9,8},{10,11... | collective-permute-start | bytes 786440 | tf_op jit(solution)/shard_map/ppermute | solution.py:560
  17.9 13.6 %collective-permute-start.2 = (bf16[4,128,256]{2,1,0:T(8,128)(2,1)}, bf16[4,128,256]{2,1,0:T(8,128)(2,1)S(1)}, u32[]{:S(2)}, u32[]{:S(2)}) collective-permute-start(bf16[4,128,256]{2,1,0:T(8,128)(2,1)} %get-tuple-element.47), channel_id=1, source_target_pairs={{0,2},{1,3},{2,0},{3,1},{4,6},{5,7},{6,4},{7,5},{8,10},{9,11},{10,... | collective-permute-start | bytes 786440 | tf_op jit(solution)/shard_map/ppermute | solution.py:560
  19.5 18.3 %collective-permute-start.3 = (bf16[4,128,256]{2,1,0:T(8,128)(2,1)}, bf16[4,128,256]{2,1,0:T(8,128)(2,1)S(1)}, u32[]{:S(2)}, u32[]{:S(2)}) collective-permute-start(bf16[4,128,256]{2,1,0:T(8,128)(2,1)} %get-tuple-element.48), channel_id=1, source_target_pairs={{0,3},{1,2},{2,1},{3,0},{4,7},{5,6},{6,5},{7,4},{8,11},{9,10},{10,... | collective-permute-start | bytes 786440 | tf_op jit(solution)/shard_map/ppermute | solution.py:560
  19.5 24.6 %collective-permute-start.4 = (bf16[128,256]{1,0:T(8,128)(2,1)}, bf16[128,256]{1,0:T(8,128)(2,1)S(1)}, u32[]{:S(2)}, u32[]{:S(2)}) collective-permute-start(bf16[128,256]{1,0:T(8,128)(2,1)} %get-tuple-element.57), channel_id=1, source_target_pairs={{0,4},{1,5},{2,6},{3,7},{4,0},{5,1},{6,2},{7,3},{8,12},{9,13},{10,... | collective-permute-start | bytes 196616 | tf_op jit(solution)/shard_map/ppermute | solution.py:560
  21.2 8.1 %copy-start.10 = (bf16[128,256]{1,0:T(8,128)(2,1)S(1)}, bf16[128,256]{1,0:T(8,128)(2,1)}, u32[]{:S(2)}) copy-start(bf16[128,256]{1,0:T(8,128)(2,1)} %get-tuple-element.59) | copy-start | bytes 196612
  21.2 35.7 %collective-permute-start.5 = (bf16[128,256]{1,0:T(8,128)(2,1)}, bf16[128,256]{1,0:T(8,128)(2,1)S(1)}, u32[]{:S(2)}, u32[]{:S(2)}) collective-permute-start(bf16[128,256]{1,0:T(8,128)(2,1)} %get-tuple-element.58), channel_id=1, source_target_pairs={{0,8},{1,9},{2,10},{3,11},{4,12},{5,13},{6,14},{7,15},{8,0},{9,1},... | collective-permute-start | bytes 196616 | tf_op jit(solution)/shard_map/ppermute | solution.py:560
  29.3 8.5 %copy-start = (bf16[4,128,256]{2,1,0:T(8,128)(2,1)}, bf16[4,128,256]{2,1,0:T(8,128)(2,1)S(1)}, u32[]{:S(2)}) copy-start(bf16[4,128,256]{2,1,0:T(8,128)(2,1)S(1)} %collective-permute-done.1.refs_0_.refs_4_) | copy-start | bytes 786436
  29.3 27.6 %collective-permute-start.6 = (bf16[128,256]{1,0:T(8,128)(2,1)S(1)}, bf16[128,256]{1,0:T(8,128)(2,1)}, u32[]{:S(2)}, u32[]{:S(2)}) collective-permute-start(bf16[128,256]{1,0:T(8,128)(2,1)S(1)} %copy-done.10), channel_id=1, source_target_pairs={{0,12},{1,13},{2,14},{3,15},{4,8},{5,9},{6,10},{7,11},{8,4},{9,5},... | collective-permute-start | bytes 196616 | tf_op jit(solution)/shard_map/ppermute | solution.py:560
  31.4 6.4 %copy-start.1 = (bf16[4,128,256]{2,1,0:T(8,128)(2,1)}, bf16[4,128,256]{2,1,0:T(8,128)(2,1)S(1)}, u32[]{:S(2)}) copy-start(bf16[4,128,256]{2,1,0:T(8,128)(2,1)S(1)} %collective-permute-done.2.refs_1_.refs_5_) | copy-start | bytes 786436
  37.8 0.7 copy-start.2
  40.5 16.5 %collective-permute-start.7 = (bf16[3,128,256]{2,1,0:T(8,128)(2,1)}, bf16[3,128,256]{2,1,0:T(8,128)(2,1)S(1)}, u32[]{:S(2)}, u32[]{:S(2)}) collective-permute-start(bf16[3,128,256]{2,1,0:T(8,128)(2,1)} %get-tuple-element.60), channel_id=1, source_target_pairs={{0,4},{1,5},{2,6},{3,7},{4,0},{5,1},{6,2},{7,3},{8,12},{9,13},{10,... | collective-permute-start | bytes 589832 | tf_op jit(solution)/shard_map/ppermute | solution.py:560
  41.8 17.3 %collective-permute-start.8 = (bf16[3,128,256]{2,1,0:T(8,128)(2,1)}, bf16[3,128,256]{2,1,0:T(8,128)(2,1)S(1)}, u32[]{:S(2)}, u32[]{:S(2)}) collective-permute-start(bf16[3,128,256]{2,1,0:T(8,128)(2,1)} %get-tuple-element.61), channel_id=1, source_target_pairs={{0,8},{1,9},{2,10},{3,11},{4,12},{5,13},{6,14},{7,15},{8,0},{9,1},... | collective-permute-start | bytes 589832 | tf_op jit(solution)/shard_map/ppermute | solution.py:560
  44.1 8.4 %copy-start.8 = (bf16[128,256]{1,0:T(8,128)(2,1)}, bf16[128,256]{1,0:T(8,128)(2,1)S(1)}, u32[]{:S(2)}) copy-start(bf16[128,256]{1,0:T(8,128)(2,1)S(1)} %collective-permute-done.4.refs_1_) | copy-start | bytes 196612
  44.1 14.9 %collective-permute-start.9 = (bf16[3,128,256]{2,1,0:T(8,128)(2,1)}, bf16[3,128,256]{2,1,0:T(8,128)(2,1)S(1)}, u32[]{:S(2)}, u32[]{:S(2)}) collective-permute-start(bf16[3,128,256]{2,1,0:T(8,128)(2,1)} %get-tuple-element.62), channel_id=1, source_target_pairs={{0,12},{1,13},{2,14},{3,15},{4,8},{5,9},{6,10},{7,11},{8,4},{9,5},... | collective-permute-start | bytes 589832 | tf_op jit(solution)/shard_map/ppermute | solution.py:560
  52.5 29.7 %all-to-all-start.1 = ((bf16[16,128,256]{2,1,0:T(8,128)(2,1)}), bf16[16,128,256]{2,1,0:T(8,128)(2,1)}, u32[]{:S(2)}, u32[]{:S(2)}) async-start(bf16[16,128,256]{2,1,0:T(8,128)(2,1)} %bitcast.12), calls=%async_computation.1 | async-start | bytes 2097152 | tf_op jit(solution)/shard_map/all_to_all | solution.py:556
  56.9 2.1 %copy-start.9 = (bf16[128,256]{1,0:T(8,128)(2,1)}, bf16[128,256]{1,0:T(8,128)(2,1)S(1)}, u32[]{:S(2)}) copy-start(bf16[128,256]{1,0:T(8,128)(2,1)S(1)} %collective-permute-done.5.refs_2_) | copy-start | bytes 196612
  56.9 2.1 %copy-start.5 = (bf16[3,128,256]{2,1,0:T(8,128)(2,1)}, bf16[3,128,256]{2,1,0:T(8,128)(2,1)S(1)}, u32[]{:S(2)}) copy-start(bf16[3,128,256]{2,1,0:T(8,128)(2,1)S(1)} %collective-permute-done.7.refs_7_) | copy-start | bytes 589828
  59.0 0.7 copy-start.6
  59.0 0.7 copy-start.7
  87.4 7.3 %collective-permute-start.12 = (f32[4,8,256]{2,1,0:T(8,128)}, f32[4,8,256]{2,1,0:T(8,128)S(1)}, u32[]{:S(2)}, u32[]{:S(2)}) collective-permute-start(f32[4,8,256]{2,1,0:T(8,128)} %get-tuple-element.72), channel_id=1, source_target_pairs={{0,12},{1,13},{2,14},{3,15},{4,8},{5,9},{6,10},{7,11},{8,4},{9,5},... | collective-permute-start | bytes 98312 | tf_op jit(solution)/shard_map/ppermute | solution.py:560
  90.2 5.0 %collective-permute-start.11 = (f32[4,8,256]{2,1,0:T(8,128)}, f32[4,8,256]{2,1,0:T(8,128)S(1)}, u32[]{:S(2)}, u32[]{:S(2)}) collective-permute-start(f32[4,8,256]{2,1,0:T(8,128)} %get-tuple-element.71), channel_id=1, source_target_pairs={{0,8},{1,9},{2,10},{3,11},{4,12},{5,13},{6,14},{7,15},{8,0},{9,1},... | collective-permute-start | bytes 98312 | tf_op jit(solution)/shard_map/ppermute | solution.py:560
  92.9 4.1 %collective-permute-start.10 = (f32[4,8,256]{2,1,0:T(8,128)}, f32[4,8,256]{2,1,0:T(8,128)S(1)}, u32[]{:S(2)}, u32[]{:S(2)}) collective-permute-start(f32[4,8,256]{2,1,0:T(8,128)} %get-tuple-element.70), channel_id=1, source_target_pairs={{0,4},{1,5},{2,6},{3,7},{4,0},{5,1},{6,2},{7,3},{8,12},{9,13},{10,... | collective-permute-start | bytes 98312 | tf_op jit(solution)/shard_map/ppermute | solution.py:560
  93.4 4.4 %collective-permute-start.13 = (bf16[2,4096]{1,0:T(2,128)(2,1)}, bf16[2,4096]{1,0:T(2,128)(2,1)S(1)}, u32[]{:S(2)}, u32[]{:S(2)}) collective-permute-start(bf16[2,4096]{1,0:T(2,128)(2,1)} %get-tuple-element.73), channel_id=1, source_target_pairs={{1,0},{2,1},{3,2},{4,3},{5,4},{6,5},{7,6},{8,7},{9,8},{10,9},{11,1... | collective-permute-start | bytes 49160 | tf_op jit(solution)/shard_map/ppermute | solution.py:18
  97.8 2.4 %copy-start.4 = (bf16[2,4096]{1,0:T(2,128)(2,1)}, bf16[2,4096]{1,0:T(2,128)(2,1)S(1)}, u32[]{:S(2)}) copy-start(bf16[2,4096]{1,0:T(2,128)(2,1)S(1)} %collective-permute-done.13.head_ref) | copy-start | bytes 49156
  97.8 4.1 %collective-permute-start.16 = (f32[8,256]{1,0:T(8,128)S(1)}, f32[8,256]{1,0:T(8,128)S(1)}, u32[]{:S(2)}, u32[]{:S(2)}) collective-permute-start(f32[8,256]{1,0:T(8,128)S(1)} %get-tuple-element.81), channel_id=1, source_target_pairs={{0,3},{1,2},{2,1},{3,0},{4,7},{5,6},{6,5},{7,4},{8,11},{9,10},{10,... | collective-permute-start | bytes 24584 | tf_op jit(solution)/shard_map/ppermute | solution.py:560
  100.0 3.7 %collective-permute-start.15 = (f32[8,256]{1,0:T(8,128)S(1)}, f32[8,256]{1,0:T(8,128)S(1)}, u32[]{:S(2)}, u32[]{:S(2)}) collective-permute-start(f32[8,256]{1,0:T(8,128)S(1)} %get-tuple-element.82), channel_id=1, source_target_pairs={{0,2},{1,3},{2,0},{3,1},{4,6},{5,7},{6,4},{7,5},{8,10},{9,11},{10,... | collective-permute-start | bytes 24584 | tf_op jit(solution)/shard_map/ppermute | solution.py:560
  100.0 3.7 %collective-permute-start.14 = (f32[8,256]{1,0:T(8,128)S(1)}, f32[8,256]{1,0:T(8,128)S(1)}, u32[]{:S(2)}, u32[]{:S(2)}) collective-permute-start(f32[8,256]{1,0:T(8,128)S(1)} %get-tuple-element.83), channel_id=1, source_target_pairs={{0,1},{1,0},{2,3},{3,2},{4,5},{5,4},{6,7},{7,6},{8,9},{9,8},{10,11... | collective-permute-start | bytes 24584 | tf_op jit(solution)/shard_map/ppermute | solution.py:560

commit v5 on v4

--- a/solution.py
+++ b/solution.py
@@ -446,7 +446,7 @@
 
 
 def gate_kernel(grad_ref, query_ref, value_ref, gated_ref, last_ref, *, width):
-    last_ref[...] = value_ref[value_ref.shape[0] - 2 :]
+    last_ref[...] = value_ref[...].astype(jnp.float32)[value_ref.shape[0] - 2 :]
     for j in range(gated_ref.shape[0]):
         cols = slice(j * width, (j + 1) * width)
         gated_ref[j] = (
@@ -465,7 +465,7 @@
             slot = (j * width + lane) // 128 % 2
             cols = slice(j * width + lane, j * width + lane + 128)
             value = value_ref[:, cols].astype(jnp.float32)
-            behind[slot, 6:8] = edge_ref[:, cols].astype(jnp.float32)
+            behind[slot, 6:8] = edge_ref[:, cols]
             behind[slot, 8 : 8 + rows] = value
             conv = (
                 short_ref[0:1, cols] * value
@@ -505,7 +505,7 @@
             lanes = slice(lane, lane + 128)
             short = [short_ref[i : i + 1, cols] for i in range(3)]
             value = value_ref[:, cols].astype(jnp.float32)
-            behind[slot, 6:8] = edge_ref[:, cols].astype(jnp.float32)
+            behind[slot, 6:8] = edge_ref[:, cols]
             behind[slot, 8 : 8 + rows] = value
             value_1 = behind[slot, 7 : 7 + rows]
             value_2 = behind[slot, 6 : 6 + rows]
@@ -515,9 +515,9 @@
             conv = short[0] * value + short[1] * value_1 + short[2] * value_2
             key_grad_ref[:, cols] = (mixed_grad * conv).astype(jnp.bfloat16)
             feature = (mixed_grad * key_ref[:, cols].astype(jnp.float32)).astype(jnp.bfloat16)
-            head_ref[:, cols] = feature[:2]
             tail_ref[:, cols] = feature[rows - 16 :]
             feature = feature.astype(jnp.float32)
+            head_ref[:, cols] = feature[:2]
             ahead[slot, 0:rows] = feature
             ahead[slot, rows : rows + 8] = jnp.zeros((8, 128), jnp.float32)
             value_grad_ref[:, cols] = (
@@ -544,7 +544,7 @@
 
 def seam_kernel(tail_ref, head_ref, short_ref, done_ref, value_grad_ref):
     feature = tail_ref[...].astype(jnp.float32)
-    head = head_ref[...].astype(jnp.float32)
+    head = head_ref[...]
     value_grad_ref[...] = (
         short_ref[0:1] * feature
         + short_ref[1:2] * shifted_up(feature, 1, head)
@@ -578,6 +578,10 @@
 
 def params(mib=63):
     return pltpu.CompilerParams(vmem_limit_bytes=mib * 1024 * 1024)
+
+
+BESIDE_EXCHANGE = 40_000_000_000
+WHOLE_EXCHANGE = 100_000_000_000
 
 
 def cost(flops, size):
@@ -616,7 +620,7 @@
         grid=(steps,),
         in_specs=[flat, flat, pl.BlockSpec((16, span), lambda i: (rows // 16 - 1, i))],
         out_specs=[owned, edge_spec],
-        out_shape=[shape((peers, rows, width), bf16), shape((2, channels), bf16)],
+        out_shape=[shape((peers, rows, width), bf16), shape((2, channels), f32)],
         compiler_params=params(),
         cost_estimate=cost(rows * channels, 6 * rows * channels),
         name="gate",
@@ -647,12 +651,11 @@
         + [shape((rows, channels), bf16)],
         scratch_shapes=[shift_scratch, pltpu.VMEM((peers, rows, width), bf16)],
         compiler_params=params(),
-        cost_estimate=cost(40000000000, 12 * rows * channels),
+        cost_estimate=cost(BESIDE_EXCHANGE, 12 * rows * channels),
         name="mix",
     )(key_feat, value_raw, edge, short_filter, out_grad, conv_out)
     near = [paired(mixed[e - 1], e) for e in range(1, INNER_PEERS)]
     placed = mixed[INNER_PEERS - 1 :]
-
     placed = [placed[0]] + [paired(placed[d], d * INNER_PEERS) for d in range(1, far)]
     across = pl.pallas_call(
         regroup_kernel,
@@ -670,7 +673,7 @@
         out_shape=spec_shape,
         scratch_shapes=[pltpu.VMEM((seq, width), f32), z_scratch],
         compiler_params=params(),
-        cost_estimate=cost(40000000000, table_bytes + spec_bytes + 2 * seq * width),
+        cost_estimate=cost(BESIDE_EXCHANGE, table_bytes + spec_bytes + 2 * seq * width),
         name="filter_spectrum",
     )(filter_taps, ahead)
 
@@ -686,12 +689,11 @@
         scratch_shapes=[pltpu.VMEM((seq, width), bf16), z_scratch, table_scratch, table_scratch, z_scratch]
         + [z_scratch, u_scratch, pltpu.SemaphoreType.DMA((5,))],
         compiler_params=params(),
-        cost_estimate=cost(40000000000, 2 * table_bytes + 2 * spec_bytes + 4 * seq * width),
+        cost_estimate=cost(BESIDE_EXCHANGE, 2 * table_bytes + 2 * spec_bytes + 4 * seq * width),
         name="conv_back",
     )(gated_got, filter_spec, ahead, back)
 
     back_got = exchanged(conv_back).reshape(peers, rows, width)
-
 
     filter_grad, skip_grad = pl.pallas_call(
         functools.partial(grad_kernel, outer=outer, width=width),
@@ -708,8 +710,8 @@
             pltpu.VMEM((seq, width), f32),
             pltpu.SemaphoreType.DMA((peers + 4,)),
         ],
-        compiler_params=params(63),
-        cost_estimate=cost(100000000000, 2 * table_bytes + spec_bytes),
+        compiler_params=params(),
+        cost_estimate=cost(WHOLE_EXCHANGE, 2 * table_bytes + spec_bytes),
         name="filter_grad",
     )(*placed, *near, *across, gated_got, gated_spec, ahead, back)
     back_got, filter_grad, skip_grad = lax.optimization_barrier((back_got, filter_grad, skip_grad))
@@ -721,10 +723,10 @@
         out_specs=[flat, flat, edge_spec, tail_spec]
         + [pl.BlockSpec((INNER_PEERS, 8, width), lambda i: (0, 0, 0))] * far,
         out_shape=[shape((rows, channels), bf16)] * 2
-        + [shape((2, channels), bf16), shape((16, channels), bf16)]
+        + [shape((2, channels), f32), shape((16, channels), bf16)]
         + [shape((INNER_PEERS, 8, width), f32)] * far,
         scratch_shapes=[pltpu.VMEM((2, rows + 8, 128), f32)] * 2 + [pltpu.VMEM((peers, 8, width), f32)],
-        compiler_params=params(63),
+        compiler_params=params(),
         cost_estimate=cost(30 * rows * channels, 12 * rows * channels),
         name="finish",
     )(back_got, gated, key_feat, value_raw, edge, short_filter, skip_row)

time: 105 us -> 105 us (level)
  no operation moved by 1% of the time
where the time goes in v5:
time: 105 us
  Pallas kernels  35.7 us (34%)
  starting transfers between devices  35.5 us (34%)
  waiting for transfers between devices  29.1 us (28%)
  local copies, waits for them, and re-layouts  2.08 us (2%)
  other arithmetic  1.37 us (1%)
    ppermute x15, starting transfers between devices, paired(): lax.ppermute(block, 'ctx', [(i, i ^ distance) for i in range(lax.axis_siz...  20.2 us
    all_to_all x2, waiting for transfers between devices, exchanged(): return lax.all_to_all(block, 'ctx', split_axis=0, concat_axis=0, tiled=True)  14.8 us
    ppermute x15, waiting for transfers between devices, paired(): lax.ppermute(block, 'ctx', [(i, i ^ distance) for i in range(lax.axis_siz...  14.3 us
    all_to_all x2, starting transfers between devices, exchanged(): return lax.all_to_all(block, 'ctx', split_axis=0, concat_axis=0, tiled=True)  11.6 us
    pallas_call x1, Pallas kernels, kernel_plan(): pl.pallas_call(functools.partial(grad_kernel, outer=outer, width=width),...  7.59 us
    pallas_call x1, Pallas kernels, kernel_plan(): pl.pallas_call(functools.partial(conv_kernel, outer=outer, width=width),...  6.9 us
    pallas_call x1, Pallas kernels, kernel_plan(): pl.pallas_call(functools.partial(filter_kernel, outer=outer, width=width)...  5.72 us
    pallas_call x1, Pallas kernels, kernel_plan(): pl.pallas_call(functools.partial(finish_kernel, width=width), grid=(steps...  5.26 us
  transfers between devices with their start and end apart: 19, of which 7 were waited for; matrix products, arithmetic and copies ran while one was open for 1% of the time, Pallas kernels for 27%

profile of v5, /device:TPU:0, one launch (start us, length us, event | category | flops | bytes accessed | tf_op | source)
XLA Modules:
  0.0 104.5 jit_solution(1362117601284711058)
XLA Ops:
  0.6 2.5 %gate.1 = (bf16[16,128,256]{2,1,0:T(8,128)(2,1)}, f32[2,4096]{1,0:T(2,128)}) custom-call(bf16[128,4096]{1,0:T(8,128)(2,1)} %grad_ref.3, bf16[128,4096]{1,0:T(8,128)(2,1)} %query_ref.1, bf16[128,4096]{1,0:T(8,128)(2,1)} %value_ref.5), custom_call_target="tpu_custom_call" | custom-call | flops 524288 | bytes 3145728 | tf_op jit(solution)/shard_map/gate/pallas_call | solution.py:618
  3.1 2.3 %collective-permute-start = (f32[2,4096]{1,0:T(2,128)}, f32[2,4096]{1,0:T(2,128)S(1)}, u32[]{:S(2)}, u32[]{:S(2)}) collective-permute-start(f32[2,4096]{1,0:T(2,128)} %get-tuple-element.43), channel_id=1, source_target_pairs={{0,1},{1,2},{2,3},{3,4},{4,5},{5,6},{6,7},{7,8},{8,9},{9,10},{10,1... | collective-permute-start | bytes 98312 | tf_op jit(solution)/shard_map/ppermute | solution.py:18
  5.5 7.3 %all-to-all-start = ((bf16[16,128,256]{2,1,0:T(8,128)(2,1)}), bf16[16,128,256]{2,1,0:T(8,128)(2,1)}, u32[]{:S(2)}, u32[]{:S(2)}) async-start(bf16[16,128,256]{2,1,0:T(8,128)(2,1)} %get-tuple-element.52.gated_ref), calls=%async_computation | async-start | bytes 2097152 | tf_op jit(solution)/shard_map/all_to_all | solution.py:556
  12.7 0.0 collective-permute-done.edge_ref
  12.8 0.0 copy-start.3
  12.8 0.6 copy-done.3
  13.4 4.1 %mix.1 = (bf16[4,128,256]{2,1,0:T(8,128)(2,1)}, bf16[4,128,256]{2,1,0:T(8,128)(2,1)}, bf16[4,128,256]{2,1,0:T(8,128)(2,1)}, bf16[128,256]{1,0:T(8,128)(2,1)}, bf...) custom-call(bf16[128,4096]{1,0:T(8,128)(2,1)} %key_ref.3, ...), custom_call_target="tpu_custom_call" | custom-call | flops 40000000000 | bytes 6291456 | tf_op jit(solution)/shard_map/mix/pallas_call | solution.py:644
  17.4 0.4 collective-permute-start.1
  17.9 1.7 %collective-permute-start.2 = (bf16[4,128,256]{2,1,0:T(8,128)(2,1)}, bf16[4,128,256]{2,1,0:T(8,128)(2,1)S(1)}, u32[]{:S(2)}, u32[]{:S(2)}) collective-permute-start(bf16[4,128,256]{2,1,0:T(8,128)(2,1)} %get-tuple-element.47), channel_id=1, source_target_pairs={{0,2},{1,3},{2,0},{3,1},{4,6},{5,7},{6,4},{7,5},{8,10},{9,11},{10,... | collective-permute-start | bytes 786440 | tf_op jit(solution)/shard_map/ppermute | solution.py:560
  19.5 0.0 collective-permute-start.3
  19.5 1.7 %collective-permute-start.4 = (bf16[128,256]{1,0:T(8,128)(2,1)}, bf16[128,256]{1,0:T(8,128)(2,1)S(1)}, u32[]{:S(2)}, u32[]{:S(2)}) collective-permute-start(bf16[128,256]{1,0:T(8,128)(2,1)} %get-tuple-element.57), channel_id=1, source_target_pairs={{0,4},{1,5},{2,6},{3,7},{4,0},{5,1},{6,2},{7,3},{8,12},{9,13},{10,... | collective-permute-start | bytes 196616 | tf_op jit(solution)/shard_map/ppermute | solution.py:560
  21.2 0.0 copy-start.10
  21.2 2.4 %collective-permute-start.5 = (bf16[128,256]{1,0:T(8,128)(2,1)}, bf16[128,256]{1,0:T(8,128)(2,1)S(1)}, u32[]{:S(2)}, u32[]{:S(2)}) collective-permute-start(bf16[128,256]{1,0:T(8,128)(2,1)} %get-tuple-element.58), channel_id=1, source_target_pairs={{0,8},{1,9},{2,10},{3,11},{4,12},{5,13},{6,14},{7,15},{8,0},{9,1},... | collective-permute-start | bytes 196616 | tf_op jit(solution)/shard_map/ppermute | solution.py:560
  23.6 5.7 %filter_spectrum.1.filter_hbm = bf16[17,256,256]{2,1,0:T(8,128)(2,1)} custom-call(bf16[256,2048]{1,0:T(8,128)(2,1)} %taps_ref, bf16[17,256,256]{2,1,0:T(8,128)(2,1)} %constant.36.clone.ahead_ref.ahead_hbm.refs_12_), custom_call_target="tpu_custom_call" | custom-call | flops 40000000000 | bytes 5505024 | tf_op jit(solution)/shard_map/filter_spectrum/pallas_call | solution.py:671
  29.3 0.0 collective-permute-done.1.refs_0_.refs_4_
  29.3 0.0 copy-done.10
  29.3 0.4 collective-permute-start.6
  29.7 1.7 %collective-permute-done.2.refs_1_.refs_5_ = bf16[4,128,256]{2,1,0:T(8,128)(2,1)S(1)} collective-permute-done((bf16[4,128,256]{2,1,0:T(8,128)(2,1)}, bf16[4,128,256]{2,1,0:T(8,128)(2,1)S(1)}, u32[]{:S(2)}, u32[]{:S(2)}) %collective-permute-start.2) | collective-permute-done | bytes 262176 | tf_op jit(solution)/shard_map/ppermute | solution.py:560
  31.4 6.4 %collective-permute-done.3.refs_2_.refs_6_ = bf16[4,128,256]{2,1,0:T(8,128)(2,1)S(1)} collective-permute-done((bf16[4,128,256]{2,1,0:T(8,128)(2,1)}, bf16[4,128,256]{2,1,0:T(8,128)(2,1)S(1)}, u32[]{:S(2)}, u32[]{:S(2)}) %collective-permute-start.3) | collective-permute-done | bytes 262176 | tf_op jit(solution)/shard_map/ppermute | solution.py:560
  37.8 0.0 copy-done
  37.8 0.0 copy-done.1
  37.8 0.7 copy-done.2
  38.5 1.9 %regroup.1 = (bf16[3,128,256]{2,1,0:T(8,128)(2,1)}, bf16[3,128,256]{2,1,0:T(8,128)(2,1)}, bf16[3,128,256]{2,1,0:T(8,128)(2,1)}) custom-call(bf16[4,128,256]{2,1,0:T(8,128)(2,1)} %copy-done, bf16[4,128,256]{2,1,0:T(8,128)(2,1)} %copy-done.1, bf16[4,128,256]{2,1,0:T(8,128)(2,1)} %copy-done.2), custom_call_target="tpu_custom_call" | custom-call | bytes 2097152 | tf_op jit(solution)/shard_map/regroup/pallas_call | solution.py:660
  40.5 0.0 all-to-all-done
  40.5 1.3 %collective-permute-start.7 = (bf16[3,128,256]{2,1,0:T(8,128)(2,1)}, bf16[3,128,256]{2,1,0:T(8,128)(2,1)S(1)}, u32[]{:S(2)}, u32[]{:S(2)}) collective-permute-start(bf16[3,128,256]{2,1,0:T(8,128)(2,1)} %get-tuple-element.60), channel_id=1, source_target_pairs={{0,4},{1,5},{2,6},{3,7},{4,0},{5,1},{6,2},{7,3},{8,12},{9,13},{10,... | collective-permute-start | bytes 589832 | tf_op jit(solution)/shard_map/ppermute | solution.py:560
  41.8 2.3 %collective-permute-start.8 = (bf16[3,128,256]{2,1,0:T(8,128)(2,1)}, bf16[3,128,256]{2,1,0:T(8,128)(2,1)S(1)}, u32[]{:S(2)}, u32[]{:S(2)}) collective-permute-start(bf16[3,128,256]{2,1,0:T(8,128)(2,1)} %get-tuple-element.61), channel_id=1, source_target_pairs={{0,8},{1,9},{2,10},{3,11},{4,12},{5,13},{6,14},{7,15},{8,0},{9,1},... | collective-permute-start | bytes 589832 | tf_op jit(solution)/shard_map/ppermute | solution.py:560
  44.1 0.0 collective-permute-done.4.refs_1_
  44.1 1.5 %collective-permute-start.9 = (bf16[3,128,256]{2,1,0:T(8,128)(2,1)}, bf16[3,128,256]{2,1,0:T(8,128)(2,1)S(1)}, u32[]{:S(2)}, u32[]{:S(2)}) collective-permute-start(bf16[3,128,256]{2,1,0:T(8,128)(2,1)} %get-tuple-element.62), channel_id=1, source_target_pairs={{0,12},{1,13},{2,14},{3,15},{4,8},{5,9},{6,10},{7,11},{8,4},{9,5},... | collective-permute-start | bytes 589832 | tf_op jit(solution)/shard_map/ppermute | solution.py:560
  45.6 6.9 %conv_back.1 = (bf16[2048,256]{1,0:T(8,128)(2,1)}, bf16[17,256,256]{2,1,0:T(8,128)(2,1)}) custom-call(bf16[2048,256]{1,0:T(8,128)(2,1)} %bitcast.gated_hbm.refs_10_, bf16[17,256,256]{2,1,0:T(8,128)(2,1)} %filter_spectrum.1.filter_hbm, bf16[17,256,256]{2,1,0:T(8,128)(2,1)} %constant.36.clone.ahead_ref.ahead_hbm.refs_12_, ...), custom_call_target="tpu_custom_call" | custom-call | flops 40000000000 | bytes 11010048 | tf_op jit(solution)/shard_map/conv_back/pallas_call | solution.py:684
  52.5 0.0 copy-done.8
  52.5 4.4 %all-to-all-start.1 = ((bf16[16,128,256]{2,1,0:T(8,128)(2,1)}), bf16[16,128,256]{2,1,0:T(8,128)(2,1)}, u32[]{:S(2)}, u32[]{:S(2)}) async-start(bf16[16,128,256]{2,1,0:T(8,128)(2,1)} %bitcast.12), calls=%async_computation.1 | async-start | bytes 2097152 | tf_op jit(solution)/shard_map/all_to_all | solution.py:556
  56.9 0.0 collective-permute-done.5.refs_2_
  56.9 0.0 copy-start.9
  56.9 0.0 collective-permute-done.6.refs_3_
  56.9 0.0 collective-permute-done.7.refs_7_
  56.9 0.0 copy-start.5
  57.0 2.1 %collective-permute-done.8.refs_8_ = bf16[3,128,256]{2,1,0:T(8,128)(2,1)S(1)} collective-permute-done((bf16[3,128,256]{2,1,0:T(8,128)(2,1)}, bf16[3,128,256]{2,1,0:T(8,128)(2,1)S(1)}, u32[]{:S(2)}, u32[]{:S(2)}) %collective-permute-start.8) | collective-permute-done | bytes 196640 | tf_op jit(solution)/shard_map/ppermute | solution.py:560
  59.0 0.0 collective-permute-done.9.refs_9_
  59.0 0.0 copy-done.9
  59.1 0.0 copy-done.5
  59.1 0.6 copy-done.6
  59.7 0.1 copy-done.7
  59.8 7.6 %filter_grad.1 = (bf16[256,2048]{1,0:T(8,128)(2,1)}, f32[1,256]{1,0:T(1,128)}) custom-call(bf16[128,256]{1,0:T(8,128)(2,1)} %get-tuple-element.56.refs_0_, bf16[128,256]{1,0:T(8,128)(2,1)} %copy-done.8, bf16[128,256]{1,0:T(8,128)(2,1)} %copy-done.9, bf16[128,256]{1,0:T(8,128)(2,1)} %collective-permute-done.6.refs_3_, bf16[4,128,256]{2,1,0:T(8,128)(2,1)} %copy-done, ...), custom_call_target="tpu_custom_call" | custom-call | flops 99999997952 | bytes 6684672 | tf_op jit(solution)/shard_map/filter_grad/pallas_call | solution.py:698
  67.4 14.8 %all-to-all-done.1.back_ref = bf16[16,128,256]{2,1,0:T(8,128)(2,1)} async-done(((bf16[16,128,256]{2,1,0:T(8,128)(2,1)}), bf16[16,128,256]{2,1,0:T(8,128)(2,1)}, u32[]{:S(2)}, u32[]{:S(2)}) %all-to-all-start.1) | async-done | bytes 1048608 | tf_op jit(solution)/shard_map/all_to_all | solution.py:556
  82.2 5.3 %finish.1 = (bf16[128,4096]{1,0:T(8,128)(2,1)}, bf16[128,4096]{1,0:T(8,128)(2,1)}, f32[2,4096]{1,0:T(2,128)}, bf16[16,4096]{1,0:T(8,128)(2,1)}, f32[4,8,256]{2,1...) custom-call(bf16[16,128,256]{2,1,0:T(8,128)(2,1)} %all-to-all-done.1.back_ref, ...), custom_call_target="tpu_custom_call" | custom-call | flops 15728640 | bytes 6291456 | tf_op jit(solution)/shard_map/finish/pallas_call | solution.py:719
  87.5 2.8 %collective-permute-start.12 = (f32[4,8,256]{2,1,0:T(8,128)}, f32[4,8,256]{2,1,0:T(8,128)S(1)}, u32[]{:S(2)}, u32[]{:S(2)}) collective-permute-start(f32[4,8,256]{2,1,0:T(8,128)} %get-tuple-element.72), channel_id=1, source_target_pairs={{0,12},{1,13},{2,14},{3,15},{4,8},{5,9},{6,10},{7,11},{8,4},{9,5},... | collective-permute-start | bytes 98312 | tf_op jit(solution)/shard_map/ppermute | solution.py:560
  90.3 2.7 %collective-permute-start.11 = (f32[4,8,256]{2,1,0:T(8,128)}, f32[4,8,256]{2,1,0:T(8,128)S(1)}, u32[]{:S(2)}, u32[]{:S(2)}) collective-permute-start(f32[4,8,256]{2,1,0:T(8,128)} %get-tuple-element.71), channel_id=1, source_target_pairs={{0,8},{1,9},{2,10},{3,11},{4,12},{5,13},{6,14},{7,15},{8,0},{9,1},... | collective-permute-start | bytes 98312 | tf_op jit(solution)/shard_map/ppermute | solution.py:560
  93.0 0.5 collective-permute-start.10
  93.4 1.3 %collective-permute-start.13 = (f32[2,4096]{1,0:T(2,128)}, f32[2,4096]{1,0:T(2,128)S(1)}, u32[]{:S(2)}, u32[]{:S(2)}) collective-permute-start(f32[2,4096]{1,0:T(2,128)} %get-tuple-element.73), channel_id=1, source_target_pairs={{1,0},{2,1},{3,2},{4,3},{5,4},{6,5},{7,6},{8,7},{9,8},{10,9},{11,1... | collective-permute-start | bytes 98312 | tf_op jit(solution)/shard_map/ppermute | solution.py:18
  94.7 0.0 collective-permute-done.12
  94.7 0.6 collective-permute-done.11
  95.3 1.7 %collective-permute-done.10 = f32[4,8,256]{2,1,0:T(8,128)S(1)} collective-permute-done((f32[4,8,256]{2,1,0:T(8,128)}, f32[4,8,256]{2,1,0:T(8,128)S(1)}, u32[]{:S(2)}, u32[]{:S(2)}) %collective-permute-start.10) | collective-permute-done | bytes 32800 | tf_op jit(solution)/shard_map/ppermute | solution.py:560
  97.1 0.8 add_add_fusion
  97.8 0.0 collective-permute-done.13.head_ref
  97.9 0.0 copy-start.4
  97.9 2.4 %collective-permute-start.16 = (f32[8,256]{1,0:T(8,128)S(1)}, f32[8,256]{1,0:T(8,128)S(1)}, u32[]{:S(2)}, u32[]{:S(2)}) collective-permute-start(f32[8,256]{1,0:T(8,128)S(1)} %get-tuple-element.81), channel_id=1, source_target_pairs={{0,3},{1,2},{2,1},{3,0},{4,7},{5,6},{6,5},{7,4},{8,11},{9,10},{10,... | collective-permute-start | bytes 24584 | tf_op jit(solution)/shard_map/ppermute | solution.py:560
  100.3 0.0 collective-permute-start.15
  100.3 0.2 collective-permute-start.14
  100.4 0.0 copy-done.4
  100.4 1.7 %seam.1 = bf16[128,4096]{1,0:T(8,128)(2,1)} custom-call(bf16[16,4096]{1,0:T(8,128)(2,1)} %get-tuple-element.68.tail_ref, f32[2,4096]{1,0:T(2,128)} %copy-done.4, f32[3,4096]{1,0:T(4,128)} %short_ref.5, bf16[128,4096]{1,0:T(8,128)(2,1)} %get-tuple-element.76.done_ref), custom_call_target="tpu_custom_call", output_to_operand_aliasing={{}: (3, {})} | custom-call | flops 327680 | bytes 393216 | tf_op jit(solution)/shard_map/seam/pallas_call | solution.py:736
  102.2 0.0 collective-permute-done.16
  102.2 1.8 %collective-permute-done.15 = f32[8,256]{1,0:T(8,128)S(1)} collective-permute-done((f32[8,256]{1,0:T(8,128)S(1)}, f32[8,256]{1,0:T(8,128)S(1)}, u32[]{:S(2)}, u32[]{:S(2)}) %collective-permute-start.15) | collective-permute-done | bytes 8224 | tf_op jit(solution)/shard_map/ppermute | solution.py:560
  103.9 0.0 collective-permute-done.14
  103.9 0.6 slice_add_fusion
  (7 shorter events, 0.0 us)
Async XLA Ops:
  3.1 9.6 %collective-permute-start = (f32[2,4096]{1,0:T(2,128)}, f32[2,4096]{1,0:T(2,128)S(1)}, u32[]{:S(2)}, u32[]{:S(2)}) collective-permute-start(f32[2,4096]{1,0:T(2,128)} %get-tuple-element.43), channel_id=1, source_target_pairs={{0,1},{1,2},{2,3},{3,4},{4,5},{5,6},{6,7},{7,8},{8,9},{9,10},{10,1... | collective-permute-start | bytes 98312 | tf_op jit(solution)/shard_map/ppermute | solution.py:18
  5.5 35.0 %all-to-all-start = ((bf16[16,128,256]{2,1,0:T(8,128)(2,1)}), bf16[16,128,256]{2,1,0:T(8,128)(2,1)}, u32[]{:S(2)}, u32[]{:S(2)}) async-start(bf16[16,128,256]{2,1,0:T(8,128)(2,1)} %get-tuple-element.52.gated_ref), calls=%async_computation | async-start | bytes 2097152 | tf_op jit(solution)/shard_map/all_to_all | solution.py:556
  12.8 0.6 copy-start.3
  17.4 11.9 %collective-permute-start.1 = (bf16[4,128,256]{2,1,0:T(8,128)(2,1)}, bf16[4,128,256]{2,1,0:T(8,128)(2,1)S(1)}, u32[]{:S(2)}, u32[]{:S(2)}) collective-permute-start(bf16[4,128,256]{2,1,0:T(8,128)(2,1)} %get-tuple-element.46), channel_id=1, source_target_pairs={{0,1},{1,0},{2,3},{3,2},{4,5},{5,4},{6,7},{7,6},{8,9},{9,8},{10,11... | collective-permute-start | bytes 786440 | tf_op jit(solution)/shard_map/ppermute | solution.py:560
  17.9 13.6 %collective-permute-start.2 = (bf16[4,128,256]{2,1,0:T(8,128)(2,1)}, bf16[4,128,256]{2,1,0:T(8,128)(2,1)S(1)}, u32[]{:S(2)}, u32[]{:S(2)}) collective-permute-start(bf16[4,128,256]{2,1,0:T(8,128)(2,1)} %get-tuple-element.47), channel_id=1, source_target_pairs={{0,2},{1,3},{2,0},{3,1},{4,6},{5,7},{6,4},{7,5},{8,10},{9,11},{10,... | collective-permute-start | bytes 786440 | tf_op jit(solution)/shard_map/ppermute | solution.py:560
  19.5 18.3 %collective-permute-start.3 = (bf16[4,128,256]{2,1,0:T(8,128)(2,1)}, bf16[4,128,256]{2,1,0:T(8,128)(2,1)S(1)}, u32[]{:S(2)}, u32[]{:S(2)}) collective-permute-start(bf16[4,128,256]{2,1,0:T(8,128)(2,1)} %get-tuple-element.48), channel_id=1, source_target_pairs={{0,3},{1,2},{2,1},{3,0},{4,7},{5,6},{6,5},{7,4},{8,11},{9,10},{10,... | collective-permute-start | bytes 786440 | tf_op jit(solution)/shard_map/ppermute | solution.py:560
  19.5 24.6 %collective-permute-start.4 = (bf16[128,256]{1,0:T(8,128)(2,1)}, bf16[128,256]{1,0:T(8,128)(2,1)S(1)}, u32[]{:S(2)}, u32[]{:S(2)}) collective-permute-start(bf16[128,256]{1,0:T(8,128)(2,1)} %get-tuple-element.57), channel_id=1, source_target_pairs={{0,4},{1,5},{2,6},{3,7},{4,0},{5,1},{6,2},{7,3},{8,12},{9,13},{10,... | collective-permute-start | bytes 196616 | tf_op jit(solution)/shard_map/ppermute | solution.py:560
  21.2 8.1 %copy-start.10 = (bf16[128,256]{1,0:T(8,128)(2,1)S(1)}, bf16[128,256]{1,0:T(8,128)(2,1)}, u32[]{:S(2)}) copy-start(bf16[128,256]{1,0:T(8,128)(2,1)} %get-tuple-element.59) | copy-start | bytes 196612
  21.2 35.7 %collective-permute-start.5 = (bf16[128,256]{1,0:T(8,128)(2,1)}, bf16[128,256]{1,0:T(8,128)(2,1)S(1)}, u32[]{:S(2)}, u32[]{:S(2)}) collective-permute-start(bf16[128,256]{1,0:T(8,128)(2,1)} %get-tuple-element.58), channel_id=1, source_target_pairs={{0,8},{1,9},{2,10},{3,11},{4,12},{5,13},{6,14},{7,15},{8,0},{9,1},... | collective-permute-start | bytes 196616 | tf_op jit(solution)/shard_map/ppermute | solution.py:560
  29.3 8.5 %copy-start = (bf16[4,128,256]{2,1,0:T(8,128)(2,1)}, bf16[4,128,256]{2,1,0:T(8,128)(2,1)S(1)}, u32[]{:S(2)}) copy-start(bf16[4,128,256]{2,1,0:T(8,128)(2,1)S(1)} %collective-permute-done.1.refs_0_.refs_4_) | copy-start | bytes 786436
  29.3 27.6 %collective-permute-start.6 = (bf16[128,256]{1,0:T(8,128)(2,1)S(1)}, bf16[128,256]{1,0:T(8,128)(2,1)}, u32[]{:S(2)}, u32[]{:S(2)}) collective-permute-start(bf16[128,256]{1,0:T(8,128)(2,1)S(1)} %copy-done.10), channel_id=1, source_target_pairs={{0,12},{1,13},{2,14},{3,15},{4,8},{5,9},{6,10},{7,11},{8,4},{9,5},... | collective-permute-start | bytes 196616 | tf_op jit(solution)/shard_map/ppermute | solution.py:560
  31.4 6.4 %copy-start.1 = (bf16[4,128,256]{2,1,0:T(8,128)(2,1)}, bf16[4,128,256]{2,1,0:T(8,128)(2,1)S(1)}, u32[]{:S(2)}) copy-start(bf16[4,128,256]{2,1,0:T(8,128)(2,1)S(1)} %collective-permute-done.2.refs_1_.refs_5_) | copy-start | bytes 786436
  37.8 0.7 copy-start.2
  40.5 16.5 %collective-permute-start.7 = (bf16[3,128,256]{2,1,0:T(8,128)(2,1)}, bf16[3,128,256]{2,1,0:T(8,128)(2,1)S(1)}, u32[]{:S(2)}, u32[]{:S(2)}) collective-permute-start(bf16[3,128,256]{2,1,0:T(8,128)(2,1)} %get-tuple-element.60), channel_id=1, source_target_pairs={{0,4},{1,5},{2,6},{3,7},{4,0},{5,1},{6,2},{7,3},{8,12},{9,13},{10,... | collective-permute-start | bytes 589832 | tf_op jit(solution)/shard_map/ppermute | solution.py:560
  41.8 17.3 %collective-permute-start.8 = (bf16[3,128,256]{2,1,0:T(8,128)(2,1)}, bf16[3,128,256]{2,1,0:T(8,128)(2,1)S(1)}, u32[]{:S(2)}, u32[]{:S(2)}) collective-permute-start(bf16[3,128,256]{2,1,0:T(8,128)(2,1)} %get-tuple-element.61), channel_id=1, source_target_pairs={{0,8},{1,9},{2,10},{3,11},{4,12},{5,13},{6,14},{7,15},{8,0},{9,1},... | collective-permute-start | bytes 589832 | tf_op jit(solution)/shard_map/ppermute | solution.py:560
  44.1 8.4 %copy-start.8 = (bf16[128,256]{1,0:T(8,128)(2,1)}, bf16[128,256]{1,0:T(8,128)(2,1)S(1)}, u32[]{:S(2)}) copy-start(bf16[128,256]{1,0:T(8,128)(2,1)S(1)} %collective-permute-done.4.refs_1_) | copy-start | bytes 196612
  44.1 14.9 %collective-permute-start.9 = (bf16[3,128,256]{2,1,0:T(8,128)(2,1)}, bf16[3,128,256]{2,1,0:T(8,128)(2,1)S(1)}, u32[]{:S(2)}, u32[]{:S(2)}) collective-permute-start(bf16[3,128,256]{2,1,0:T(8,128)(2,1)} %get-tuple-element.62), channel_id=1, source_target_pairs={{0,12},{1,13},{2,14},{3,15},{4,8},{5,9},{6,10},{7,11},{8,4},{9,5},... | collective-permute-start | bytes 589832 | tf_op jit(solution)/shard_map/ppermute | solution.py:560
  52.5 29.7 %all-to-all-start.1 = ((bf16[16,128,256]{2,1,0:T(8,128)(2,1)}), bf16[16,128,256]{2,1,0:T(8,128)(2,1)}, u32[]{:S(2)}, u32[]{:S(2)}) async-start(bf16[16,128,256]{2,1,0:T(8,128)(2,1)} %bitcast.12), calls=%async_computation.1 | async-start | bytes 2097152 | tf_op jit(solution)/shard_map/all_to_all | solution.py:556
  56.9 2.1 %copy-start.9 = (bf16[128,256]{1,0:T(8,128)(2,1)}, bf16[128,256]{1,0:T(8,128)(2,1)S(1)}, u32[]{:S(2)}) copy-start(bf16[128,256]{1,0:T(8,128)(2,1)S(1)} %collective-permute-done.5.refs_2_) | copy-start | bytes 196612
  56.9 2.1 %copy-start.5 = (bf16[3,128,256]{2,1,0:T(8,128)(2,1)}, bf16[3,128,256]{2,1,0:T(8,128)(2,1)S(1)}, u32[]{:S(2)}) copy-start(bf16[3,128,256]{2,1,0:T(8,128)(2,1)S(1)} %collective-permute-done.7.refs_7_) | copy-start | bytes 589828
  59.0 0.7 copy-start.6
  59.0 0.7 copy-start.7
  87.5 7.3 %collective-permute-start.12 = (f32[4,8,256]{2,1,0:T(8,128)}, f32[4,8,256]{2,1,0:T(8,128)S(1)}, u32[]{:S(2)}, u32[]{:S(2)}) collective-permute-start(f32[4,8,256]{2,1,0:T(8,128)} %get-tuple-element.72), channel_id=1, source_target_pairs={{0,12},{1,13},{2,14},{3,15},{4,8},{5,9},{6,10},{7,11},{8,4},{9,5},... | collective-permute-start | bytes 98312 | tf_op jit(solution)/shard_map/ppermute | solution.py:560
  90.3 5.0 %collective-permute-start.11 = (f32[4,8,256]{2,1,0:T(8,128)}, f32[4,8,256]{2,1,0:T(8,128)S(1)}, u32[]{:S(2)}, u32[]{:S(2)}) collective-permute-start(f32[4,8,256]{2,1,0:T(8,128)} %get-tuple-element.71), channel_id=1, source_target_pairs={{0,8},{1,9},{2,10},{3,11},{4,12},{5,13},{6,14},{7,15},{8,0},{9,1},... | collective-permute-start | bytes 98312 | tf_op jit(solution)/shard_map/ppermute | solution.py:560
  93.0 4.1 %collective-permute-start.10 = (f32[4,8,256]{2,1,0:T(8,128)}, f32[4,8,256]{2,1,0:T(8,128)S(1)}, u32[]{:S(2)}, u32[]{:S(2)}) collective-permute-start(f32[4,8,256]{2,1,0:T(8,128)} %get-tuple-element.70), channel_id=1, source_target_pairs={{0,4},{1,5},{2,6},{3,7},{4,0},{5,1},{6,2},{7,3},{8,12},{9,13},{10,... | collective-permute-start | bytes 98312 | tf_op jit(solution)/shard_map/ppermute | solution.py:560
  93.4 4.4 %collective-permute-start.13 = (f32[2,4096]{1,0:T(2,128)}, f32[2,4096]{1,0:T(2,128)S(1)}, u32[]{:S(2)}, u32[]{:S(2)}) collective-permute-start(f32[2,4096]{1,0:T(2,128)} %get-tuple-element.73), channel_id=1, source_target_pairs={{1,0},{2,1},{3,2},{4,3},{5,4},{6,5},{7,6},{8,7},{9,8},{10,9},{11,1... | collective-permute-start | bytes 98312 | tf_op jit(solution)/shard_map/ppermute | solution.py:18
  97.9 2.6 %copy-start.4 = (f32[2,4096]{1,0:T(2,128)}, f32[2,4096]{1,0:T(2,128)S(1)}, u32[]{:S(2)}) copy-start(f32[2,4096]{1,0:T(2,128)S(1)} %collective-permute-done.13.head_ref) | copy-start | bytes 98308
  97.9 4.3 %collective-permute-start.16 = (f32[8,256]{1,0:T(8,128)S(1)}, f32[8,256]{1,0:T(8,128)S(1)}, u32[]{:S(2)}, u32[]{:S(2)}) collective-permute-start(f32[8,256]{1,0:T(8,128)S(1)} %get-tuple-element.81), channel_id=1, source_target_pairs={{0,3},{1,2},{2,1},{3,0},{4,7},{5,6},{6,5},{7,4},{8,11},{9,10},{10,... | collective-permute-start | bytes 24584 | tf_op jit(solution)/shard_map/ppermute | solution.py:560
  100.3 3.7 %collective-permute-start.15 = (f32[8,256]{1,0:T(8,128)S(1)}, f32[8,256]{1,0:T(8,128)S(1)}, u32[]{:S(2)}, u32[]{:S(2)}) collective-permute-start(f32[8,256]{1,0:T(8,128)S(1)} %get-tuple-element.82), channel_id=1, source_target_pairs={{0,2},{1,3},{2,0},{3,1},{4,6},{5,7},{6,4},{7,5},{8,10},{9,11},{10,... | collective-permute-start | bytes 24584 | tf_op jit(solution)/shard_map/ppermute | solution.py:560
  100.3 3.7 %collective-permute-start.14 = (f32[8,256]{1,0:T(8,128)S(1)}, f32[8,256]{1,0:T(8,128)S(1)}, u32[]{:S(2)}, u32[]{:S(2)}) collective-permute-start(f32[8,256]{1,0:T(8,128)S(1)} %get-tuple-element.83), channel_id=1, source_target_pairs={{0,1},{1,0},{2,3},{3,2},{4,5},{5,4},{6,7},{7,6},{8,9},{9,8},{10,11... | collective-permute-start | bytes 24584 | tf_op jit(solution)/shard_map/ppermute | solution.py:560

commit v6 on v5

--- a/solution.py
+++ b/solution.py
@@ -330,7 +330,7 @@
 
 
 def conv_kernel(
-    gated_hbm, filter_hbm, ahead_hbm, back_hbm, conv_ref, spec_hbm,
+    gated_hbm, filter_hbm, ahead_hbm, back_hbm, skip_ref, conv_ref, spec_hbm,
     gated_ref, filter_ref, ahead_ref, back_ref, spec_ref, z_ref, u_ref, sems, *, outer, width,
 ):
     gated_in = begun(gated_hbm, gated_ref, sems.at[0])
@@ -353,8 +353,13 @@
     for k in range(outer // 2 + 1):
         u_ref[k] = dot32(back_ref[k], z_ref[k])
 
+    first = lax.axis_index("ctx") * width
+
     def store(a, row, lane, value):
-        conv_ref[pl.ds(a * INNER + row, 16), lane : lane + 128] = value.astype(jnp.bfloat16)
+        place = pl.ds(a * INNER + row, 16)
+        skip = skip_ref[:, pl.ds(pl.multiple_of(first + lane, 128), 128)]
+        gated = gated_ref[place, lane : lane + 128].astype(jnp.float32)
+        conv_ref[place, lane : lane + 128] = (value + skip * gated).astype(jnp.bfloat16)
 
     outer_back(u_ref, store, outer, width)
     spec_out.wait()
@@ -490,11 +495,10 @@
             place_ref[...] = mixed_ref[(own_row ^ d) * INNER_PEERS + place]
 
 
-def finish_kernel(
-    back_ref, gated_ref, key_ref, value_ref, edge_ref, short_ref, skip_ref,
-    key_grad_ref, value_grad_ref, head_ref, tail_ref, *rest, width,
+def sums_kernel(
+    back_ref, key_ref, value_ref, edge_ref, head_ref, tail_ref, *rest, width
 ):
-    part_refs, behind, ahead, sums_ref = rest[:-3], rest[-3], rest[-2], rest[-1]
+    part_refs, behind, sums_ref = rest[:-2], rest[-2], rest[-1]
     rows = key_ref.shape[0]
     owners = back_ref.shape[0]
     step = pl.program_id(0)
@@ -503,21 +507,51 @@
             slot = (j * width + lane) // 128 % 2
             cols = slice(j * width + lane, j * width + lane + 128)
             lanes = slice(lane, lane + 128)
+            value = value_ref[:, cols].astype(jnp.float32)
+            behind[slot, 6:8] = edge_ref[:, cols]
+            behind[slot, 8 : 8 + rows] = value
+            mixed_grad = back_ref[j, :, lanes].astype(jnp.float32)
+            feature = (mixed_grad * key_ref[:, cols].astype(jnp.float32)).astype(jnp.bfloat16)
+            tail_ref[:, cols] = feature[rows - 16 :]
+            feature = feature.astype(jnp.float32)
+            head_ref[:, cols] = feature[:2]
+            shifted = (value, behind[slot, 7 : 7 + rows], behind[slot, 6 : 6 + rows])
+            sums_ref[step * owners + j, :, lanes] = jnp.concatenate(
+                [jnp.sum(feature * other, axis=0, keepdims=True) for other in shifted]
+                + [jnp.zeros((5, 128), jnp.float32)],
+                0,
+            )
+
+    @pl.when(step == pl.num_programs(0) - 1)
+    def _():
+        own = lax.axis_index("ctx") // INNER_PEERS
+        for d, part_ref in enumerate(part_refs):
+            part_ref[...] = sums_ref[pl.ds((own ^ d) * INNER_PEERS, INNER_PEERS)]
+
+
+def finish_kernel(
+    back_ref, key_ref, value_ref, edge_ref, short_ref,
+    key_grad_ref, value_grad_ref, behind, ahead, *, width,
+):
+    rows = key_ref.shape[0]
+    for j in range(back_ref.shape[0]):
+        for lane in range(0, width, 128):
+            slot = (j * width + lane) // 128 % 2
+            cols = slice(j * width + lane, j * width + lane + 128)
+            lanes = slice(lane, lane + 128)
             short = [short_ref[i : i + 1, cols] for i in range(3)]
             value = value_ref[:, cols].astype(jnp.float32)
             behind[slot, 6:8] = edge_ref[:, cols]
             behind[slot, 8 : 8 + rows] = value
-            value_1 = behind[slot, 7 : 7 + rows]
-            value_2 = behind[slot, 6 : 6 + rows]
-            mixed_grad = back_ref[j, :, lanes].astype(jnp.float32) + skip_ref[:, cols] * gated_ref[
-                j, :, lanes
-            ].astype(jnp.float32)
-            conv = short[0] * value + short[1] * value_1 + short[2] * value_2
+            mixed_grad = back_ref[j, :, lanes].astype(jnp.float32)
+            conv = (
+                short[0] * value
+                + short[1] * behind[slot, 7 : 7 + rows]
+                + short[2] * behind[slot, 6 : 6 + rows]
+            )
             key_grad_ref[:, cols] = (mixed_grad * conv).astype(jnp.bfloat16)
             feature = (mixed_grad * key_ref[:, cols].astype(jnp.float32)).astype(jnp.bfloat16)
-            tail_ref[:, cols] = feature[rows - 16 :]
             feature = feature.astype(jnp.float32)
-            head_ref[:, cols] = feature[:2]
             ahead[slot, 0:rows] = feature
             ahead[slot, rows : rows + 8] = jnp.zeros((8, 128), jnp.float32)
             value_grad_ref[:, cols] = (
@@ -525,21 +559,6 @@
                 + short[1] * ahead[slot, 1 : 1 + rows]
                 + short[2] * ahead[slot, 2 : 2 + rows]
             ).astype(jnp.bfloat16)
-            sums = jnp.concatenate(
-                [
-                    jnp.sum(feature * other, axis=0, keepdims=True)
-                    for other in (value, value_1, value_2)
-                ]
-                + [jnp.zeros((5, 128), jnp.float32)],
-                0,
-            )
-            sums_ref[step * owners + j, :, lanes] = sums
-
-    @pl.when(step == pl.num_programs(0) - 1)
-    def _():
-        own = lax.axis_index("ctx") // INNER_PEERS
-        for d, part_ref in enumerate(part_refs):
-            part_ref[...] = sums_ref[pl.ds((own ^ d) * INNER_PEERS, INNER_PEERS)]
 
 
 def seam_kernel(tail_ref, head_ref, short_ref, done_ref, value_grad_ref):
@@ -574,6 +593,10 @@
 
 def after(value, *others):
     return lax.optimization_barrier((value,) + others)[0]
+
+
+def in_hbm(*values):
+    return [pltpu.with_memory_space_constraint(value, pltpu.HBM) for value in values]
 
 
 def params(mib=63):
@@ -613,7 +636,6 @@
     edge_spec = pl.BlockSpec((2, span), lambda i: (0, i))
     tail_spec = pl.BlockSpec((16, span), lambda i: (0, i))
     short_spec = pl.BlockSpec((3, span), lambda i: (0, i))
-    skip_spec = pl.BlockSpec((1, span), lambda i: (0, i))
 
     gated, last = pl.pallas_call(
         functools.partial(gate_kernel, width=width),
@@ -683,7 +705,7 @@
 
     conv_back, gated_spec = pl.pallas_call(
         functools.partial(conv_kernel, outer=outer, width=width),
-        in_specs=[hbm] * 4,
+        in_specs=[hbm] * 4 + [pl.BlockSpec(memory_space=pltpu.VMEM)],
         out_specs=[pl.BlockSpec(memory_space=pltpu.VMEM), hbm],
         out_shape=(shape((seq, width), bf16), spec_shape),
         scratch_shapes=[pltpu.VMEM((seq, width), bf16), z_scratch, table_scratch, table_scratch, z_scratch]
@@ -691,7 +713,7 @@
         compiler_params=params(),
         cost_estimate=cost(BESIDE_EXCHANGE, 2 * table_bytes + 2 * spec_bytes + 4 * seq * width),
         name="conv_back",
-    )(gated_got, filter_spec, ahead, back)
+    )(gated_got, filter_spec, ahead, back, skip_row)
 
     back_got = exchanged(conv_back).reshape(peers, rows, width)
 
@@ -710,26 +732,37 @@
             pltpu.VMEM((seq, width), f32),
             pltpu.SemaphoreType.DMA((peers + 4,)),
         ],
-        compiler_params=params(),
+        compiler_params=params(30),
         cost_estimate=cost(WHOLE_EXCHANGE, 2 * table_bytes + spec_bytes),
         name="filter_grad",
-    )(*placed, *near, *across, gated_got, gated_spec, ahead, back)
+    )(*in_hbm(*placed, *near, *across, gated_got, gated_spec, ahead, back))
     back_got, filter_grad, skip_grad = lax.optimization_barrier((back_got, filter_grad, skip_grad))
 
-    key_grad, value_grad, head, tail, *short_parts = pl.pallas_call(
+    head, tail, *short_parts = pl.pallas_call(
+        functools.partial(sums_kernel, width=width),
+        grid=(steps,),
+        in_specs=[owned, flat, flat, edge_spec],
+        out_specs=[edge_spec, tail_spec]
+        + [pl.BlockSpec((INNER_PEERS, 8, width), lambda i: (0, 0, 0))] * far,
+        out_shape=[pltpu.HBM((2, channels), f32), pltpu.HBM((16, channels), bf16)]
+        + [pltpu.HBM((INNER_PEERS, 8, width), f32)] * far,
+        scratch_shapes=[shift_scratch, pltpu.VMEM((peers, 8, width), f32)],
+        compiler_params=params(30),
+        cost_estimate=cost(20 * rows * channels, 8 * rows * channels),
+        name="sums",
+    )(*in_hbm(back_got), key_feat, value_raw, edge)
+
+    key_grad, value_grad = pl.pallas_call(
         functools.partial(finish_kernel, width=width),
         grid=(steps,),
-        in_specs=[owned, owned, flat, flat, edge_spec, short_spec, skip_spec],
-        out_specs=[flat, flat, edge_spec, tail_spec]
-        + [pl.BlockSpec((INNER_PEERS, 8, width), lambda i: (0, 0, 0))] * far,
-        out_shape=[shape((rows, channels), bf16)] * 2
-        + [shape((2, channels), f32), shape((16, channels), bf16)]
-        + [shape((INNER_PEERS, 8, width), f32)] * far,
-        scratch_shapes=[pltpu.VMEM((2, rows + 8, 128), f32)] * 2 + [pltpu.VMEM((peers, 8, width), f32)],
-        compiler_params=params(),
+        in_specs=[owned, flat, flat, edge_spec, short_spec],
+        out_specs=[flat, flat],
+        out_shape=[pltpu.HBM((rows, channels), bf16)] * 2,
+        scratch_shapes=[shift_scratch] * 2,
+        compiler_params=params(30),
         cost_estimate=cost(30 * rows * channels, 12 * rows * channels),
         name="finish",
-    )(back_got, gated, key_feat, value_raw, edge, short_filter, skip_row)
+    )(*in_hbm(back_got), key_feat, value_raw, edge, short_filter)
 
     head_got = passed_along(head, "ctx", -1)
     short_grad, head_got, value_grad = summed_at_owner(short_parts, head_got, value_grad)

time: 105 us -> 103 us (0.981)
  waiting for transfers between devices: 29.1 us -> 24.8 us
  Pallas kernels: 35.7 us -> 38.3 us
    ppermute x15, waiting for transfers between devices: 14.3 us -> 10 us  [paired(): lax.ppermute(block, 'ctx', [(i, i ^ distance) for i in range(lax.axis_siz...]
    pallas_call x0 -> x1, Pallas kernels: none -> 2.92 us  [kernel_plan(): pl.pallas_call(functools.partial(sums_kernel, width=width), grid=(steps,)...]
    pallas_call x1, Pallas kernels: 5.26 us -> 3.81 us  [kernel_plan(): pl.pallas_call(functools.partial(finish_kernel, width=width), grid=(steps...]
  transfers between devices with their start and end apart: 19 -> 19, of which waited for: 7 -> 5; matrix products, arithmetic and copies ran while one was open for 1% -> 0% of each run, Pallas kernels for 27% -> 32%
where the time goes in v6:
time: 103 us; the launch traced here: 102 us
  Pallas kernels  38.3 us (37%)
  starting transfers between devices  35.7 us (35%)
  waiting for transfers between devices  24.8 us (24%)
  local copies, waits for them, and re-layouts  2.1 us (2%)
    ppermute x15, starting transfers between devices, paired(): lax.ppermute(block, 'ctx', [(i, i ^ distance) for i in range(lax.axis_siz...  20.5 us
    all_to_all x2, waiting for transfers between devices, exchanged(): return lax.all_to_all(block, 'ctx', split_axis=0, concat_axis=0, tiled=True)  14.7 us
    all_to_all x2, starting transfers between devices, exchanged(): return lax.all_to_all(block, 'ctx', split_axis=0, concat_axis=0, tiled=True)  11.6 us
    ppermute x15, waiting for transfers between devices, paired(): lax.ppermute(block, 'ctx', [(i, i ^ distance) for i in range(lax.axis_siz...  10 us
    pallas_call x1, Pallas kernels, kernel_plan(): pl.pallas_call(functools.partial(conv_kernel, outer=outer, width=width),...  7.86 us
    pallas_call x1, Pallas kernels, kernel_plan(): pl.pallas_call(functools.partial(grad_kernel, outer=outer, width=width),...  7.71 us
    pallas_call x1, Pallas kernels, kernel_plan(): pl.pallas_call(functools.partial(filter_kernel, outer=outer, width=width)...  5.72 us
    pallas_call x1, Pallas kernels, kernel_plan(): pl.pallas_call(functools.partial(mix_kernel, width=width), grid=(steps,),...  4.07 us
  transfers between devices with their start and end apart: 19, of which 5 were waited for; matrix products, arithmetic and copies ran while one was open for 0% of the time, Pallas kernels for 32%

profile of v6, /device:TPU:0, one launch (start us, length us, event | category | flops | bytes accessed | tf_op | source)
XLA Modules:
  0.0 102.3 jit_solution(17343060365651748911)
XLA Ops:
  0.6 2.5 %gate.1 = (bf16[16,128,256]{2,1,0:T(8,128)(2,1)}, f32[2,4096]{1,0:T(2,128)}) custom-call(bf16[128,4096]{1,0:T(8,128)(2,1)} %grad_ref.3, bf16[128,4096]{1,0:T(8,128)(2,1)} %query_ref.1, bf16[128,4096]{1,0:T(8,128)(2,1)} %value_ref.7), custom_call_target="tpu_custom_call" | custom-call | flops 524288 | bytes 3145728 | tf_op jit(solution)/shard_map/gate/pallas_call | solution.py:640
  3.1 2.3 %collective-permute-start = (f32[2,4096]{1,0:T(2,128)}, f32[2,4096]{1,0:T(2,128)S(1)}, u32[]{:S(2)}, u32[]{:S(2)}) collective-permute-start(f32[2,4096]{1,0:T(2,128)} %get-tuple-element.43), channel_id=1, source_target_pairs={{0,1},{1,2},{2,3},{3,4},{4,5},{5,6},{6,7},{7,8},{8,9},{9,10},{10,1... | collective-permute-start | bytes 98312 | tf_op jit(solution)/shard_map/ppermute | solution.py:18
  5.5 7.3 %all-to-all-start = ((bf16[16,128,256]{2,1,0:T(8,128)(2,1)}), bf16[16,128,256]{2,1,0:T(8,128)(2,1)}, u32[]{:S(2)}, u32[]{:S(2)}) async-start(bf16[16,128,256]{2,1,0:T(8,128)(2,1)} %get-tuple-element.52), calls=%async_computation | async-start | bytes 2097152 | tf_op jit(solution)/shard_map/all_to_all | solution.py:575
  12.7 0.0 collective-permute-done.edge_ref
  12.7 0.0 copy-start.3
  12.8 0.6 copy-done.3
  13.4 4.1 %mix.1 = (bf16[4,128,256]{2,1,0:T(8,128)(2,1)}, bf16[4,128,256]{2,1,0:T(8,128)(2,1)}, bf16[4,128,256]{2,1,0:T(8,128)(2,1)}, bf16[128,256]{1,0:T(8,128)(2,1)}, bf...) custom-call(bf16[128,4096]{1,0:T(8,128)(2,1)} %key_ref.5, ...), custom_call_target="tpu_custom_call" | custom-call | flops 40000000000 | bytes 6291456 | tf_op jit(solution)/shard_map/mix/pallas_call | solution.py:666
  17.4 0.4 collective-permute-start.1
  17.8 1.7 %collective-permute-start.2 = (bf16[4,128,256]{2,1,0:T(8,128)(2,1)}, bf16[4,128,256]{2,1,0:T(8,128)(2,1)S(1)}, u32[]{:S(2)}, u32[]{:S(2)}) collective-permute-start(bf16[4,128,256]{2,1,0:T(8,128)(2,1)} %get-tuple-element.47), channel_id=1, source_target_pairs={{0,2},{1,3},{2,0},{3,1},{4,6},{5,7},{6,4},{7,5},{8,10},{9,11},{10,... | collective-permute-start | bytes 786440 | tf_op jit(solution)/shard_map/ppermute | solution.py:579
  19.5 0.0 collective-permute-start.3
  19.5 1.7 %collective-permute-start.4 = (bf16[128,256]{1,0:T(8,128)(2,1)}, bf16[128,256]{1,0:T(8,128)(2,1)S(1)}, u32[]{:S(2)}, u32[]{:S(2)}) collective-permute-start(bf16[128,256]{1,0:T(8,128)(2,1)} %get-tuple-element.57), channel_id=1, source_target_pairs={{0,4},{1,5},{2,6},{3,7},{4,0},{5,1},{6,2},{7,3},{8,12},{9,13},{10,... | collective-permute-start | bytes 196616 | tf_op jit(solution)/shard_map/ppermute | solution.py:579
  21.2 2.4 %collective-permute-start.5 = (bf16[128,256]{1,0:T(8,128)(2,1)}, bf16[128,256]{1,0:T(8,128)(2,1)S(1)}, u32[]{:S(2)}, u32[]{:S(2)}) collective-permute-start(bf16[128,256]{1,0:T(8,128)(2,1)} %get-tuple-element.58), channel_id=1, source_target_pairs={{0,8},{1,9},{2,10},{3,11},{4,12},{5,13},{6,14},{7,15},{8,0},{9,1},... | collective-permute-start | bytes 196616 | tf_op jit(solution)/shard_map/ppermute | solution.py:579
  23.6 5.7 %filter_spectrum.1.filter_hbm = bf16[17,256,256]{2,1,0:T(8,128)(2,1)} custom-call(bf16[256,2048]{1,0:T(8,128)(2,1)} %taps_ref, bf16[17,256,256]{2,1,0:T(8,128)(2,1)} %constant.36.clone.ahead_ref.ahead_hbm.refs_12_), custom_call_target="tpu_custom_call" | custom-call | flops 40000000000 | bytes 5505024 | tf_op jit(solution)/shard_map/filter_spectrum/pallas_call | solution.py:693
  29.3 0.0 collective-permute-done.1.refs_0_.refs_4_
  29.3 0.0 copy-done.15
  29.3 0.4 collective-permute-start.6
  29.7 1.7 %collective-permute-done.2.refs_1_.refs_5_ = bf16[4,128,256]{2,1,0:T(8,128)(2,1)S(1)} collective-permute-done((bf16[4,128,256]{2,1,0:T(8,128)(2,1)}, bf16[4,128,256]{2,1,0:T(8,128)(2,1)S(1)}, u32[]{:S(2)}, u32[]{:S(2)}) %collective-permute-start.2) | collective-permute-done | bytes 262176 | tf_op jit(solution)/shard_map/ppermute | solution.py:579
  31.4 6.4 %collective-permute-done.3.refs_2_.refs_6_ = bf16[4,128,256]{2,1,0:T(8,128)(2,1)S(1)} collective-permute-done((bf16[4,128,256]{2,1,0:T(8,128)(2,1)}, bf16[4,128,256]{2,1,0:T(8,128)(2,1)S(1)}, u32[]{:S(2)}, u32[]{:S(2)}) %collective-permute-start.3) | collective-permute-done | bytes 262176 | tf_op jit(solution)/shard_map/ppermute | solution.py:579
  37.8 0.0 copy-done.5
  37.8 0.0 copy-done.6
  37.8 0.7 copy-done.7
  38.5 2.0 %regroup.1 = (bf16[3,128,256]{2,1,0:T(8,128)(2,1)}, bf16[3,128,256]{2,1,0:T(8,128)(2,1)}, bf16[3,128,256]{2,1,0:T(8,128)(2,1)}) custom-call(bf16[4,128,256]{2,1,0:T(8,128)(2,1)} %copy-done.5, bf16[4,128,256]{2,1,0:T(8,128)(2,1)} %copy-done.6, bf16[4,128,256]{2,1,0:T(8,128)(2,1)} %copy-done.7), custom_call_target="tpu_custom_call" | custom-call | bytes 2097152 | tf_op jit(solution)/shard_map/regroup/pallas_call | solution.py:682
  40.5 0.0 all-to-all-done
  40.5 1.2 %collective-permute-start.7 = (bf16[3,128,256]{2,1,0:T(8,128)(2,1)}, bf16[3,128,256]{2,1,0:T(8,128)(2,1)S(1)}, u32[]{:S(2)}, u32[]{:S(2)}) collective-permute-start(bf16[3,128,256]{2,1,0:T(8,128)(2,1)} %get-tuple-element.60), channel_id=1, source_target_pairs={{0,4},{1,5},{2,6},{3,7},{4,0},{5,1},{6,2},{7,3},{8,12},{9,13},{10,... | collective-permute-start | bytes 589832 | tf_op jit(solution)/shard_map/ppermute | solution.py:579
  41.8 2.3 %collective-permute-start.8 = (bf16[3,128,256]{2,1,0:T(8,128)(2,1)}, bf16[3,128,256]{2,1,0:T(8,128)(2,1)S(1)}, u32[]{:S(2)}, u32[]{:S(2)}) collective-permute-start(bf16[3,128,256]{2,1,0:T(8,128)(2,1)} %get-tuple-element.61), channel_id=1, source_target_pairs={{0,8},{1,9},{2,10},{3,11},{4,12},{5,13},{6,14},{7,15},{8,0},{9,1},... | collective-permute-start | bytes 589832 | tf_op jit(solution)/shard_map/ppermute | solution.py:579
  44.1 0.0 collective-permute-done.4.refs_1_
  44.1 1.5 %collective-permute-start.9 = (bf16[3,128,256]{2,1,0:T(8,128)(2,1)}, bf16[3,128,256]{2,1,0:T(8,128)(2,1)S(1)}, u32[]{:S(2)}, u32[]{:S(2)}) collective-permute-start(bf16[3,128,256]{2,1,0:T(8,128)(2,1)} %get-tuple-element.62), channel_id=1, source_target_pairs={{0,12},{1,13},{2,14},{3,15},{4,8},{5,9},{6,10},{7,11},{8,4},{9,5},... | collective-permute-start | bytes 589832 | tf_op jit(solution)/shard_map/ppermute | solution.py:579
  45.6 7.9 %conv_back.1 = (bf16[2048,256]{1,0:T(8,128)(2,1)}, bf16[17,256,256]{2,1,0:T(8,128)(2,1)}) custom-call(bf16[2048,256]{1,0:T(8,128)(2,1)} %bitcast.gated_hbm.refs_10_, bf16[17,256,256]{2,1,0:T(8,128)(2,1)} %filter_spectrum.1.filter_hbm, bf16[17,256,256]{2,1,0:T(8,128)(2,1)} %constant.36.clone.ahead_ref.ahead_hbm.refs_12_, ...), custom_call_target="tpu_custom_call" | custom-call | flops 40000000000 | bytes 11010048 | tf_op jit(solution)/shard_map/conv_back/pallas_call | solution.py:706
  53.5 0.0 copy-done.13
  53.5 4.3 %all-to-all-start.1 = ((bf16[16,128,256]{2,1,0:T(8,128)(2,1)}), bf16[16,128,256]{2,1,0:T(8,128)(2,1)}, u32[]{:S(2)}, u32[]{:S(2)}) async-start(bf16[16,128,256]{2,1,0:T(8,128)(2,1)} %bitcast.12), calls=%async_computation.1 | async-start | bytes 2097152 | tf_op jit(solution)/shard_map/all_to_all | solution.py:575
  57.8 0.0 collective-permute-done.5.refs_2_
  57.9 0.0 copy-start.14
  57.9 0.0 collective-permute-done.6.refs_3_
  57.9 0.0 collective-permute-done.7.refs_7_
  57.9 0.0 copy-start.10
  57.9 1.1 %collective-permute-done.8.refs_8_ = bf16[3,128,256]{2,1,0:T(8,128)(2,1)S(1)} collective-permute-done((bf16[3,128,256]{2,1,0:T(8,128)(2,1)}, bf16[3,128,256]{2,1,0:T(8,128)(2,1)S(1)}, u32[]{:S(2)}, u32[]{:S(2)}) %collective-permute-start.8) | collective-permute-done | bytes 196640 | tf_op jit(solution)/shard_map/ppermute | solution.py:579
  59.0 0.0 collective-permute-done.9.refs_9_
  59.0 0.0 copy-done.14
  59.0 0.0 copy-done.10
  59.1 0.6 copy-done.11
  59.7 0.1 copy-done.12
  59.8 7.7 %filter_grad.1 = (bf16[256,2048]{1,0:T(8,128)(2,1)}, f32[1,256]{1,0:T(1,128)}) custom-call(bf16[128,256]{1,0:T(8,128)(2,1)} %get-tuple-element.56.refs_0_, bf16[128,256]{1,0:T(8,128)(2,1)} %copy-done.13, bf16[128,256]{1,0:T(8,128)(2,1)} %copy-done.14, bf16[128,256]{1,0:T(8,128)(2,1)} %collective-permute-done.6.refs_3_, bf16[4,128,256]{2,1,0:T(8,128)(2,1)} %copy-done.5, ...), custom_call_target="tpu_custom_call" | custom-call | flops 99999997952 | bytes 6684672 | tf_op jit(solution)/shard_map/filter_grad/pallas_call | solution.py:720
  67.5 0.0 copy-start.2
  67.5 14.7 %all-to-all-done.1.back_ref = bf16[16,128,256]{2,1,0:T(8,128)(2,1)} async-done(((bf16[16,128,256]{2,1,0:T(8,128)(2,1)}), bf16[16,128,256]{2,1,0:T(8,128)(2,1)}, u32[]{:S(2)}, u32[]{:S(2)}) %all-to-all-start.1) | async-done | bytes 1048608 | tf_op jit(solution)/shard_map/all_to_all | solution.py:575
  82.2 0.0 copy-done.1
  82.3 2.9 %sums.1 = (f32[2,4096]{1,0:T(2,128)}, bf16[16,4096]{1,0:T(8,128)(2,1)}, f32[4,8,256]{2,1,0:T(8,128)}, f32[4,8,256]{2,1,0:T(8,128)}, f32[4,8,256]{2,1,0:T(8,128)}, /*index=5*/f32[4,8,256]{2,1,0:T(8,128)}) custom-call(bf16[16,128,256]{2,1,0:T(8,128)(2,1)} %all-to-all-done.1.back_ref, bf16[128,4096]{1,0:T(8,128)(2,1)S(1)} %copy-done.1, ...), custom_call_target="tpu_custom_call" | custom-call | flops 10485760 | bytes 4194304 | tf_op jit(solution)/shard_map/sums/pallas_call | solution.py:741
  85.2 0.0 copy-start.9
  85.2 2.8 %collective-permute-start.12 = (f32[4,8,256]{2,1,0:T(8,128)}, f32[4,8,256]{2,1,0:T(8,128)S(1)}, u32[]{:S(2)}, u32[]{:S(2)}) collective-permute-start(f32[4,8,256]{2,1,0:T(8,128)} %get-tuple-element.72), channel_id=1, source_target_pairs={{0,12},{1,13},{2,14},{3,15},{4,8},{5,9},{6,10},{7,11},{8,4},{9,5},... | collective-permute-start | bytes 98312 | tf_op jit(solution)/shard_map/ppermute | solution.py:579
  88.0 2.7 %collective-permute-start.11 = (f32[4,8,256]{2,1,0:T(8,128)}, f32[4,8,256]{2,1,0:T(8,128)S(1)}, u32[]{:S(2)}, u32[]{:S(2)}) collective-permute-start(f32[4,8,256]{2,1,0:T(8,128)} %get-tuple-element.71), channel_id=1, source_target_pairs={{0,8},{1,9},{2,10},{3,11},{4,12},{5,13},{6,14},{7,15},{8,0},{9,1},... | collective-permute-start | bytes 98312 | tf_op jit(solution)/shard_map/ppermute | solution.py:579
  90.7 0.5 collective-permute-start.10
  91.2 1.3 %collective-permute-start.13 = (f32[2,4096]{1,0:T(2,128)}, f32[2,4096]{1,0:T(2,128)S(1)}, u32[]{:S(2)}, u32[]{:S(2)}) collective-permute-start(f32[2,4096]{1,0:T(2,128)} %get-tuple-element.73), channel_id=1, source_target_pairs={{1,0},{2,1},{3,2},{4,3},{5,4},{6,5},{7,6},{8,7},{9,8},{10,9},{11,1... | collective-permute-start | bytes 98312 | tf_op jit(solution)/shard_map/ppermute | solution.py:18
  92.5 3.8 %finish.1 = (bf16[128,4096]{1,0:T(8,128)(2,1)}, bf16[128,4096]{1,0:T(8,128)(2,1)}) custom-call(bf16[16,128,256]{2,1,0:T(8,128)(2,1)} %all-to-all-done.1.back_ref, bf16[128,4096]{1,0:T(8,128)(2,1)S(1)} %copy-done.1, bf16[128,4096]{1,0:T(8,128)(2,1)S(1)} %copy-done, f32[2,4096]{1,0:T(2,128)S(1)} %copy-done.4, f32[3,4096]{1,0:T(4,128)S(1)} %copy-done.2), custom_call_target="tpu_custom_call" | custom-call | flops 15728640 | bytes 6291456 | tf_op jit(solution)/shard_map/finish/pallas_call | solution.py:755
  96.3 0.0 collective-permute-done.12
  96.3 0.0 collective-permute-done.11
  96.3 0.0 collective-permute-done.10
  96.3 0.0 collective-permute-done.13.head_ref
  96.4 1.7 %collective-permute-start.16 = (f32[8,256]{1,0:T(8,128)S(1)}, f32[8,256]{1,0:T(8,128)S(1)}, u32[]{:S(2)}, u32[]{:S(2)}) collective-permute-start(f32[8,256]{1,0:T(8,128)S(1)} %get-tuple-element.81), channel_id=1, source_target_pairs={{0,3},{1,2},{2,1},{3,0},{4,7},{5,6},{6,5},{7,4},{8,11},{9,10},{10,... | collective-permute-start | bytes 24584 | tf_op jit(solution)/shard_map/ppermute | solution.py:579
  98.1 1.1 %collective-permute-start.15 = (f32[8,256]{1,0:T(8,128)S(1)}, f32[8,256]{1,0:T(8,128)S(1)}, u32[]{:S(2)}, u32[]{:S(2)}) collective-permute-start(f32[8,256]{1,0:T(8,128)S(1)} %get-tuple-element.82), channel_id=1, source_target_pairs={{0,2},{1,3},{2,0},{3,1},{4,6},{5,7},{6,4},{7,5},{8,10},{9,11},{10,... | collective-permute-start | bytes 24584 | tf_op jit(solution)/shard_map/ppermute | solution.py:579
  99.2 0.0 collective-permute-start.14
  99.2 1.7 %seam.1 = bf16[128,4096]{1,0:T(8,128)(2,1)} custom-call(bf16[16,4096]{1,0:T(8,128)(2,1)} %get-tuple-element.68.tail_ref, f32[2,4096]{1,0:T(2,128)} %copy-done.8, f32[3,4096]{1,0:T(4,128)} %short_ref.5, bf16[128,4096]{1,0:T(8,128)(2,1)} %get-tuple-element.76.done_ref), custom_call_target="tpu_custom_call", output_to_operand_aliasing={{}: (3, {})} | custom-call | flops 327680 | bytes 393216 | tf_op jit(solution)/shard_map/seam/pallas_call | solution.py:769
  100.9 0.0 collective-permute-done.16
  100.9 0.8 collective-permute-done.15
  101.7 0.0 collective-permute-done.14
  101.7 0.6 slice_add_fusion
  (18 shorter events, 0.1 us)
Async XLA Ops:
  3.1 9.6 %collective-permute-start = (f32[2,4096]{1,0:T(2,128)}, f32[2,4096]{1,0:T(2,128)S(1)}, u32[]{:S(2)}, u32[]{:S(2)}) collective-permute-start(f32[2,4096]{1,0:T(2,128)} %get-tuple-element.43), channel_id=1, source_target_pairs={{0,1},{1,2},{2,3},{3,4},{4,5},{5,6},{6,7},{7,8},{8,9},{9,10},{10,1... | collective-permute-start | bytes 98312 | tf_op jit(solution)/shard_map/ppermute | solution.py:18
  5.5 35.0 %all-to-all-start = ((bf16[16,128,256]{2,1,0:T(8,128)(2,1)}), bf16[16,128,256]{2,1,0:T(8,128)(2,1)}, u32[]{:S(2)}, u32[]{:S(2)}) async-start(bf16[16,128,256]{2,1,0:T(8,128)(2,1)} %get-tuple-element.52), calls=%async_computation | async-start | bytes 2097152 | tf_op jit(solution)/shard_map/all_to_all | solution.py:575
  12.7 0.6 copy-start.3
  17.4 11.9 %collective-permute-start.1 = (bf16[4,128,256]{2,1,0:T(8,128)(2,1)}, bf16[4,128,256]{2,1,0:T(8,128)(2,1)S(1)}, u32[]{:S(2)}, u32[]{:S(2)}) collective-permute-start(bf16[4,128,256]{2,1,0:T(8,128)(2,1)} %get-tuple-element.46), channel_id=1, source_target_pairs={{0,1},{1,0},{2,3},{3,2},{4,5},{5,4},{6,7},{7,6},{8,9},{9,8},{10,11... | collective-permute-start | bytes 786440 | tf_op jit(solution)/shard_map/ppermute | solution.py:579
  17.8 13.6 %collective-permute-start.2 = (bf16[4,128,256]{2,1,0:T(8,128)(2,1)}, bf16[4,128,256]{2,1,0:T(8,128)(2,1)S(1)}, u32[]{:S(2)}, u32[]{:S(2)}) collective-permute-start(bf16[4,128,256]{2,1,0:T(8,128)(2,1)} %get-tuple-element.47), channel_id=1, source_target_pairs={{0,2},{1,3},{2,0},{3,1},{4,6},{5,7},{6,4},{7,5},{8,10},{9,11},{10,... | collective-permute-start | bytes 786440 | tf_op jit(solution)/shard_map/ppermute | solution.py:579
  19.5 18.3 %collective-permute-start.3 = (bf16[4,128,256]{2,1,0:T(8,128)(2,1)}, bf16[4,128,256]{2,1,0:T(8,128)(2,1)S(1)}, u32[]{:S(2)}, u32[]{:S(2)}) collective-permute-start(bf16[4,128,256]{2,1,0:T(8,128)(2,1)} %get-tuple-element.48), channel_id=1, source_target_pairs={{0,3},{1,2},{2,1},{3,0},{4,7},{5,6},{6,5},{7,4},{8,11},{9,10},{10,... | collective-permute-start | bytes 786440 | tf_op jit(solution)/shard_map/ppermute | solution.py:579
  19.5 24.5 %collective-permute-start.4 = (bf16[128,256]{1,0:T(8,128)(2,1)}, bf16[128,256]{1,0:T(8,128)(2,1)S(1)}, u32[]{:S(2)}, u32[]{:S(2)}) collective-permute-start(bf16[128,256]{1,0:T(8,128)(2,1)} %get-tuple-element.57), channel_id=1, source_target_pairs={{0,4},{1,5},{2,6},{3,7},{4,0},{5,1},{6,2},{7,3},{8,12},{9,13},{10,... | collective-permute-start | bytes 196616 | tf_op jit(solution)/shard_map/ppermute | solution.py:579
  21.2 8.1 %copy-start.15 = (bf16[128,256]{1,0:T(8,128)(2,1)S(1)}, bf16[128,256]{1,0:T(8,128)(2,1)}, u32[]{:S(2)}) copy-start(bf16[128,256]{1,0:T(8,128)(2,1)} %get-tuple-element.59) | copy-start | bytes 196612
  21.2 36.6 %collective-permute-start.5 = (bf16[128,256]{1,0:T(8,128)(2,1)}, bf16[128,256]{1,0:T(8,128)(2,1)S(1)}, u32[]{:S(2)}, u32[]{:S(2)}) collective-permute-start(bf16[128,256]{1,0:T(8,128)(2,1)} %get-tuple-element.58), channel_id=1, source_target_pairs={{0,8},{1,9},{2,10},{3,11},{4,12},{5,13},{6,14},{7,15},{8,0},{9,1},... | collective-permute-start | bytes 196616 | tf_op jit(solution)/shard_map/ppermute | solution.py:579
  29.3 8.5 %copy-start.5 = (bf16[4,128,256]{2,1,0:T(8,128)(2,1)}, bf16[4,128,256]{2,1,0:T(8,128)(2,1)S(1)}, u32[]{:S(2)}) copy-start(bf16[4,128,256]{2,1,0:T(8,128)(2,1)S(1)} %collective-permute-done.1.refs_0_.refs_4_) | copy-start | bytes 786436
  29.3 28.5 %collective-permute-start.6 = (bf16[128,256]{1,0:T(8,128)(2,1)S(1)}, bf16[128,256]{1,0:T(8,128)(2,1)}, u32[]{:S(2)}, u32[]{:S(2)}) collective-permute-start(bf16[128,256]{1,0:T(8,128)(2,1)S(1)} %copy-done.15), channel_id=1, source_target_pairs={{0,12},{1,13},{2,14},{3,15},{4,8},{5,9},{6,10},{7,11},{8,4},{9,5},... | collective-permute-start | bytes 196616 | tf_op jit(solution)/shard_map/ppermute | solution.py:579
  31.4 6.4 %copy-start.6 = (bf16[4,128,256]{2,1,0:T(8,128)(2,1)}, bf16[4,128,256]{2,1,0:T(8,128)(2,1)S(1)}, u32[]{:S(2)}) copy-start(bf16[4,128,256]{2,1,0:T(8,128)(2,1)S(1)} %collective-permute-done.2.refs_1_.refs_5_) | copy-start | bytes 786436
  37.8 0.7 copy-start.7
  40.5 17.4 %collective-permute-start.7 = (bf16[3,128,256]{2,1,0:T(8,128)(2,1)}, bf16[3,128,256]{2,1,0:T(8,128)(2,1)S(1)}, u32[]{:S(2)}, u32[]{:S(2)}) collective-permute-start(bf16[3,128,256]{2,1,0:T(8,128)(2,1)} %get-tuple-element.60), channel_id=1, source_target_pairs={{0,4},{1,5},{2,6},{3,7},{4,0},{5,1},{6,2},{7,3},{8,12},{9,13},{10,... | collective-permute-start | bytes 589832 | tf_op jit(solution)/shard_map/ppermute | solution.py:579
  41.8 17.3 %collective-permute-start.8 = (bf16[3,128,256]{2,1,0:T(8,128)(2,1)}, bf16[3,128,256]{2,1,0:T(8,128)(2,1)S(1)}, u32[]{:S(2)}, u32[]{:S(2)}) collective-permute-start(bf16[3,128,256]{2,1,0:T(8,128)(2,1)} %get-tuple-element.61), channel_id=1, source_target_pairs={{0,8},{1,9},{2,10},{3,11},{4,12},{5,13},{6,14},{7,15},{8,0},{9,1},... | collective-permute-start | bytes 589832 | tf_op jit(solution)/shard_map/ppermute | solution.py:579
  44.1 9.4 %copy-start.13 = (bf16[128,256]{1,0:T(8,128)(2,1)}, bf16[128,256]{1,0:T(8,128)(2,1)S(1)}, u32[]{:S(2)}) copy-start(bf16[128,256]{1,0:T(8,128)(2,1)S(1)} %collective-permute-done.4.refs_1_) | copy-start | bytes 196612
  44.1 15.0 %collective-permute-start.9 = (bf16[3,128,256]{2,1,0:T(8,128)(2,1)}, bf16[3,128,256]{2,1,0:T(8,128)(2,1)S(1)}, u32[]{:S(2)}, u32[]{:S(2)}) collective-permute-start(bf16[3,128,256]{2,1,0:T(8,128)(2,1)} %get-tuple-element.62), channel_id=1, source_target_pairs={{0,12},{1,13},{2,14},{3,15},{4,8},{5,9},{6,10},{7,11},{8,4},{9,5},... | collective-permute-start | bytes 589832 | tf_op jit(solution)/shard_map/ppermute | solution.py:579
  53.5 28.8 %all-to-all-start.1 = ((bf16[16,128,256]{2,1,0:T(8,128)(2,1)}), bf16[16,128,256]{2,1,0:T(8,128)(2,1)}, u32[]{:S(2)}, u32[]{:S(2)}) async-start(bf16[16,128,256]{2,1,0:T(8,128)(2,1)} %bitcast.12), calls=%async_computation.1 | async-start | bytes 2097152 | tf_op jit(solution)/shard_map/all_to_all | solution.py:575
  57.9 1.2 %copy-start.14 = (bf16[128,256]{1,0:T(8,128)(2,1)}, bf16[128,256]{1,0:T(8,128)(2,1)S(1)}, u32[]{:S(2)}) copy-start(bf16[128,256]{1,0:T(8,128)(2,1)S(1)} %collective-permute-done.5.refs_2_) | copy-start | bytes 196612
  57.9 1.2 %copy-start.10 = (bf16[3,128,256]{2,1,0:T(8,128)(2,1)}, bf16[3,128,256]{2,1,0:T(8,128)(2,1)S(1)}, u32[]{:S(2)}) copy-start(bf16[3,128,256]{2,1,0:T(8,128)(2,1)S(1)} %collective-permute-done.7.refs_7_) | copy-start | bytes 589828
  59.0 0.7 copy-start.11
  59.0 0.7 copy-start.12
  59.8 22.5 %copy-start = (bf16[128,4096]{1,0:T(8,128)(2,1)S(1)}, bf16[128,4096]{1,0:T(8,128)(2,1)}, u32[]{:S(2)}) copy-start(bf16[128,4096]{1,0:T(8,128)(2,1)} %value_ref.7) | copy-start | bytes 3145732
  59.8 22.5 %copy-start.1 = (bf16[128,4096]{1,0:T(8,128)(2,1)S(1)}, bf16[128,4096]{1,0:T(8,128)(2,1)}, u32[]{:S(2)}) copy-start(bf16[128,4096]{1,0:T(8,128)(2,1)} %key_ref.5) | copy-start | bytes 3145732
  59.8 22.5 %copy-start.4 = (f32[2,4096]{1,0:T(2,128)S(1)}, f32[2,4096]{1,0:T(2,128)}, u32[]{:S(2)}) copy-start(f32[2,4096]{1,0:T(2,128)} %copy-done.3) | copy-start | bytes 98308
  67.5 25.0 %copy-start.2 = (f32[3,4096]{1,0:T(4,128)S(1)}, f32[3,4096]{1,0:T(4,128)}, u32[]{:S(2)}) copy-start(f32[3,4096]{1,0:T(4,128)} %short_ref.5) | copy-start | bytes 147460
  85.2 11.1 %copy-start.9 = (f32[4,8,256]{2,1,0:T(8,128)S(1)}, f32[4,8,256]{2,1,0:T(8,128)}, u32[]{:S(2)}) copy-start(f32[4,8,256]{2,1,0:T(8,128)} %get-tuple-element.69) | copy-start | bytes 98308
  85.2 11.1 %collective-permute-start.12 = (f32[4,8,256]{2,1,0:T(8,128)}, f32[4,8,256]{2,1,0:T(8,128)S(1)}, u32[]{:S(2)}, u32[]{:S(2)}) collective-permute-start(f32[4,8,256]{2,1,0:T(8,128)} %get-tuple-element.72), channel_id=1, source_target_pairs={{0,12},{1,13},{2,14},{3,15},{4,8},{5,9},{6,10},{7,11},{8,4},{9,5},... | collective-permute-start | bytes 98312 | tf_op jit(solution)/shard_map/ppermute | solution.py:579
  88.0 8.3 %collective-permute-start.11 = (f32[4,8,256]{2,1,0:T(8,128)}, f32[4,8,256]{2,1,0:T(8,128)S(1)}, u32[]{:S(2)}, u32[]{:S(2)}) collective-permute-start(f32[4,8,256]{2,1,0:T(8,128)} %get-tuple-element.71), channel_id=1, source_target_pairs={{0,8},{1,9},{2,10},{3,11},{4,12},{5,13},{6,14},{7,15},{8,0},{9,1},... | collective-permute-start | bytes 98312 | tf_op jit(solution)/shard_map/ppermute | solution.py:579
  90.7 5.6 %collective-permute-start.10 = (f32[4,8,256]{2,1,0:T(8,128)}, f32[4,8,256]{2,1,0:T(8,128)S(1)}, u32[]{:S(2)}, u32[]{:S(2)}) collective-permute-start(f32[4,8,256]{2,1,0:T(8,128)} %get-tuple-element.70), channel_id=1, source_target_pairs={{0,4},{1,5},{2,6},{3,7},{4,0},{5,1},{6,2},{7,3},{8,12},{9,13},{10,... | collective-permute-start | bytes 98312 | tf_op jit(solution)/shard_map/ppermute | solution.py:579
  91.2 5.2 %collective-permute-start.13 = (f32[2,4096]{1,0:T(2,128)}, f32[2,4096]{1,0:T(2,128)S(1)}, u32[]{:S(2)}, u32[]{:S(2)}) collective-permute-start(f32[2,4096]{1,0:T(2,128)} %get-tuple-element.73), channel_id=1, source_target_pairs={{1,0},{2,1},{3,2},{4,3},{5,4},{6,5},{7,6},{8,7},{9,8},{10,9},{11,1... | collective-permute-start | bytes 98312 | tf_op jit(solution)/shard_map/ppermute | solution.py:18
  96.3 2.9 %copy-start.8 = (f32[2,4096]{1,0:T(2,128)}, f32[2,4096]{1,0:T(2,128)S(1)}, u32[]{:S(2)}) copy-start(f32[2,4096]{1,0:T(2,128)S(1)} %collective-permute-done.13.head_ref) | copy-start | bytes 98308
  96.4 4.5 %collective-permute-start.16 = (f32[8,256]{1,0:T(8,128)S(1)}, f32[8,256]{1,0:T(8,128)S(1)}, u32[]{:S(2)}, u32[]{:S(2)}) collective-permute-start(f32[8,256]{1,0:T(8,128)S(1)} %get-tuple-element.81), channel_id=1, source_target_pairs={{0,3},{1,2},{2,1},{3,0},{4,7},{5,6},{6,5},{7,4},{8,11},{9,10},{10,... | collective-permute-start | bytes 24584 | tf_op jit(solution)/shard_map/ppermute | solution.py:579
  98.1 3.7 %collective-permute-start.15 = (f32[8,256]{1,0:T(8,128)S(1)}, f32[8,256]{1,0:T(8,128)S(1)}, u32[]{:S(2)}, u32[]{:S(2)}) collective-permute-start(f32[8,256]{1,0:T(8,128)S(1)} %get-tuple-element.82), channel_id=1, source_target_pairs={{0,2},{1,3},{2,0},{3,1},{4,6},{5,7},{6,4},{7,5},{8,10},{9,11},{10,... | collective-permute-start | bytes 24584 | tf_op jit(solution)/shard_map/ppermute | solution.py:579
  99.2 2.5 %collective-permute-start.14 = (f32[8,256]{1,0:T(8,128)S(1)}, f32[8,256]{1,0:T(8,128)S(1)}, u32[]{:S(2)}, u32[]{:S(2)}) collective-permute-start(f32[8,256]{1,0:T(8,128)S(1)} %get-tuple-element.83), channel_id=1, source_target_pairs={{0,1},{1,0},{2,3},{3,2},{4,5},{5,4},{6,7},{7,6},{8,9},{9,8},{10,11... | collective-permute-start | bytes 24584 | tf_op jit(solution)/shard_map/ppermute | solution.py:579

commit v7 on v6

--- a/solution.py
+++ b/solution.py
@@ -432,24 +432,6 @@
             far[d - 1][e - 1] = near[e - 1][own_row ^ d]
 
 
-def shifted_down(values, distance, edge):
-    moved = pltpu.roll(values, distance, 0)
-    row = lax.broadcasted_iota(jnp.int32, values.shape, 0)
-    for i in range(distance):
-        source = edge.shape[0] - distance + i
-        moved = jnp.where(row == i, edge[source : source + 1], moved)
-    return moved
-
-
-def shifted_up(values, distance, edge):
-    count = values.shape[0]
-    moved = pltpu.roll(values, count - distance, 0)
-    row = lax.broadcasted_iota(jnp.int32, values.shape, 0)
-    for i in range(distance):
-        moved = jnp.where(row == count - distance + i, edge[i : i + 1], moved)
-    return moved
-
-
 def gate_kernel(grad_ref, query_ref, value_ref, gated_ref, last_ref, *, width):
     last_ref[...] = value_ref[...].astype(jnp.float32)[value_ref.shape[0] - 2 :]
     for j in range(gated_ref.shape[0]):
@@ -496,7 +478,7 @@
 
 
 def sums_kernel(
-    back_ref, key_ref, value_ref, edge_ref, head_ref, tail_ref, *rest, width
+    back_ref, key_ref, value_ref, edge_ref, head_ref, *rest, width
 ):
     part_refs, behind, sums_ref = rest[:-2], rest[-2], rest[-1]
     rows = key_ref.shape[0]
@@ -512,7 +494,6 @@
             behind[slot, 8 : 8 + rows] = value
             mixed_grad = back_ref[j, :, lanes].astype(jnp.float32)
             feature = (mixed_grad * key_ref[:, cols].astype(jnp.float32)).astype(jnp.bfloat16)
-            tail_ref[:, cols] = feature[rows - 16 :]
             feature = feature.astype(jnp.float32)
             head_ref[:, cols] = feature[:2]
             shifted = (value, behind[slot, 7 : 7 + rows], behind[slot, 6 : 6 + rows])
@@ -530,7 +511,7 @@
 
 
 def finish_kernel(
-    back_ref, key_ref, value_ref, edge_ref, short_ref,
+    back_ref, key_ref, value_ref, edge_ref, next_ref, short_ref,
     key_grad_ref, value_grad_ref, behind, ahead, *, width,
 ):
     rows = key_ref.shape[0]
@@ -553,22 +534,12 @@
             feature = (mixed_grad * key_ref[:, cols].astype(jnp.float32)).astype(jnp.bfloat16)
             feature = feature.astype(jnp.float32)
             ahead[slot, 0:rows] = feature
-            ahead[slot, rows : rows + 8] = jnp.zeros((8, 128), jnp.float32)
+            ahead[slot, rows : rows + 2] = next_ref[:, cols]
             value_grad_ref[:, cols] = (
                 short[0] * feature
                 + short[1] * ahead[slot, 1 : 1 + rows]
                 + short[2] * ahead[slot, 2 : 2 + rows]
             ).astype(jnp.bfloat16)
-
-
-def seam_kernel(tail_ref, head_ref, short_ref, done_ref, value_grad_ref):
-    feature = tail_ref[...].astype(jnp.float32)
-    head = head_ref[...]
-    value_grad_ref[...] = (
-        short_ref[0:1] * feature
-        + short_ref[1:2] * shifted_up(feature, 1, head)
-        + short_ref[2:3] * shifted_up(feature, 2, head)
-    ).astype(jnp.bfloat16)
 
 
 def exchanged(block):
@@ -634,7 +605,6 @@
     flat = pl.BlockSpec((rows, span), lambda i: (0, i))
     owned = pl.BlockSpec((group, rows, width), lambda i: (i, 0, 0))
     edge_spec = pl.BlockSpec((2, span), lambda i: (0, i))
-    tail_spec = pl.BlockSpec((16, span), lambda i: (0, i))
     short_spec = pl.BlockSpec((3, span), lambda i: (0, i))
 
     gated, last = pl.pallas_call(
@@ -658,7 +628,6 @@
     spec_bytes = 4 * bins * INNER * width
     work = 2 * bins * (2 * INNER) ** 2 * width
     edge = passed_along(last, "ctx", 1)
-    whole = lambda size: pl.BlockSpec((size, channels), lambda i: (0, 0))
     shift_scratch = pltpu.VMEM((2, rows + 8, 128), f32)
     near_spec = pl.BlockSpec((far, rows, width), lambda i: (0, 0, 0))
     far_spec = pl.BlockSpec((INNER_PEERS - 1, rows, width), lambda i: (0, 0, 0))
@@ -738,45 +707,33 @@
     )(*in_hbm(*placed, *near, *across, gated_got, gated_spec, ahead, back))
     back_got, filter_grad, skip_grad = lax.optimization_barrier((back_got, filter_grad, skip_grad))
 
-    head, tail, *short_parts = pl.pallas_call(
+    head, *short_parts = pl.pallas_call(
         functools.partial(sums_kernel, width=width),
         grid=(steps,),
         in_specs=[owned, flat, flat, edge_spec],
-        out_specs=[edge_spec, tail_spec]
+        out_specs=[edge_spec]
         + [pl.BlockSpec((INNER_PEERS, 8, width), lambda i: (0, 0, 0))] * far,
-        out_shape=[pltpu.HBM((2, channels), f32), pltpu.HBM((16, channels), bf16)]
+        out_shape=[pltpu.HBM((2, channels), f32)]
         + [pltpu.HBM((INNER_PEERS, 8, width), f32)] * far,
         scratch_shapes=[shift_scratch, pltpu.VMEM((peers, 8, width), f32)],
         compiler_params=params(30),
         cost_estimate=cost(20 * rows * channels, 8 * rows * channels),
         name="sums",
-    )(*in_hbm(back_got), key_feat, value_raw, edge)
-
+    )(back_got, key_feat, value_raw, edge)
+
+    head_got = passed_along(head, "ctx", -1)
+    short_grad, head_got = summed_at_owner(short_parts, head_got)
     key_grad, value_grad = pl.pallas_call(
         functools.partial(finish_kernel, width=width),
         grid=(steps,),
-        in_specs=[owned, flat, flat, edge_spec, short_spec],
+        in_specs=[owned, flat, flat, edge_spec, edge_spec, short_spec],
         out_specs=[flat, flat],
         out_shape=[pltpu.HBM((rows, channels), bf16)] * 2,
         scratch_shapes=[shift_scratch] * 2,
         compiler_params=params(30),
         cost_estimate=cost(30 * rows * channels, 12 * rows * channels),
         name="finish",
-    )(*in_hbm(back_got), key_feat, value_raw, edge, short_filter)
-
-    head_got = passed_along(head, "ctx", -1)
-    short_grad, head_got, value_grad = summed_at_owner(short_parts, head_got, value_grad)
-    value_grad = pl.pallas_call(
-        seam_kernel,
-        grid=(1,),
-        in_specs=[whole(16), whole(2), whole(3), hbm],
-        out_specs=pl.BlockSpec((16, channels), lambda i: (rows // 16 - 1, 0)),
-        out_shape=shape((rows, channels), bf16),
-        input_output_aliases={3: 0},
-        compiler_params=params(),
-        cost_estimate=cost(5 * 16 * channels, 6 * 16 * channels),
-        name="seam",
-    )(tail, head_got, short_filter, value_grad)
+    )(back_got, key_feat, value_raw, edge, head_got, short_filter)
     return query_grad, key_grad, value_grad, filter_grad, skip_grad.reshape(width), short_grad[:3]
 
 

time: 103 us -> 102 us (level)
  Pallas kernels: 38.3 us -> 34.7 us
  waiting for transfers between devices: 24.8 us -> 26.9 us
    ppermute x15, waiting for transfers between devices: 10 us -> 12.3 us  [paired(): lax.ppermute(block, 'ctx', [(i, i ^ distance) for i in range(lax.axis_siz...]
    pallas_call x1 -> x0, Pallas kernels: 1.7 us -> none  [kernel_plan(): pl.pallas_call(seam_kernel, grid=(1,), in_specs=[whole(16), whole(2), who...]
    unnamed x32 -> x26, local copies, waits for them, and re-layouts: 2.08 us -> 2.07 us
  transfers between devices with their start and end apart: 19 -> 19, of which waited for: 5 -> 7; matrix products, arithmetic and copies ran while one was open for 0% -> 1% of each run, Pallas kernels for 32% -> 30%
where the time goes in v7:
time: 102 us; the launch traced here: 101 us
  starting transfers between devices  35.1 us (34%)
  Pallas kernels  34.7 us (34%)
  waiting for transfers between devices  26.9 us (26%)
  local copies, waits for them, and re-layouts  2.09 us (2%)
  other arithmetic  1.37 us (1%)
    ppermute x15, starting transfers between devices, paired(): lax.ppermute(block, 'ctx', [(i, i ^ distance) for i in range(lax.axis_siz...  20 us
    all_to_all x2, waiting for transfers between devices, exchanged(): return lax.all_to_all(block, 'ctx', split_axis=0, concat_axis=0, tiled=True)  14.6 us
    ppermute x15, waiting for transfers between devices, paired(): lax.ppermute(block, 'ctx', [(i, i ^ distance) for i in range(lax.axis_siz...  12.3 us
    all_to_all x2, starting transfers between devices, exchanged(): return lax.all_to_all(block, 'ctx', split_axis=0, concat_axis=0, tiled=True)  11.5 us
    pallas_call x1, Pallas kernels, kernel_plan(): pl.pallas_call(functools.partial(conv_kernel, outer=outer, width=width),...  7.86 us
    pallas_call x1, Pallas kernels, kernel_plan(): pl.pallas_call(functools.partial(grad_kernel, outer=outer, width=width),...  7.72 us
    pallas_call x1, Pallas kernels, kernel_plan(): pl.pallas_call(functools.partial(filter_kernel, outer=outer, width=width)...  5.72 us
    pallas_call x1, Pallas kernels, kernel_plan(): pl.pallas_call(functools.partial(mix_kernel, width=width), grid=(steps,),...  4.06 us
  transfers between devices with their start and end apart: 19, of which 7 were waited for; matrix products, arithmetic and copies ran while one was open for 1% of the time, Pallas kernels for 30%

profile of v7, /device:TPU:0, one launch (start us, length us, event | category | flops | bytes accessed | tf_op | source)
XLA Modules:
  0.0 101.0 jit_solution(9844913773897482243)
XLA Ops:
  0.6 2.5 %gate.1 = (bf16[16,128,256]{2,1,0:T(8,128)(2,1)}, f32[2,4096]{1,0:T(2,128)}) custom-call(bf16[128,4096]{1,0:T(8,128)(2,1)} %grad_ref.3, bf16[128,4096]{1,0:T(8,128)(2,1)} %query_ref.1, bf16[128,4096]{1,0:T(8,128)(2,1)} %value_ref.7), custom_call_target="tpu_custom_call" | custom-call | flops 524288 | bytes 3145728 | tf_op jit(solution)/shard_map/gate/pallas_call | solution.py:610
  3.1 2.3 %collective-permute-start = (f32[2,4096]{1,0:T(2,128)}, f32[2,4096]{1,0:T(2,128)S(1)}, u32[]{:S(2)}, u32[]{:S(2)}) collective-permute-start(f32[2,4096]{1,0:T(2,128)} %get-tuple-element.41), channel_id=1, source_target_pairs={{0,1},{1,2},{2,3},{3,4},{4,5},{5,6},{6,7},{7,8},{8,9},{9,10},{10,1... | collective-permute-start | bytes 98312 | tf_op jit(solution)/shard_map/ppermute | solution.py:18
  5.5 7.3 %all-to-all-start = ((bf16[16,128,256]{2,1,0:T(8,128)(2,1)}), bf16[16,128,256]{2,1,0:T(8,128)(2,1)}, u32[]{:S(2)}, u32[]{:S(2)}) async-start(bf16[16,128,256]{2,1,0:T(8,128)(2,1)} %get-tuple-element.50), calls=%async_computation | async-start | bytes 2097152 | tf_op jit(solution)/shard_map/all_to_all | solution.py:546
  12.7 0.0 collective-permute-done.edge_ref
  12.7 0.0 copy-start.2
  12.8 0.6 copy-done.2
  13.3 4.1 %mix.1 = (bf16[4,128,256]{2,1,0:T(8,128)(2,1)}, bf16[4,128,256]{2,1,0:T(8,128)(2,1)}, bf16[4,128,256]{2,1,0:T(8,128)(2,1)}, bf16[128,256]{1,0:T(8,128)(2,1)}, bf...) custom-call(bf16[128,4096]{1,0:T(8,128)(2,1)} %key_ref.5, ...), custom_call_target="tpu_custom_call" | custom-call | flops 40000000000 | bytes 6291456 | tf_op jit(solution)/shard_map/mix/pallas_call | solution.py:635
  17.4 0.4 collective-permute-start.1
  17.8 1.7 %collective-permute-start.2 = (bf16[4,128,256]{2,1,0:T(8,128)(2,1)}, bf16[4,128,256]{2,1,0:T(8,128)(2,1)S(1)}, u32[]{:S(2)}, u32[]{:S(2)}) collective-permute-start(bf16[4,128,256]{2,1,0:T(8,128)(2,1)} %get-tuple-element.45), channel_id=1, source_target_pairs={{0,2},{1,3},{2,0},{3,1},{4,6},{5,7},{6,4},{7,5},{8,10},{9,11},{10,... | collective-permute-start | bytes 786440 | tf_op jit(solution)/shard_map/ppermute | solution.py:550
  19.5 0.0 collective-permute-start.3
  19.5 1.7 %collective-permute-start.4 = (bf16[128,256]{1,0:T(8,128)(2,1)}, bf16[128,256]{1,0:T(8,128)(2,1)S(1)}, u32[]{:S(2)}, u32[]{:S(2)}) collective-permute-start(bf16[128,256]{1,0:T(8,128)(2,1)} %get-tuple-element.55), channel_id=1, source_target_pairs={{0,4},{1,5},{2,6},{3,7},{4,0},{5,1},{6,2},{7,3},{8,12},{9,13},{10,... | collective-permute-start | bytes 196616 | tf_op jit(solution)/shard_map/ppermute | solution.py:550
  21.2 2.4 %collective-permute-start.5 = (bf16[128,256]{1,0:T(8,128)(2,1)}, bf16[128,256]{1,0:T(8,128)(2,1)S(1)}, u32[]{:S(2)}, u32[]{:S(2)}) collective-permute-start(bf16[128,256]{1,0:T(8,128)(2,1)} %get-tuple-element.56), channel_id=1, source_target_pairs={{0,8},{1,9},{2,10},{3,11},{4,12},{5,13},{6,14},{7,15},{8,0},{9,1},... | collective-permute-start | bytes 196616 | tf_op jit(solution)/shard_map/ppermute | solution.py:550
  23.6 5.7 %filter_spectrum.1.filter_hbm = bf16[17,256,256]{2,1,0:T(8,128)(2,1)} custom-call(bf16[256,2048]{1,0:T(8,128)(2,1)} %taps_ref, bf16[17,256,256]{2,1,0:T(8,128)(2,1)} %constant.36.clone.ahead_ref.ahead_hbm.refs_12_), custom_call_target="tpu_custom_call" | custom-call | flops 40000000000 | bytes 5505024 | tf_op jit(solution)/shard_map/filter_spectrum/pallas_call | solution.py:662
  29.3 0.0 collective-permute-done.1.refs_0_.refs_4_
  29.3 0.3 collective-permute-start.6
  29.6 1.8 %collective-permute-done.2.refs_1_.refs_5_ = bf16[4,128,256]{2,1,0:T(8,128)(2,1)S(1)} collective-permute-done((bf16[4,128,256]{2,1,0:T(8,128)(2,1)}, bf16[4,128,256]{2,1,0:T(8,128)(2,1)S(1)}, u32[]{:S(2)}, u32[]{:S(2)}) %collective-permute-start.2) | collective-permute-done | bytes 262176 | tf_op jit(solution)/shard_map/ppermute | solution.py:550
  31.4 6.4 %collective-permute-done.3.refs_2_.refs_6_ = bf16[4,128,256]{2,1,0:T(8,128)(2,1)S(1)} collective-permute-done((bf16[4,128,256]{2,1,0:T(8,128)(2,1)}, bf16[4,128,256]{2,1,0:T(8,128)(2,1)S(1)}, u32[]{:S(2)}, u32[]{:S(2)}) %collective-permute-start.3) | collective-permute-done | bytes 262176 | tf_op jit(solution)/shard_map/ppermute | solution.py:550
  37.8 0.0 copy-done.5
  37.8 0.0 copy-done.6
  37.8 0.7 copy-done.7
  38.5 2.0 %regroup.1 = (bf16[3,128,256]{2,1,0:T(8,128)(2,1)}, bf16[3,128,256]{2,1,0:T(8,128)(2,1)}, bf16[3,128,256]{2,1,0:T(8,128)(2,1)}) custom-call(bf16[4,128,256]{2,1,0:T(8,128)(2,1)} %copy-done.5, bf16[4,128,256]{2,1,0:T(8,128)(2,1)} %copy-done.6, bf16[4,128,256]{2,1,0:T(8,128)(2,1)} %copy-done.7), custom_call_target="tpu_custom_call" | custom-call | bytes 2097152 | tf_op jit(solution)/shard_map/regroup/pallas_call | solution.py:651
  40.5 0.0 all-to-all-done
  40.5 1.3 %collective-permute-start.7 = (bf16[3,128,256]{2,1,0:T(8,128)(2,1)}, bf16[3,128,256]{2,1,0:T(8,128)(2,1)S(1)}, u32[]{:S(2)}, u32[]{:S(2)}) collective-permute-start(bf16[3,128,256]{2,1,0:T(8,128)(2,1)} %get-tuple-element.58), channel_id=1, source_target_pairs={{0,4},{1,5},{2,6},{3,7},{4,0},{5,1},{6,2},{7,3},{8,12},{9,13},{10,... | collective-permute-start | bytes 589832 | tf_op jit(solution)/shard_map/ppermute | solution.py:550
  41.7 2.3 %collective-permute-start.8 = (bf16[3,128,256]{2,1,0:T(8,128)(2,1)}, bf16[3,128,256]{2,1,0:T(8,128)(2,1)S(1)}, u32[]{:S(2)}, u32[]{:S(2)}) collective-permute-start(bf16[3,128,256]{2,1,0:T(8,128)(2,1)} %get-tuple-element.59), channel_id=1, source_target_pairs={{0,8},{1,9},{2,10},{3,11},{4,12},{5,13},{6,14},{7,15},{8,0},{9,1},... | collective-permute-start | bytes 589832 | tf_op jit(solution)/shard_map/ppermute | solution.py:550
  44.1 0.0 collective-permute-done.4.refs_1_
  44.1 1.5 %collective-permute-start.9 = (bf16[3,128,256]{2,1,0:T(8,128)(2,1)}, bf16[3,128,256]{2,1,0:T(8,128)(2,1)S(1)}, u32[]{:S(2)}, u32[]{:S(2)}) collective-permute-start(bf16[3,128,256]{2,1,0:T(8,128)(2,1)} %get-tuple-element.60), channel_id=1, source_target_pairs={{0,12},{1,13},{2,14},{3,15},{4,8},{5,9},{6,10},{7,11},{8,4},{9,5},... | collective-permute-start | bytes 589832 | tf_op jit(solution)/shard_map/ppermute | solution.py:550
  45.6 7.9 %conv_back.1 = (bf16[2048,256]{1,0:T(8,128)(2,1)}, bf16[17,256,256]{2,1,0:T(8,128)(2,1)}) custom-call(bf16[2048,256]{1,0:T(8,128)(2,1)} %bitcast.gated_hbm.refs_10_, bf16[17,256,256]{2,1,0:T(8,128)(2,1)} %filter_spectrum.1.filter_hbm, bf16[17,256,256]{2,1,0:T(8,128)(2,1)} %constant.36.clone.ahead_ref.ahead_hbm.refs_12_, ...), custom_call_target="tpu_custom_call" | custom-call | flops 40000000000 | bytes 11010048 | tf_op jit(solution)/shard_map/conv_back/pallas_call | solution.py:675
  53.5 0.0 copy-done.11
  53.5 4.2 %all-to-all-start.1 = ((bf16[16,128,256]{2,1,0:T(8,128)(2,1)}), bf16[16,128,256]{2,1,0:T(8,128)(2,1)S(1)}, u32[]{:S(2)}, u32[]{:S(2)}) async-start(bf16[16,128,256]{2,1,0:T(8,128)(2,1)} %bitcast.12), calls=%async_computation.1 | async-start | bytes 2097152 | tf_op jit(solution)/shard_map/all_to_all | solution.py:546
  57.7 0.0 collective-permute-done.5.refs_2_
  57.7 0.0 copy-start.12
  57.7 0.0 collective-permute-done.6.refs_3_
  57.7 0.0 collective-permute-done.7.refs_7_
  57.7 0.0 copy-start.8
  57.7 1.3 %collective-permute-done.8.refs_8_ = bf16[3,128,256]{2,1,0:T(8,128)(2,1)S(1)} collective-permute-done((bf16[3,128,256]{2,1,0:T(8,128)(2,1)}, bf16[3,128,256]{2,1,0:T(8,128)(2,1)S(1)}, u32[]{:S(2)}, u32[]{:S(2)}) %collective-permute-start.8) | collective-permute-done | bytes 196640 | tf_op jit(solution)/shard_map/ppermute | solution.py:550
  59.0 0.0 collective-permute-done.9.refs_9_
  59.0 0.0 copy-done.12
  59.0 0.7 copy-done.9
  59.7 0.1 copy-done.10
  59.8 0.0 copy-done.8
  59.8 7.7 %filter_grad.1 = (bf16[256,2048]{1,0:T(8,128)(2,1)}, f32[1,256]{1,0:T(1,128)}) custom-call(bf16[128,256]{1,0:T(8,128)(2,1)} %get-tuple-element.54.refs_0_, bf16[128,256]{1,0:T(8,128)(2,1)} %copy-done.11, bf16[128,256]{1,0:T(8,128)(2,1)} %copy-done.12, bf16[128,256]{1,0:T(8,128)(2,1)} %collective-permute-done.6.refs_3_, bf16[4,128,256]{2,1,0:T(8,128)(2,1)} %copy-done.5, ...), custom_call_target="tpu_custom_call" | custom-call | flops 99999997952 | bytes 6684672 | tf_op jit(solution)/shard_map/filter_grad/pallas_call | solution.py:689
  67.5 0.0 copy-start.4
  67.5 14.6 %all-to-all-done.1.back_ref = bf16[16,128,256]{2,1,0:T(8,128)(2,1)S(1)} async-done(((bf16[16,128,256]{2,1,0:T(8,128)(2,1)}), bf16[16,128,256]{2,1,0:T(8,128)(2,1)S(1)}, u32[]{:S(2)}, u32[]{:S(2)}) %all-to-all-start.1) | async-done | bytes 1048608 | tf_op jit(solution)/shard_map/all_to_all | solution.py:546
  82.1 0.0 copy-done
  82.1 0.0 copy-done.1
  82.1 0.0 copy-done.3
  82.2 1.9 %sums.1 = (f32[2,4096]{1,0:T(2,128)}, f32[4,8,256]{2,1,0:T(8,128)}, f32[4,8,256]{2,1,0:T(8,128)}, f32[4,8,256]{2,1,0:T(8,128)}, f32[4,8,256]{2,1,0:T(8,128)}) custom-call(bf16[16,128,256]{2,1,0:T(8,128)(2,1)S(1)} %all-to-all-done.1.back_ref, bf16[128,4096]{1,0:T(8,128)(2,1)S(1)} %copy-done.1, bf16[128,4096]{1,0:T(8,128)(2,1)S(1)} %copy-done, ...), custom_call_target="tpu_custom_call" | custom-call | flops 10485760 | bytes 4194304 | tf_op jit(solution)/shard_map/sums/pallas_call | solution.py:710
  84.1 2.7 %collective-permute-start.12 = (f32[4,8,256]{2,1,0:T(8,128)}, f32[4,8,256]{2,1,0:T(8,128)S(1)}, u32[]{:S(2)}, u32[]{:S(2)}) collective-permute-start(f32[4,8,256]{2,1,0:T(8,128)} %get-tuple-element.68), channel_id=1, source_target_pairs={{0,12},{1,13},{2,14},{3,15},{4,8},{5,9},{6,10},{7,11},{8,4},{9,5},... | collective-permute-start | bytes 98312 | tf_op jit(solution)/shard_map/ppermute | solution.py:550
  86.8 2.6 %collective-permute-start.11 = (f32[4,8,256]{2,1,0:T(8,128)}, f32[4,8,256]{2,1,0:T(8,128)S(1)}, u32[]{:S(2)}, u32[]{:S(2)}) collective-permute-start(f32[4,8,256]{2,1,0:T(8,128)} %get-tuple-element.67), channel_id=1, source_target_pairs={{0,8},{1,9},{2,10},{3,11},{4,12},{5,13},{6,14},{7,15},{8,0},{9,1},... | collective-permute-start | bytes 98312 | tf_op jit(solution)/shard_map/ppermute | solution.py:550
  89.5 0.5 collective-permute-start.10
  90.0 1.3 %collective-permute-start.13 = (f32[2,4096]{1,0:T(2,128)}, f32[2,4096]{1,0:T(2,128)S(1)}, u32[]{:S(2)}, u32[]{:S(2)}) collective-permute-start(f32[2,4096]{1,0:T(2,128)} %get-tuple-element.69), channel_id=1, source_target_pairs={{1,0},{2,1},{3,2},{4,3},{5,4},{6,5},{7,6},{8,7},{9,8},{10,9},{11,1... | collective-permute-start | bytes 98312 | tf_op jit(solution)/shard_map/ppermute | solution.py:18
  91.2 0.0 collective-permute-done.12
  91.3 0.6 collective-permute-done.11
  91.9 1.7 %collective-permute-done.10 = f32[4,8,256]{2,1,0:T(8,128)S(1)} collective-permute-done((f32[4,8,256]{2,1,0:T(8,128)}, f32[4,8,256]{2,1,0:T(8,128)S(1)}, u32[]{:S(2)}, u32[]{:S(2)}) %collective-permute-start.10) | collective-permute-done | bytes 32800 | tf_op jit(solution)/shard_map/ppermute | solution.py:550
  93.6 0.8 add_add_fusion
  94.4 0.0 collective-permute-done.13.next_ref
  94.4 2.4 %collective-permute-start.16 = (f32[8,256]{1,0:T(8,128)S(1)}, f32[8,256]{1,0:T(8,128)S(1)}, u32[]{:S(2)}, u32[]{:S(2)}) collective-permute-start(f32[8,256]{1,0:T(8,128)S(1)} %get-tuple-element.77), channel_id=1, source_target_pairs={{0,3},{1,2},{2,1},{3,0},{4,7},{5,6},{6,5},{7,4},{8,11},{9,10},{10,... | collective-permute-start | bytes 24584 | tf_op jit(solution)/shard_map/ppermute | solution.py:550
  96.7 0.0 collective-permute-start.15
  96.7 0.2 collective-permute-start.14
  96.9 2.9 %finish.1 = (bf16[128,4096]{1,0:T(8,128)(2,1)}, bf16[128,4096]{1,0:T(8,128)(2,1)}) custom-call(bf16[16,128,256]{2,1,0:T(8,128)(2,1)S(1)} %all-to-all-done.1.back_ref, bf16[128,4096]{1,0:T(8,128)(2,1)S(1)} %copy-done.1, bf16[128,4096]{1,0:T(8,128)(2,1)S(1)} %copy-done, f32[2,4096]{1,0:T(2,128)S(1)} %copy-done.3, ...), custom_call_target="tpu_custom_call" | custom-call | flops 15728640 | bytes 6291456 | tf_op jit(solution)/shard_map/finish/pallas_call | solution.py:726
  99.8 0.0 collective-permute-done.16
  99.8 0.5 collective-permute-done.15
  100.4 0.0 collective-permute-done.14
  100.4 0.6 slice_add_fusion
  (11 shorter events, 0.0 us)
Async XLA Ops:
  3.1 9.6 %collective-permute-start = (f32[2,4096]{1,0:T(2,128)}, f32[2,4096]{1,0:T(2,128)S(1)}, u32[]{:S(2)}, u32[]{:S(2)}) collective-permute-start(f32[2,4096]{1,0:T(2,128)} %get-tuple-element.41), channel_id=1, source_target_pairs={{0,1},{1,2},{2,3},{3,4},{4,5},{5,6},{6,7},{7,8},{8,9},{9,10},{10,1... | collective-permute-start | bytes 98312 | tf_op jit(solution)/shard_map/ppermute | solution.py:18
  5.5 35.0 %all-to-all-start = ((bf16[16,128,256]{2,1,0:T(8,128)(2,1)}), bf16[16,128,256]{2,1,0:T(8,128)(2,1)}, u32[]{:S(2)}, u32[]{:S(2)}) async-start(bf16[16,128,256]{2,1,0:T(8,128)(2,1)} %get-tuple-element.50), calls=%async_computation | async-start | bytes 2097152 | tf_op jit(solution)/shard_map/all_to_all | solution.py:546
  12.7 0.6 copy-start.2
  17.4 11.9 %collective-permute-start.1 = (bf16[4,128,256]{2,1,0:T(8,128)(2,1)}, bf16[4,128,256]{2,1,0:T(8,128)(2,1)S(1)}, u32[]{:S(2)}, u32[]{:S(2)}) collective-permute-start(bf16[4,128,256]{2,1,0:T(8,128)(2,1)} %get-tuple-element.44), channel_id=1, source_target_pairs={{0,1},{1,0},{2,3},{3,2},{4,5},{5,4},{6,7},{7,6},{8,9},{9,8},{10,11... | collective-permute-start | bytes 786440 | tf_op jit(solution)/shard_map/ppermute | solution.py:550
  17.8 13.6 %collective-permute-start.2 = (bf16[4,128,256]{2,1,0:T(8,128)(2,1)}, bf16[4,128,256]{2,1,0:T(8,128)(2,1)S(1)}, u32[]{:S(2)}, u32[]{:S(2)}) collective-permute-start(bf16[4,128,256]{2,1,0:T(8,128)(2,1)} %get-tuple-element.45), channel_id=1, source_target_pairs={{0,2},{1,3},{2,0},{3,1},{4,6},{5,7},{6,4},{7,5},{8,10},{9,11},{10,... | collective-permute-start | bytes 786440 | tf_op jit(solution)/shard_map/ppermute | solution.py:550
  19.5 18.3 %collective-permute-start.3 = (bf16[4,128,256]{2,1,0:T(8,128)(2,1)}, bf16[4,128,256]{2,1,0:T(8,128)(2,1)S(1)}, u32[]{:S(2)}, u32[]{:S(2)}) collective-permute-start(bf16[4,128,256]{2,1,0:T(8,128)(2,1)} %get-tuple-element.46), channel_id=1, source_target_pairs={{0,3},{1,2},{2,1},{3,0},{4,7},{5,6},{6,5},{7,4},{8,11},{9,10},{10,... | collective-permute-start | bytes 786440 | tf_op jit(solution)/shard_map/ppermute | solution.py:550
  19.5 24.6 %collective-permute-start.4 = (bf16[128,256]{1,0:T(8,128)(2,1)}, bf16[128,256]{1,0:T(8,128)(2,1)S(1)}, u32[]{:S(2)}, u32[]{:S(2)}) collective-permute-start(bf16[128,256]{1,0:T(8,128)(2,1)} %get-tuple-element.55), channel_id=1, source_target_pairs={{0,4},{1,5},{2,6},{3,7},{4,0},{5,1},{6,2},{7,3},{8,12},{9,13},{10,... | collective-permute-start | bytes 196616 | tf_op jit(solution)/shard_map/ppermute | solution.py:550
  21.2 36.5 %collective-permute-start.5 = (bf16[128,256]{1,0:T(8,128)(2,1)}, bf16[128,256]{1,0:T(8,128)(2,1)S(1)}, u32[]{:S(2)}, u32[]{:S(2)}) collective-permute-start(bf16[128,256]{1,0:T(8,128)(2,1)} %get-tuple-element.56), channel_id=1, source_target_pairs={{0,8},{1,9},{2,10},{3,11},{4,12},{5,13},{6,14},{7,15},{8,0},{9,1},... | collective-permute-start | bytes 196616 | tf_op jit(solution)/shard_map/ppermute | solution.py:550
  29.3 8.5 %copy-start.5 = (bf16[4,128,256]{2,1,0:T(8,128)(2,1)}, bf16[4,128,256]{2,1,0:T(8,128)(2,1)S(1)}, u32[]{:S(2)}) copy-start(bf16[4,128,256]{2,1,0:T(8,128)(2,1)S(1)} %collective-permute-done.1.refs_0_.refs_4_) | copy-start | bytes 786436
  29.3 28.4 %collective-permute-start.6 = (bf16[128,256]{1,0:T(8,128)(2,1)}, bf16[128,256]{1,0:T(8,128)(2,1)}, u32[]{:S(2)}, u32[]{:S(2)}) collective-permute-start(bf16[128,256]{1,0:T(8,128)(2,1)} %get-tuple-element.57), channel_id=1, source_target_pairs={{0,12},{1,13},{2,14},{3,15},{4,8},{5,9},{6,10},{7,11},{8,4},{9,5},... | collective-permute-start | bytes 196616 | tf_op jit(solution)/shard_map/ppermute | solution.py:550
  31.4 6.4 %copy-start.6 = (bf16[4,128,256]{2,1,0:T(8,128)(2,1)}, bf16[4,128,256]{2,1,0:T(8,128)(2,1)S(1)}, u32[]{:S(2)}) copy-start(bf16[4,128,256]{2,1,0:T(8,128)(2,1)S(1)} %collective-permute-done.2.refs_1_.refs_5_) | copy-start | bytes 786436
  37.8 0.7 copy-start.7
  40.5 17.3 %collective-permute-start.7 = (bf16[3,128,256]{2,1,0:T(8,128)(2,1)}, bf16[3,128,256]{2,1,0:T(8,128)(2,1)S(1)}, u32[]{:S(2)}, u32[]{:S(2)}) collective-permute-start(bf16[3,128,256]{2,1,0:T(8,128)(2,1)} %get-tuple-element.58), channel_id=1, source_target_pairs={{0,4},{1,5},{2,6},{3,7},{4,0},{5,1},{6,2},{7,3},{8,12},{9,13},{10,... | collective-permute-start | bytes 589832 | tf_op jit(solution)/shard_map/ppermute | solution.py:550
  41.7 17.3 %collective-permute-start.8 = (bf16[3,128,256]{2,1,0:T(8,128)(2,1)}, bf16[3,128,256]{2,1,0:T(8,128)(2,1)S(1)}, u32[]{:S(2)}, u32[]{:S(2)}) collective-permute-start(bf16[3,128,256]{2,1,0:T(8,128)(2,1)} %get-tuple-element.59), channel_id=1, source_target_pairs={{0,8},{1,9},{2,10},{3,11},{4,12},{5,13},{6,14},{7,15},{8,0},{9,1},... | collective-permute-start | bytes 589832 | tf_op jit(solution)/shard_map/ppermute | solution.py:550
  44.1 9.4 %copy-start.11 = (bf16[128,256]{1,0:T(8,128)(2,1)}, bf16[128,256]{1,0:T(8,128)(2,1)S(1)}, u32[]{:S(2)}) copy-start(bf16[128,256]{1,0:T(8,128)(2,1)S(1)} %collective-permute-done.4.refs_1_) | copy-start | bytes 196612
  44.1 14.9 %collective-permute-start.9 = (bf16[3,128,256]{2,1,0:T(8,128)(2,1)}, bf16[3,128,256]{2,1,0:T(8,128)(2,1)S(1)}, u32[]{:S(2)}, u32[]{:S(2)}) collective-permute-start(bf16[3,128,256]{2,1,0:T(8,128)(2,1)} %get-tuple-element.60), channel_id=1, source_target_pairs={{0,12},{1,13},{2,14},{3,15},{4,8},{5,9},{6,10},{7,11},{8,4},{9,5},... | collective-permute-start | bytes 589832 | tf_op jit(solution)/shard_map/ppermute | solution.py:550
  53.5 28.7 %all-to-all-start.1 = ((bf16[16,128,256]{2,1,0:T(8,128)(2,1)}), bf16[16,128,256]{2,1,0:T(8,128)(2,1)S(1)}, u32[]{:S(2)}, u32[]{:S(2)}) async-start(bf16[16,128,256]{2,1,0:T(8,128)(2,1)} %bitcast.12), calls=%async_computation.1 | async-start | bytes 2097152 | tf_op jit(solution)/shard_map/all_to_all | solution.py:546
  57.7 1.3 %copy-start.12 = (bf16[128,256]{1,0:T(8,128)(2,1)}, bf16[128,256]{1,0:T(8,128)(2,1)S(1)}, u32[]{:S(2)}) copy-start(bf16[128,256]{1,0:T(8,128)(2,1)S(1)} %collective-permute-done.5.refs_2_) | copy-start | bytes 196612
  57.7 2.0 %copy-start.8 = (bf16[3,128,256]{2,1,0:T(8,128)(2,1)}, bf16[3,128,256]{2,1,0:T(8,128)(2,1)S(1)}, u32[]{:S(2)}) copy-start(bf16[3,128,256]{2,1,0:T(8,128)(2,1)S(1)} %collective-permute-done.7.refs_7_) | copy-start | bytes 589828
  59.0 0.7 copy-start.9
  59.0 0.8 copy-start.10
  59.8 22.4 %copy-start = (bf16[128,4096]{1,0:T(8,128)(2,1)S(1)}, bf16[128,4096]{1,0:T(8,128)(2,1)}, u32[]{:S(2)}) copy-start(bf16[128,4096]{1,0:T(8,128)(2,1)} %value_ref.7) | copy-start | bytes 3145732
  59.8 22.4 %copy-start.1 = (bf16[128,4096]{1,0:T(8,128)(2,1)S(1)}, bf16[128,4096]{1,0:T(8,128)(2,1)}, u32[]{:S(2)}) copy-start(bf16[128,4096]{1,0:T(8,128)(2,1)} %key_ref.5) | copy-start | bytes 3145732
  59.8 22.4 %copy-start.3 = (f32[2,4096]{1,0:T(2,128)S(1)}, f32[2,4096]{1,0:T(2,128)}, u32[]{:S(2)}) copy-start(f32[2,4096]{1,0:T(2,128)} %copy-done.2) | copy-start | bytes 98308
  67.5 29.4 %copy-start.4 = (f32[3,4096]{1,0:T(4,128)S(1)}, f32[3,4096]{1,0:T(4,128)}, u32[]{:S(2)}) copy-start(f32[3,4096]{1,0:T(4,128)} %short_ref.3) | copy-start | bytes 147460
  84.1 7.2 %collective-permute-start.12 = (f32[4,8,256]{2,1,0:T(8,128)}, f32[4,8,256]{2,1,0:T(8,128)S(1)}, u32[]{:S(2)}, u32[]{:S(2)}) collective-permute-start(f32[4,8,256]{2,1,0:T(8,128)} %get-tuple-element.68), channel_id=1, source_target_pairs={{0,12},{1,13},{2,14},{3,15},{4,8},{5,9},{6,10},{7,11},{8,4},{9,5},... | collective-permute-start | bytes 98312 | tf_op jit(solution)/shard_map/ppermute | solution.py:550
  86.8 5.0 %collective-permute-start.11 = (f32[4,8,256]{2,1,0:T(8,128)}, f32[4,8,256]{2,1,0:T(8,128)S(1)}, u32[]{:S(2)}, u32[]{:S(2)}) collective-permute-start(f32[4,8,256]{2,1,0:T(8,128)} %get-tuple-element.67), channel_id=1, source_target_pairs={{0,8},{1,9},{2,10},{3,11},{4,12},{5,13},{6,14},{7,15},{8,0},{9,1},... | collective-permute-start | bytes 98312 | tf_op jit(solution)/shard_map/ppermute | solution.py:550
  89.5 4.1 %collective-permute-start.10 = (f32[4,8,256]{2,1,0:T(8,128)}, f32[4,8,256]{2,1,0:T(8,128)S(1)}, u32[]{:S(2)}, u32[]{:S(2)}) collective-permute-start(f32[4,8,256]{2,1,0:T(8,128)} %get-tuple-element.66), channel_id=1, source_target_pairs={{0,4},{1,5},{2,6},{3,7},{4,0},{5,1},{6,2},{7,3},{8,12},{9,13},{10,... | collective-permute-start | bytes 98312 | tf_op jit(solution)/shard_map/ppermute | solution.py:550
  90.0 4.4 %collective-permute-start.13 = (f32[2,4096]{1,0:T(2,128)}, f32[2,4096]{1,0:T(2,128)S(1)}, u32[]{:S(2)}, u32[]{:S(2)}) collective-permute-start(f32[2,4096]{1,0:T(2,128)} %get-tuple-element.69), channel_id=1, source_target_pairs={{1,0},{2,1},{3,2},{4,3},{5,4},{6,5},{7,6},{8,7},{9,8},{10,9},{11,1... | collective-permute-start | bytes 98312 | tf_op jit(solution)/shard_map/ppermute | solution.py:18
  94.4 5.5 %collective-permute-start.16 = (f32[8,256]{1,0:T(8,128)S(1)}, f32[8,256]{1,0:T(8,128)S(1)}, u32[]{:S(2)}, u32[]{:S(2)}) collective-permute-start(f32[8,256]{1,0:T(8,128)S(1)} %get-tuple-element.77), channel_id=1, source_target_pairs={{0,3},{1,2},{2,1},{3,0},{4,7},{5,6},{6,5},{7,4},{8,11},{9,10},{10,... | collective-permute-start | bytes 24584 | tf_op jit(solution)/shard_map/ppermute | solution.py:550
  96.7 3.7 %collective-permute-start.15 = (f32[8,256]{1,0:T(8,128)S(1)}, f32[8,256]{1,0:T(8,128)S(1)}, u32[]{:S(2)}, u32[]{:S(2)}) collective-permute-start(f32[8,256]{1,0:T(8,128)S(1)} %get-tuple-element.78), channel_id=1, source_target_pairs={{0,2},{1,3},{2,0},{3,1},{4,6},{5,7},{6,4},{7,5},{8,10},{9,11},{10,... | collective-permute-start | bytes 24584 | tf_op jit(solution)/shard_map/ppermute | solution.py:550
  96.7 3.7 %collective-permute-start.14 = (f32[8,256]{1,0:T(8,128)S(1)}, f32[8,256]{1,0:T(8,128)S(1)}, u32[]{:S(2)}, u32[]{:S(2)}) collective-permute-start(f32[8,256]{1,0:T(8,128)S(1)} %get-tuple-element.79), channel_id=1, source_target_pairs={{0,1},{1,0},{2,3},{3,2},{4,5},{5,4},{6,7},{7,6},{8,9},{9,8},{10,11... | collective-permute-start | bytes 24584 | tf_op jit(solution)/shard_map/ppermute | solution.py:550

commit v8 on v7

--- a/solution.py
+++ b/solution.py
@@ -550,16 +550,15 @@
     return lax.ppermute(block, "ctx", [(i, i ^ distance) for i in range(lax.axis_size("ctx"))])
 
 
-def summed_at_owner(parts, *beside):
+def summed_at_owner(parts):
     place = lax.axis_index("ctx") % INNER_PEERS
     got = [parts[0]] + [paired(parts[d], d * INNER_PEERS) for d in range(1, len(parts))]
     rows = sum(got[1:], got[0])
-    rows, beside = lax.optimization_barrier((rows, beside))
     total = lax.dynamic_index_in_dim(rows, place, 0, keepdims=False)
     for distance in range(1, INNER_PEERS):
         other = lax.dynamic_index_in_dim(rows, place ^ distance, 0, keepdims=False)
         total = total + paired(other, distance)
-    return total, *beside
+    return total
 
 
 def after(value, *others):
@@ -722,7 +721,7 @@
     )(back_got, key_feat, value_raw, edge)
 
     head_got = passed_along(head, "ctx", -1)
-    short_grad, head_got = summed_at_owner(short_parts, head_got)
+    short_grad = summed_at_owner(short_parts)
     key_grad, value_grad = pl.pallas_call(
         functools.partial(finish_kernel, width=width),
         grid=(steps,),

time: 102 us -> 100 us (0.980)
  transfers between devices with their start and end apart: 19 -> 19, of which waited for: 7 -> 6; matrix products, arithmetic and copies ran while one was open for 1% -> 1% of each run, Pallas kernels for 30% -> 30%
where the time goes in v8:
time: 100 us; the launch traced here: 99.8 us
  Pallas kernels  34.7 us (35%)
  starting transfers between devices  34.5 us (34%)
  waiting for transfers between devices  26.4 us (26%)
  local copies, waits for them, and re-layouts  2.09 us (2%)
  other arithmetic  1.37 us (1%)
    ppermute x15, starting transfers between devices, paired(): lax.ppermute(block, 'ctx', [(i, i ^ distance) for i in range(lax.axis_siz...  19.4 us
    all_to_all x2, waiting for transfers between devices, exchanged(): return lax.all_to_all(block, 'ctx', split_axis=0, concat_axis=0, tiled=True)  14.6 us
    ppermute x15, waiting for transfers between devices, paired(): lax.ppermute(block, 'ctx', [(i, i ^ distance) for i in range(lax.axis_siz...  11.8 us
    all_to_all x2, starting transfers between devices, exchanged(): return lax.all_to_all(block, 'ctx', split_axis=0, concat_axis=0, tiled=True)  11.5 us
    pallas_call x1, Pallas kernels, kernel_plan(): pl.pallas_call(functools.partial(conv_kernel, outer=outer, width=width),...  7.86 us
    pallas_call x1, Pallas kernels, kernel_plan(): pl.pallas_call(functools.partial(grad_kernel, outer=outer, width=width),...  7.72 us
    pallas_call x1, Pallas kernels, kernel_plan(): pl.pallas_call(functools.partial(filter_kernel, outer=outer, width=width)...  5.72 us
    pallas_call x1, Pallas kernels, kernel_plan(): pl.pallas_call(functools.partial(mix_kernel, width=width), grid=(steps,),...  4.06 us
  transfers between devices with their start and end apart: 19, of which 6 were waited for; matrix products, arithmetic and copies ran while one was open for 1% of the time, Pallas kernels for 30%

profile of v8, /device:TPU:0, one launch (start us, length us, event | category | flops | bytes accessed | tf_op | source)
XLA Modules:
  0.0 99.8 jit_solution(16020207206316142683)
XLA Ops:
  0.6 2.5 %gate.1 = (bf16[16,128,256]{2,1,0:T(8,128)(2,1)}, f32[2,4096]{1,0:T(2,128)}) custom-call(bf16[128,4096]{1,0:T(8,128)(2,1)} %grad_ref.3, bf16[128,4096]{1,0:T(8,128)(2,1)} %query_ref.1, bf16[128,4096]{1,0:T(8,128)(2,1)} %value_ref.7), custom_call_target="tpu_custom_call" | custom-call | flops 524288 | bytes 3145728 | tf_op jit(solution)/shard_map/gate/pallas_call | solution.py:609
  3.1 2.3 %collective-permute-start = (f32[2,4096]{1,0:T(2,128)}, f32[2,4096]{1,0:T(2,128)S(1)}, u32[]{:S(2)}, u32[]{:S(2)}) collective-permute-start(f32[2,4096]{1,0:T(2,128)} %get-tuple-element.39), channel_id=1, source_target_pairs={{0,1},{1,2},{2,3},{3,4},{4,5},{5,6},{6,7},{7,8},{8,9},{9,10},{10,1... | collective-permute-start | bytes 98312 | tf_op jit(solution)/shard_map/ppermute | solution.py:18
  5.5 7.3 %all-to-all-start = ((bf16[16,128,256]{2,1,0:T(8,128)(2,1)}), bf16[16,128,256]{2,1,0:T(8,128)(2,1)}, u32[]{:S(2)}, u32[]{:S(2)}) async-start(bf16[16,128,256]{2,1,0:T(8,128)(2,1)} %get-tuple-element.48), calls=%async_computation | async-start | bytes 2097152 | tf_op jit(solution)/shard_map/all_to_all | solution.py:546
  12.7 0.0 collective-permute-done.edge_ref
  12.7 0.0 copy-start.2
  12.8 0.6 copy-done.2
  13.3 4.1 %mix.1 = (bf16[4,128,256]{2,1,0:T(8,128)(2,1)}, bf16[4,128,256]{2,1,0:T(8,128)(2,1)}, bf16[4,128,256]{2,1,0:T(8,128)(2,1)}, bf16[128,256]{1,0:T(8,128)(2,1)}, bf...) custom-call(bf16[128,4096]{1,0:T(8,128)(2,1)} %key_ref.5, ...), custom_call_target="tpu_custom_call" | custom-call | flops 40000000000 | bytes 6291456 | tf_op jit(solution)/shard_map/mix/pallas_call | solution.py:634
  17.4 0.4 collective-permute-start.1
  17.8 1.7 %collective-permute-start.2 = (bf16[4,128,256]{2,1,0:T(8,128)(2,1)}, bf16[4,128,256]{2,1,0:T(8,128)(2,1)S(1)}, u32[]{:S(2)}, u32[]{:S(2)}) collective-permute-start(bf16[4,128,256]{2,1,0:T(8,128)(2,1)} %get-tuple-element.43), channel_id=1, source_target_pairs={{0,2},{1,3},{2,0},{3,1},{4,6},{5,7},{6,4},{7,5},{8,10},{9,11},{10,... | collective-permute-start | bytes 786440 | tf_op jit(solution)/shard_map/ppermute | solution.py:550
  19.5 0.0 collective-permute-start.3
  19.5 1.7 %collective-permute-start.4 = (bf16[128,256]{1,0:T(8,128)(2,1)}, bf16[128,256]{1,0:T(8,128)(2,1)S(1)}, u32[]{:S(2)}, u32[]{:S(2)}) collective-permute-start(bf16[128,256]{1,0:T(8,128)(2,1)} %get-tuple-element.53), channel_id=1, source_target_pairs={{0,4},{1,5},{2,6},{3,7},{4,0},{5,1},{6,2},{7,3},{8,12},{9,13},{10,... | collective-permute-start | bytes 196616 | tf_op jit(solution)/shard_map/ppermute | solution.py:550
  21.2 2.4 %collective-permute-start.5 = (bf16[128,256]{1,0:T(8,128)(2,1)}, bf16[128,256]{1,0:T(8,128)(2,1)S(1)}, u32[]{:S(2)}, u32[]{:S(2)}) collective-permute-start(bf16[128,256]{1,0:T(8,128)(2,1)} %get-tuple-element.54), channel_id=1, source_target_pairs={{0,8},{1,9},{2,10},{3,11},{4,12},{5,13},{6,14},{7,15},{8,0},{9,1},... | collective-permute-start | bytes 196616 | tf_op jit(solution)/shard_map/ppermute | solution.py:550
  23.6 5.7 %filter_spectrum.1.filter_hbm = bf16[17,256,256]{2,1,0:T(8,128)(2,1)} custom-call(bf16[256,2048]{1,0:T(8,128)(2,1)} %taps_ref, bf16[17,256,256]{2,1,0:T(8,128)(2,1)} %constant.36.clone.ahead_ref.ahead_hbm.refs_12_), custom_call_target="tpu_custom_call" | custom-call | flops 40000000000 | bytes 5505024 | tf_op jit(solution)/shard_map/filter_spectrum/pallas_call | solution.py:661
  29.3 0.0 collective-permute-done.1.refs_0_.refs_4_
  29.3 0.3 collective-permute-start.6
  29.6 1.8 %collective-permute-done.2.refs_1_.refs_5_ = bf16[4,128,256]{2,1,0:T(8,128)(2,1)S(1)} collective-permute-done((bf16[4,128,256]{2,1,0:T(8,128)(2,1)}, bf16[4,128,256]{2,1,0:T(8,128)(2,1)S(1)}, u32[]{:S(2)}, u32[]{:S(2)}) %collective-permute-start.2) | collective-permute-done | bytes 262176 | tf_op jit(solution)/shard_map/ppermute | solution.py:550
  31.4 6.4 %collective-permute-done.3.refs_2_.refs_6_ = bf16[4,128,256]{2,1,0:T(8,128)(2,1)S(1)} collective-permute-done((bf16[4,128,256]{2,1,0:T(8,128)(2,1)}, bf16[4,128,256]{2,1,0:T(8,128)(2,1)S(1)}, u32[]{:S(2)}, u32[]{:S(2)}) %collective-permute-start.3) | collective-permute-done | bytes 262176 | tf_op jit(solution)/shard_map/ppermute | solution.py:550
  37.8 0.0 copy-done.5
  37.8 0.0 copy-done.6
  37.8 0.7 copy-done.7
  38.5 2.0 %regroup.1 = (bf16[3,128,256]{2,1,0:T(8,128)(2,1)}, bf16[3,128,256]{2,1,0:T(8,128)(2,1)}, bf16[3,128,256]{2,1,0:T(8,128)(2,1)}) custom-call(bf16[4,128,256]{2,1,0:T(8,128)(2,1)} %copy-done.5, bf16[4,128,256]{2,1,0:T(8,128)(2,1)} %copy-done.6, bf16[4,128,256]{2,1,0:T(8,128)(2,1)} %copy-done.7), custom_call_target="tpu_custom_call" | custom-call | bytes 2097152 | tf_op jit(solution)/shard_map/regroup/pallas_call | solution.py:650
  40.5 0.0 all-to-all-done
  40.5 1.3 %collective-permute-start.7 = (bf16[3,128,256]{2,1,0:T(8,128)(2,1)}, bf16[3,128,256]{2,1,0:T(8,128)(2,1)S(1)}, u32[]{:S(2)}, u32[]{:S(2)}) collective-permute-start(bf16[3,128,256]{2,1,0:T(8,128)(2,1)} %get-tuple-element.56), channel_id=1, source_target_pairs={{0,4},{1,5},{2,6},{3,7},{4,0},{5,1},{6,2},{7,3},{8,12},{9,13},{10,... | collective-permute-start | bytes 589832 | tf_op jit(solution)/shard_map/ppermute | solution.py:550
  41.7 2.3 %collective-permute-start.8 = (bf16[3,128,256]{2,1,0:T(8,128)(2,1)}, bf16[3,128,256]{2,1,0:T(8,128)(2,1)S(1)}, u32[]{:S(2)}, u32[]{:S(2)}) collective-permute-start(bf16[3,128,256]{2,1,0:T(8,128)(2,1)} %get-tuple-element.57), channel_id=1, source_target_pairs={{0,8},{1,9},{2,10},{3,11},{4,12},{5,13},{6,14},{7,15},{8,0},{9,1},... | collective-permute-start | bytes 589832 | tf_op jit(solution)/shard_map/ppermute | solution.py:550
  44.1 0.0 collective-permute-done.4.refs_1_
  44.1 1.5 %collective-permute-start.9 = (bf16[3,128,256]{2,1,0:T(8,128)(2,1)}, bf16[3,128,256]{2,1,0:T(8,128)(2,1)S(1)}, u32[]{:S(2)}, u32[]{:S(2)}) collective-permute-start(bf16[3,128,256]{2,1,0:T(8,128)(2,1)} %get-tuple-element.58), channel_id=1, source_target_pairs={{0,12},{1,13},{2,14},{3,15},{4,8},{5,9},{6,10},{7,11},{8,4},{9,5},... | collective-permute-start | bytes 589832 | tf_op jit(solution)/shard_map/ppermute | solution.py:550
  45.6 7.9 %conv_back.1 = (bf16[2048,256]{1,0:T(8,128)(2,1)}, bf16[17,256,256]{2,1,0:T(8,128)(2,1)}) custom-call(bf16[2048,256]{1,0:T(8,128)(2,1)} %bitcast.gated_hbm.refs_10_, bf16[17,256,256]{2,1,0:T(8,128)(2,1)} %filter_spectrum.1.filter_hbm, bf16[17,256,256]{2,1,0:T(8,128)(2,1)} %constant.36.clone.ahead_ref.ahead_hbm.refs_12_, ...), custom_call_target="tpu_custom_call" | custom-call | flops 40000000000 | bytes 11010048 | tf_op jit(solution)/shard_map/conv_back/pallas_call | solution.py:674
  53.5 0.0 copy-done.11
  53.5 4.2 %all-to-all-start.1 = ((bf16[16,128,256]{2,1,0:T(8,128)(2,1)}), bf16[16,128,256]{2,1,0:T(8,128)(2,1)S(1)}, u32[]{:S(2)}, u32[]{:S(2)}) async-start(bf16[16,128,256]{2,1,0:T(8,128)(2,1)} %bitcast.12), calls=%async_computation.1 | async-start | bytes 2097152 | tf_op jit(solution)/shard_map/all_to_all | solution.py:546
  57.7 0.0 collective-permute-done.5.refs_2_
  57.7 0.0 copy-start.12
  57.7 0.0 collective-permute-done.6.refs_3_
  57.7 0.0 collective-permute-done.7.refs_7_
  57.7 0.0 copy-start.8
  57.7 1.3 %collective-permute-done.8.refs_8_ = bf16[3,128,256]{2,1,0:T(8,128)(2,1)S(1)} collective-permute-done((bf16[3,128,256]{2,1,0:T(8,128)(2,1)}, bf16[3,128,256]{2,1,0:T(8,128)(2,1)S(1)}, u32[]{:S(2)}, u32[]{:S(2)}) %collective-permute-start.8) | collective-permute-done | bytes 196640 | tf_op jit(solution)/shard_map/ppermute | solution.py:550
  59.0 0.0 collective-permute-done.9.refs_9_
  59.0 0.0 copy-done.12
  59.0 0.7 copy-done.9
  59.7 0.1 copy-done.10
  59.8 0.0 copy-done.8
  59.8 7.7 %filter_grad.1 = (bf16[256,2048]{1,0:T(8,128)(2,1)}, f32[1,256]{1,0:T(1,128)}) custom-call(bf16[128,256]{1,0:T(8,128)(2,1)} %get-tuple-element.52.refs_0_, bf16[128,256]{1,0:T(8,128)(2,1)} %copy-done.11, bf16[128,256]{1,0:T(8,128)(2,1)} %copy-done.12, bf16[128,256]{1,0:T(8,128)(2,1)} %collective-permute-done.6.refs_3_, bf16[4,128,256]{2,1,0:T(8,128)(2,1)} %copy-done.5, ...), custom_call_target="tpu_custom_call" | custom-call | flops 99999997952 | bytes 6684672 | tf_op jit(solution)/shard_map/filter_grad/pallas_call | solution.py:688
  67.5 0.0 copy-start.4
  67.5 14.6 %all-to-all-done.1.back_ref = bf16[16,128,256]{2,1,0:T(8,128)(2,1)S(1)} async-done(((bf16[16,128,256]{2,1,0:T(8,128)(2,1)}), bf16[16,128,256]{2,1,0:T(8,128)(2,1)S(1)}, u32[]{:S(2)}, u32[]{:S(2)}) %all-to-all-start.1) | async-done | bytes 1048608 | tf_op jit(solution)/shard_map/all_to_all | solution.py:546
  82.1 0.0 copy-done
  82.1 0.0 copy-done.1
  82.1 0.0 copy-done.3
  82.2 1.9 %sums.1 = (f32[2,4096]{1,0:T(2,128)}, f32[4,8,256]{2,1,0:T(8,128)}, f32[4,8,256]{2,1,0:T(8,128)}, f32[4,8,256]{2,1,0:T(8,128)}, f32[4,8,256]{2,1,0:T(8,128)}) custom-call(bf16[16,128,256]{2,1,0:T(8,128)(2,1)S(1)} %all-to-all-done.1.back_ref, bf16[128,4096]{1,0:T(8,128)(2,1)S(1)} %copy-done.1, bf16[128,4096]{1,0:T(8,128)(2,1)S(1)} %copy-done, ...), custom_call_target="tpu_custom_call" | custom-call | flops 10485760 | bytes 4194304 | tf_op jit(solution)/shard_map/sums/pallas_call | solution.py:709
  84.1 2.7 %collective-permute-start.13 = (f32[4,8,256]{2,1,0:T(8,128)}, f32[4,8,256]{2,1,0:T(8,128)S(1)}, u32[]{:S(2)}, u32[]{:S(2)}) collective-permute-start(f32[4,8,256]{2,1,0:T(8,128)} %get-tuple-element.71), channel_id=1, source_target_pairs={{0,12},{1,13},{2,14},{3,15},{4,8},{5,9},{6,10},{7,11},{8,4},{9,5},... | collective-permute-start | bytes 98312 | tf_op jit(solution)/shard_map/ppermute | solution.py:550
  86.8 2.6 %collective-permute-start.12 = (f32[4,8,256]{2,1,0:T(8,128)}, f32[4,8,256]{2,1,0:T(8,128)S(1)}, u32[]{:S(2)}, u32[]{:S(2)}) collective-permute-start(f32[4,8,256]{2,1,0:T(8,128)} %get-tuple-element.70), channel_id=1, source_target_pairs={{0,8},{1,9},{2,10},{3,11},{4,12},{5,13},{6,14},{7,15},{8,0},{9,1},... | collective-permute-start | bytes 98312 | tf_op jit(solution)/shard_map/ppermute | solution.py:550
  89.5 0.5 collective-permute-start.11
  90.0 1.3 %collective-permute-start.10 = (f32[2,4096]{1,0:T(2,128)}, f32[2,4096]{1,0:T(2,128)S(1)}, u32[]{:S(2)}, u32[]{:S(2)}) collective-permute-start(f32[2,4096]{1,0:T(2,128)} %get-tuple-element.63), channel_id=1, source_target_pairs={{1,0},{2,1},{3,2},{4,3},{5,4},{6,5},{7,6},{8,7},{9,8},{10,9},{11,1... | collective-permute-start | bytes 98312 | tf_op jit(solution)/shard_map/ppermute | solution.py:18
  91.2 0.0 collective-permute-done.13
  91.3 0.6 collective-permute-done.12
  91.9 1.7 %collective-permute-done.11 = f32[4,8,256]{2,1,0:T(8,128)S(1)} collective-permute-done((f32[4,8,256]{2,1,0:T(8,128)}, f32[4,8,256]{2,1,0:T(8,128)S(1)}, u32[]{:S(2)}, u32[]{:S(2)}) %collective-permute-start.11) | collective-permute-done | bytes 32800 | tf_op jit(solution)/shard_map/ppermute | solution.py:550
  93.6 0.8 add_add_fusion
  94.4 0.7 collective-permute-start.16
  95.1 0.9 collective-permute-start.15
  96.0 0.3 collective-permute-start.14
  96.3 0.0 collective-permute-done.10.next_ref
  96.3 2.9 %finish.1 = (bf16[128,4096]{1,0:T(8,128)(2,1)}, bf16[128,4096]{1,0:T(8,128)(2,1)}) custom-call(bf16[16,128,256]{2,1,0:T(8,128)(2,1)S(1)} %all-to-all-done.1.back_ref, bf16[128,4096]{1,0:T(8,128)(2,1)S(1)} %copy-done.1, bf16[128,4096]{1,0:T(8,128)(2,1)S(1)} %copy-done, f32[2,4096]{1,0:T(2,128)S(1)} %copy-done.3, ...), custom_call_target="tpu_custom_call" | custom-call | flops 15728640 | bytes 6291456 | tf_op jit(solution)/shard_map/finish/pallas_call | solution.py:725
  99.2 0.0 collective-permute-done.16
  99.2 0.0 collective-permute-done.15
  99.2 0.0 collective-permute-done.14
  99.2 0.6 slice_add_fusion
  (11 shorter events, 0.0 us)
Async XLA Ops:
  3.1 9.6 %collective-permute-start = (f32[2,4096]{1,0:T(2,128)}, f32[2,4096]{1,0:T(2,128)S(1)}, u32[]{:S(2)}, u32[]{:S(2)}) collective-permute-start(f32[2,4096]{1,0:T(2,128)} %get-tuple-element.39), channel_id=1, source_target_pairs={{0,1},{1,2},{2,3},{3,4},{4,5},{5,6},{6,7},{7,8},{8,9},{9,10},{10,1... | collective-permute-start | bytes 98312 | tf_op jit(solution)/shard_map/ppermute | solution.py:18
  5.5 35.0 %all-to-all-start = ((bf16[16,128,256]{2,1,0:T(8,128)(2,1)}), bf16[16,128,256]{2,1,0:T(8,128)(2,1)}, u32[]{:S(2)}, u32[]{:S(2)}) async-start(bf16[16,128,256]{2,1,0:T(8,128)(2,1)} %get-tuple-element.48), calls=%async_computation | async-start | bytes 2097152 | tf_op jit(solution)/shard_map/all_to_all | solution.py:546
  12.7 0.6 copy-start.2
  17.4 11.9 %collective-permute-start.1 = (bf16[4,128,256]{2,1,0:T(8,128)(2,1)}, bf16[4,128,256]{2,1,0:T(8,128)(2,1)S(1)}, u32[]{:S(2)}, u32[]{:S(2)}) collective-permute-start(bf16[4,128,256]{2,1,0:T(8,128)(2,1)} %get-tuple-element.42), channel_id=1, source_target_pairs={{0,1},{1,0},{2,3},{3,2},{4,5},{5,4},{6,7},{7,6},{8,9},{9,8},{10,11... | collective-permute-start | bytes 786440 | tf_op jit(solution)/shard_map/ppermute | solution.py:550
  17.8 13.6 %collective-permute-start.2 = (bf16[4,128,256]{2,1,0:T(8,128)(2,1)}, bf16[4,128,256]{2,1,0:T(8,128)(2,1)S(1)}, u32[]{:S(2)}, u32[]{:S(2)}) collective-permute-start(bf16[4,128,256]{2,1,0:T(8,128)(2,1)} %get-tuple-element.43), channel_id=1, source_target_pairs={{0,2},{1,3},{2,0},{3,1},{4,6},{5,7},{6,4},{7,5},{8,10},{9,11},{10,... | collective-permute-start | bytes 786440 | tf_op jit(solution)/shard_map/ppermute | solution.py:550
  19.5 18.3 %collective-permute-start.3 = (bf16[4,128,256]{2,1,0:T(8,128)(2,1)}, bf16[4,128,256]{2,1,0:T(8,128)(2,1)S(1)}, u32[]{:S(2)}, u32[]{:S(2)}) collective-permute-start(bf16[4,128,256]{2,1,0:T(8,128)(2,1)} %get-tuple-element.44), channel_id=1, source_target_pairs={{0,3},{1,2},{2,1},{3,0},{4,7},{5,6},{6,5},{7,4},{8,11},{9,10},{10,... | collective-permute-start | bytes 786440 | tf_op jit(solution)/shard_map/ppermute | solution.py:550
  19.5 24.6 %collective-permute-start.4 = (bf16[128,256]{1,0:T(8,128)(2,1)}, bf16[128,256]{1,0:T(8,128)(2,1)S(1)}, u32[]{:S(2)}, u32[]{:S(2)}) collective-permute-start(bf16[128,256]{1,0:T(8,128)(2,1)} %get-tuple-element.53), channel_id=1, source_target_pairs={{0,4},{1,5},{2,6},{3,7},{4,0},{5,1},{6,2},{7,3},{8,12},{9,13},{10,... | collective-permute-start | bytes 196616 | tf_op jit(solution)/shard_map/ppermute | solution.py:550
  21.2 36.5 %collective-permute-start.5 = (bf16[128,256]{1,0:T(8,128)(2,1)}, bf16[128,256]{1,0:T(8,128)(2,1)S(1)}, u32[]{:S(2)}, u32[]{:S(2)}) collective-permute-start(bf16[128,256]{1,0:T(8,128)(2,1)} %get-tuple-element.54), channel_id=1, source_target_pairs={{0,8},{1,9},{2,10},{3,11},{4,12},{5,13},{6,14},{7,15},{8,0},{9,1},... | collective-permute-start | bytes 196616 | tf_op jit(solution)/shard_map/ppermute | solution.py:550
  29.3 8.5 %copy-start.5 = (bf16[4,128,256]{2,1,0:T(8,128)(2,1)}, bf16[4,128,256]{2,1,0:T(8,128)(2,1)S(1)}, u32[]{:S(2)}) copy-start(bf16[4,128,256]{2,1,0:T(8,128)(2,1)S(1)} %collective-permute-done.1.refs_0_.refs_4_) | copy-start | bytes 786436
  29.3 28.4 %collective-permute-start.6 = (bf16[128,256]{1,0:T(8,128)(2,1)}, bf16[128,256]{1,0:T(8,128)(2,1)}, u32[]{:S(2)}, u32[]{:S(2)}) collective-permute-start(bf16[128,256]{1,0:T(8,128)(2,1)} %get-tuple-element.55), channel_id=1, source_target_pairs={{0,12},{1,13},{2,14},{3,15},{4,8},{5,9},{6,10},{7,11},{8,4},{9,5},... | collective-permute-start | bytes 196616 | tf_op jit(solution)/shard_map/ppermute | solution.py:550
  31.4 6.4 %copy-start.6 = (bf16[4,128,256]{2,1,0:T(8,128)(2,1)}, bf16[4,128,256]{2,1,0:T(8,128)(2,1)S(1)}, u32[]{:S(2)}) copy-start(bf16[4,128,256]{2,1,0:T(8,128)(2,1)S(1)} %collective-permute-done.2.refs_1_.refs_5_) | copy-start | bytes 786436
  37.8 0.7 copy-start.7
  40.5 17.3 %collective-permute-start.7 = (bf16[3,128,256]{2,1,0:T(8,128)(2,1)}, bf16[3,128,256]{2,1,0:T(8,128)(2,1)S(1)}, u32[]{:S(2)}, u32[]{:S(2)}) collective-permute-start(bf16[3,128,256]{2,1,0:T(8,128)(2,1)} %get-tuple-element.56), channel_id=1, source_target_pairs={{0,4},{1,5},{2,6},{3,7},{4,0},{5,1},{6,2},{7,3},{8,12},{9,13},{10,... | collective-permute-start | bytes 589832 | tf_op jit(solution)/shard_map/ppermute | solution.py:550
  41.7 17.3 %collective-permute-start.8 = (bf16[3,128,256]{2,1,0:T(8,128)(2,1)}, bf16[3,128,256]{2,1,0:T(8,128)(2,1)S(1)}, u32[]{:S(2)}, u32[]{:S(2)}) collective-permute-start(bf16[3,128,256]{2,1,0:T(8,128)(2,1)} %get-tuple-element.57), channel_id=1, source_target_pairs={{0,8},{1,9},{2,10},{3,11},{4,12},{5,13},{6,14},{7,15},{8,0},{9,1},... | collective-permute-start | bytes 589832 | tf_op jit(solution)/shard_map/ppermute | solution.py:550
  44.1 9.4 %copy-start.11 = (bf16[128,256]{1,0:T(8,128)(2,1)}, bf16[128,256]{1,0:T(8,128)(2,1)S(1)}, u32[]{:S(2)}) copy-start(bf16[128,256]{1,0:T(8,128)(2,1)S(1)} %collective-permute-done.4.refs_1_) | copy-start | bytes 196612
  44.1 14.9 %collective-permute-start.9 = (bf16[3,128,256]{2,1,0:T(8,128)(2,1)}, bf16[3,128,256]{2,1,0:T(8,128)(2,1)S(1)}, u32[]{:S(2)}, u32[]{:S(2)}) collective-permute-start(bf16[3,128,256]{2,1,0:T(8,128)(2,1)} %get-tuple-element.58), channel_id=1, source_target_pairs={{0,12},{1,13},{2,14},{3,15},{4,8},{5,9},{6,10},{7,11},{8,4},{9,5},... | collective-permute-start | bytes 589832 | tf_op jit(solution)/shard_map/ppermute | solution.py:550
  53.5 28.7 %all-to-all-start.1 = ((bf16[16,128,256]{2,1,0:T(8,128)(2,1)}), bf16[16,128,256]{2,1,0:T(8,128)(2,1)S(1)}, u32[]{:S(2)}, u32[]{:S(2)}) async-start(bf16[16,128,256]{2,1,0:T(8,128)(2,1)} %bitcast.12), calls=%async_computation.1 | async-start | bytes 2097152 | tf_op jit(solution)/shard_map/all_to_all | solution.py:546
  57.7 1.3 %copy-start.12 = (bf16[128,256]{1,0:T(8,128)(2,1)}, bf16[128,256]{1,0:T(8,128)(2,1)S(1)}, u32[]{:S(2)}) copy-start(bf16[128,256]{1,0:T(8,128)(2,1)S(1)} %collective-permute-done.5.refs_2_) | copy-start | bytes 196612
  57.7 2.0 %copy-start.8 = (bf16[3,128,256]{2,1,0:T(8,128)(2,1)}, bf16[3,128,256]{2,1,0:T(8,128)(2,1)S(1)}, u32[]{:S(2)}) copy-start(bf16[3,128,256]{2,1,0:T(8,128)(2,1)S(1)} %collective-permute-done.7.refs_7_) | copy-start | bytes 589828
  59.0 0.7 copy-start.9
  59.0 0.8 copy-start.10
  59.8 22.4 %copy-start = (bf16[128,4096]{1,0:T(8,128)(2,1)S(1)}, bf16[128,4096]{1,0:T(8,128)(2,1)}, u32[]{:S(2)}) copy-start(bf16[128,4096]{1,0:T(8,128)(2,1)} %value_ref.7) | copy-start | bytes 3145732
  59.8 22.4 %copy-start.1 = (bf16[128,4096]{1,0:T(8,128)(2,1)S(1)}, bf16[128,4096]{1,0:T(8,128)(2,1)}, u32[]{:S(2)}) copy-start(bf16[128,4096]{1,0:T(8,128)(2,1)} %key_ref.5) | copy-start | bytes 3145732
  59.8 22.4 %copy-start.3 = (f32[2,4096]{1,0:T(2,128)S(1)}, f32[2,4096]{1,0:T(2,128)}, u32[]{:S(2)}) copy-start(f32[2,4096]{1,0:T(2,128)} %copy-done.2) | copy-start | bytes 98308
  67.5 28.8 %copy-start.4 = (f32[3,4096]{1,0:T(4,128)S(1)}, f32[3,4096]{1,0:T(4,128)}, u32[]{:S(2)}) copy-start(f32[3,4096]{1,0:T(4,128)} %short_ref.3) | copy-start | bytes 147460
  84.1 7.2 %collective-permute-start.13 = (f32[4,8,256]{2,1,0:T(8,128)}, f32[4,8,256]{2,1,0:T(8,128)S(1)}, u32[]{:S(2)}, u32[]{:S(2)}) collective-permute-start(f32[4,8,256]{2,1,0:T(8,128)} %get-tuple-element.71), channel_id=1, source_target_pairs={{0,12},{1,13},{2,14},{3,15},{4,8},{5,9},{6,10},{7,11},{8,4},{9,5},... | collective-permute-start | bytes 98312 | tf_op jit(solution)/shard_map/ppermute | solution.py:550
  86.8 5.0 %collective-permute-start.12 = (f32[4,8,256]{2,1,0:T(8,128)}, f32[4,8,256]{2,1,0:T(8,128)S(1)}, u32[]{:S(2)}, u32[]{:S(2)}) collective-permute-start(f32[4,8,256]{2,1,0:T(8,128)} %get-tuple-element.70), channel_id=1, source_target_pairs={{0,8},{1,9},{2,10},{3,11},{4,12},{5,13},{6,14},{7,15},{8,0},{9,1},... | collective-permute-start | bytes 98312 | tf_op jit(solution)/shard_map/ppermute | solution.py:550
  89.5 4.1 %collective-permute-start.11 = (f32[4,8,256]{2,1,0:T(8,128)}, f32[4,8,256]{2,1,0:T(8,128)S(1)}, u32[]{:S(2)}, u32[]{:S(2)}) collective-permute-start(f32[4,8,256]{2,1,0:T(8,128)} %get-tuple-element.69), channel_id=1, source_target_pairs={{0,4},{1,5},{2,6},{3,7},{4,0},{5,1},{6,2},{7,3},{8,12},{9,13},{10,... | collective-permute-start | bytes 98312 | tf_op jit(solution)/shard_map/ppermute | solution.py:550
  90.0 6.4 %collective-permute-start.10 = (f32[2,4096]{1,0:T(2,128)}, f32[2,4096]{1,0:T(2,128)S(1)}, u32[]{:S(2)}, u32[]{:S(2)}) collective-permute-start(f32[2,4096]{1,0:T(2,128)} %get-tuple-element.63), channel_id=1, source_target_pairs={{1,0},{2,1},{3,2},{4,3},{5,4},{6,5},{7,6},{8,7},{9,8},{10,9},{11,1... | collective-permute-start | bytes 98312 | tf_op jit(solution)/shard_map/ppermute | solution.py:18
  94.4 4.9 %collective-permute-start.16 = (f32[8,256]{1,0:T(8,128)S(1)}, f32[8,256]{1,0:T(8,128)S(1)}, u32[]{:S(2)}, u32[]{:S(2)}) collective-permute-start(f32[8,256]{1,0:T(8,128)S(1)} %get-tuple-element.73), channel_id=1, source_target_pairs={{0,3},{1,2},{2,1},{3,0},{4,7},{5,6},{6,5},{7,4},{8,11},{9,10},{10,... | collective-permute-start | bytes 24584 | tf_op jit(solution)/shard_map/ppermute | solution.py:550
  95.1 4.2 %collective-permute-start.15 = (f32[8,256]{1,0:T(8,128)S(1)}, f32[8,256]{1,0:T(8,128)S(1)}, u32[]{:S(2)}, u32[]{:S(2)}) collective-permute-start(f32[8,256]{1,0:T(8,128)S(1)} %get-tuple-element.74), channel_id=1, source_target_pairs={{0,2},{1,3},{2,0},{3,1},{4,6},{5,7},{6,4},{7,5},{8,10},{9,11},{10,... | collective-permute-start | bytes 24584 | tf_op jit(solution)/shard_map/ppermute | solution.py:550
  96.0 3.3 %collective-permute-start.14 = (f32[8,256]{1,0:T(8,128)S(1)}, f32[8,256]{1,0:T(8,128)S(1)}, u32[]{:S(2)}, u32[]{:S(2)}) collective-permute-start(f32[8,256]{1,0:T(8,128)S(1)} %get-tuple-element.75), channel_id=1, source_target_pairs={{0,1},{1,0},{2,3},{3,2},{4,5},{5,4},{6,7},{7,6},{8,9},{9,8},{10,11... | collective-permute-start | bytes 24584 | tf_op jit(solution)/shard_map/ppermute | solution.py:550
